TPU v7x, 32 devices: a whole 2x2x4 slice. The times are simulated.
32 devices in a mesh: dp: 8 (over z, x), row: 2 (over y), col: 2 (over core).
Axes of the slice: x: 2, y: 2, z: 4, core: 2. Of those that a mesh axis runs over, the one named last changes fastest.
Arguments:
- latents: bfloat16 [16384, 1152], P(('dp', 'row'), 'col'), may hold values from -6 to 6
- skip_input: bfloat16 [16384, 1152], P(('dp', 'row'), 'col'), may hold values from -6 to 6
- condition: bfloat16 [16, 1152], P('dp', 'col'), may hold values from -6 to 6
- text_states: bfloat16 [5328, 1024], P(('dp', 'col'), 'row'), may hold values from -6 to 6
- positions: int32 [16384, 2], P(('dp', 'row')), may hold values from 0 to 63, as said below
- cotangent: bfloat16 [16384, 1152], P(('dp', 'col'), 'row'), may hold values from -6 to 6
- skip_gain: float32 [2, 1152], P(None, 'col'), may hold values from 0.1 to 1.9
- skip_weight: bfloat16 [2, 1152, 1152], P(None, 'col', 'row'), may hold values from -0.125 to 0.125
- shift_weight: bfloat16 [1152, 1152], P('col', 'row'), may hold values from -0.1875 to 0.1875
- self_gain: float32 [1152], P('row'), may hold values from 0.1 to 1.9
- self_weight: bfloat16 [1152, 3, 1152], P('row', None, 'col'), may hold values from -0.1875 to 0.1875
- query_gain: float32 [72], replicated, may hold values from 0.1 to 1.9
- key_gain: float32 [72], replicated, may hold values from 0.1 to 1.9
- self_out: bfloat16 [1152, 1152], P('col', 'row'), may hold values from -0.3125 to 0.3125
- cross_gain: float32 [1152], P('row'), may hold values from 0.1 to 1.9
- cross_query: bfloat16 [1152, 1152], P('row', 'col'), may hold values from -1 to 1
- cross_context: bfloat16 [1024, 2, 1152], P('row', None, 'col'), may hold values from -0.1875 to 0.1875
- cross_query_gain: float32 [72], replicated, may hold values from 0.1 to 1.9
- cross_key_gain: float32 [72], replicated, may hold values from 0.1 to 1.9
- cross_out: bfloat16 [1152, 1152], P('col', 'row'), may hold values from -0.625 to 0.625
- feed_gain: float32 [1152], P('row'), may hold values from 0.1 to 1.9
- up_weight: bfloat16 [1152, 4608], P('row', 'col'), may hold values from -1 to 1
- down_weight: bfloat16 [4608, 1152], P('col', 'row'), may hold values from -0.09375 to 0.09375
Outputs:
- block_out: bfloat16 [16384, 1152], P(('dp', 'col'), 'row')
- grad_latents: bfloat16 [16384, 1152], P(('dp', 'row'), 'col')
- grad_skip_input: bfloat16 [16384, 1152], P(('dp', 'row'), 'col')
- grad_text_states: bfloat16 [5328, 1024], P(('dp', 'col'), 'row')
- grad_skip_gain: float32 [2, 1152], P(None, 'col')
- grad_skip_weight: float32 [2, 1152, 1152], P(None, 'col', 'row')
- grad_shift_weight: float32 [1152, 1152], P('col', 'row')
- grad_self_gain: float32 [1152], P('row')
- grad_self_weight: float32 [1152, 3, 1152], P('row', None, 'col')
- grad_query_gain: float32 [72], replicated
- grad_key_gain: float32 [72], replicated
- grad_self_out: float32 [1152, 1152], P('col', 'row')
- grad_cross_gain: float32 [1152], P('row')
- grad_cross_query: float32 [1152, 1152], P('row', 'col')
- grad_cross_context: float32 [1024, 2, 1152], P('row', None, 'col')
- grad_cross_query_gain: float32 [72], replicated
- grad_cross_key_gain: float32 [72], replicated
- grad_cross_out: float32 [1152, 1152], P('col', 'row')
- grad_feed_gain: float32 [1152], P('row')
- grad_up_weight: float32 [1152, 4608], P('row', 'col')
- grad_down_weight: float32 [4608, 1152], P('col', 'row')
Inputs may be any that keep to these rules, and one draw needn't show every extreme that they name: `positions`: within each image of 1024 latent tokens, token i stands at (i // w, i % w) for a width w drawn per image from 16, 32 and 64.
All inputs are finite; a program needn't handle non-finite values.
Results may differ from a plain program's by a relative error of at most 0.02.
Values may be sent and summed in bfloat16 or wider, within the bound.
A program may use at most 256 MiB of HBM per device.

v0:
```python
import jax
import jax.numpy as jnp
from jax import lax
from jax.sharding import PartitionSpec as P

D = 1152
HD = 72
TXT = 333
LAT = 1024


EPSILON = 1e-06
PRECISE = lax.Precision.HIGHEST


def contract(left_side, right_side, transposed):
    if transposed:
        numbers = (((1,), (1,)), ((), ()))
    else:
        numbers = (((1,), (0,)), ((), ()))
    return lax.dot_general(left_side, right_side, numbers, preferred_element_type=jnp.float32)


def token_sum(left_side, right_side):
    return lax.dot_general(
        left_side, right_side, (((0,), (0,)), ((), ())), preferred_element_type=jnp.float32
    )


def collect_cols(values):
    return lax.all_gather(values, "col", axis=0, tiled=True)


def spread_cols(term_fn, own_rows):
    return lax.psum_scatter(
        term_fn(jnp.int32(0), own_rows * lax.axis_size("col")),
        "col",
        scatter_dimension=0,
        tiled=True,
    )


def to_heads(values, weight, transposed):
    gathered = collect_cols(values)
    own_rows = gathered.shape[0] // lax.axis_size("row")

    def partial_term(row_start, row_count):
        return contract(gathered, weight, transposed)

    return (
        lax.psum_scatter(
            partial_term(jnp.int32(0), own_rows * lax.axis_size("row")),
            "row",
            scatter_dimension=0,
            tiled=True,
        ),
        gathered,
    )


def to_tokens(values, weight, transposed):
    gathered = lax.all_gather(values, "row", axis=0, tiled=True)
    own_rows = gathered.shape[0] // lax.axis_size("col")

    def partial_term(row_start, row_count):
        return contract(gathered, weight, transposed)

    return (spread_cols(partial_term, own_rows), gathered)


def row_totals(first_term, second_term):
    return lax.psum((first_term, second_term), "row")


def col_totals(first_term, second_term):
    return lax.psum((first_term, second_term), "col")


def shift_total(values):
    return lax.psum(values, "col")


def gain_totals(
    skip_part, self_part, cross_part, feed_part, query_part, key_part, probe_part, memory_part
):
    return lax.psum(
        (
            skip_part,
            self_part,
            cross_part,
            feed_part,
            query_part,
            key_part,
            probe_part,
            memory_part,
        ),
        ("dp", "row", "col"),
    )


def finish_weights(
    grad_skip,
    grad_shift,
    grad_self,
    grad_self_out,
    grad_cross_query,
    grad_context,
    grad_cross_out,
    grad_up,
    grad_down,
):
    return (
        lax.psum(grad_skip.astype(jnp.bfloat16), "dp").astype(jnp.float32),
        lax.psum(grad_shift.astype(jnp.bfloat16), "dp").astype(jnp.float32),
        lax.psum(grad_self.astype(jnp.bfloat16), "dp").astype(jnp.float32),
        lax.psum(grad_self_out.astype(jnp.bfloat16), "dp").astype(jnp.float32),
        lax.psum(grad_cross_query.astype(jnp.bfloat16), "dp").astype(jnp.float32),
        lax.psum(grad_context.astype(jnp.bfloat16), "dp").astype(jnp.float32),
        lax.psum(grad_cross_out.astype(jnp.bfloat16), "dp").astype(jnp.float32),
        lax.psum(grad_up.astype(jnp.bfloat16), "dp").astype(jnp.float32),
        lax.psum(grad_down.astype(jnp.bfloat16), "dp").astype(jnp.float32),
    )


def head_norm(values, norm_gain):
    average = jnp.mean(values, axis=-1, keepdims=True)
    variance = jnp.mean(values * values, axis=-1, keepdims=True) - average * average
    return (values - average) * lax.rsqrt(variance + EPSILON) * norm_gain


def gelu_tanh(values):
    return jax.nn.gelu(values, approximate=True)


def rotate(values, row_place, col_place):
    half_width = values.shape[-1] // 2
    quarter = half_width // 2
    frequency = 10000.0 ** (-jnp.arange(quarter, dtype=jnp.float32) / quarter)

    def turn_half(portion, place):
        angles = place[:, None] * frequency[None, :]
        cosine = jnp.cos(angles)[:, None, :]
        sine_value = jnp.sin(angles)[:, None, :]
        leading = portion[..., :quarter]
        trailing = portion[..., quarter:]
        return jnp.concatenate(
            [leading * cosine - trailing * sine_value, trailing * cosine + leading * sine_value],
            axis=-1,
        )

    return jnp.concatenate(
        [
            turn_half(values[..., :half_width], row_place),
            turn_half(values[..., half_width:], col_place),
        ],
        axis=-1,
    )


def norm_across(values):
    totals = row_totals(jnp.sum(values, axis=1), jnp.sum(values * values, axis=1))
    average = totals[0] / D
    variance = totals[1] / D - average * average
    inverse = lax.rsqrt(variance + EPSILON)
    normed = (values - average[:, None]) * inverse[:, None]
    return (normed, inverse)


def norm_across_back(grad_normed, normed, inverse, norm_gain):
    scaled = grad_normed * norm_gain
    totals = row_totals(jnp.sum(scaled, axis=1), jnp.sum(scaled * normed, axis=1))
    first_mean = totals[0] / D
    second_mean = totals[1] / D
    grad_input = inverse[:, None] * (scaled - first_mean[:, None] - normed * second_mean[:, None])
    return (grad_input, jnp.sum(grad_normed * normed, axis=0))


def attend_forward(queries, key_rows, value_rows, key_len, first_row, block_len):
    heads_here = queries.shape[1]
    head_width = queries.shape[2]
    score_scale = head_width ** (-0.5)
    groups = key_rows.shape[0] // key_len
    key_groups = key_rows.reshape(groups, key_len, heads_here, head_width)
    value_groups = value_rows.reshape(groups, key_len, heads_here, head_width)
    block_count = queries.shape[0] // block_len
    query_blocks = queries.reshape(block_count, block_len, heads_here, head_width)
    block_ids = jnp.arange(block_count, dtype=jnp.int32)

    def one_block(packed):
        block_id, query_block = packed
        group_index = (first_row + block_id * block_len) // LAT
        key_block = lax.dynamic_index_in_dim(key_groups, group_index, 0, keepdims=False)
        value_block = lax.dynamic_index_in_dim(value_groups, group_index, 0, keepdims=False)
        scores = (
            jnp.einsum("qhe,khe->hqk", query_block, key_block, preferred_element_type=jnp.float32)
            * score_scale
        )
        row_top = jnp.max(scores, axis=-1, keepdims=True)
        row_total = jnp.sum(jnp.exp(scores - row_top), axis=-1, keepdims=True)
        log_total = row_top + jnp.log(row_total)
        weights_low = jnp.exp(scores - log_total).astype(jnp.bfloat16)
        output = jnp.einsum(
            "hqk,khe->qhe", weights_low, value_block, preferred_element_type=jnp.float32
        )
        return (output, log_total[..., 0])

    outputs, log_totals = lax.map(one_block, (block_ids, query_blocks))
    return (outputs.reshape(queries.shape), log_totals)


def attend_backward(
    queries, key_rows, value_rows, grad_heads, log_totals, key_len, first_row, block_len
):
    heads_here = queries.shape[1]
    head_width = queries.shape[2]
    score_scale = head_width ** (-0.5)
    groups = key_rows.shape[0] // key_len
    key_groups = key_rows.reshape(groups, key_len, heads_here, head_width)
    value_groups = value_rows.reshape(groups, key_len, heads_here, head_width)
    block_count = queries.shape[0] // block_len
    query_blocks = queries.reshape(block_count, block_len, heads_here, head_width)
    grad_blocks = grad_heads.reshape(block_count, block_len, heads_here, head_width)
    block_ids = jnp.arange(block_count, dtype=jnp.int32)

    def one_block(carry, packed):
        key_store, value_store = carry
        block_id, query_block, grad_block, log_block = packed
        group_index = (first_row + block_id * block_len) // LAT
        key_block = lax.dynamic_index_in_dim(key_groups, group_index, 0, keepdims=False)
        value_block = lax.dynamic_index_in_dim(value_groups, group_index, 0, keepdims=False)
        scores = (
            jnp.einsum("qhe,khe->hqk", query_block, key_block, preferred_element_type=jnp.float32)
            * score_scale
        )
        weights_full = jnp.exp(scores - log_block[..., None])
        grad_weights = jnp.einsum(
            "qhe,khe->hqk", grad_block, value_block, preferred_element_type=jnp.float32
        )
        inner_sum = jnp.sum(weights_full * grad_weights, axis=-1, keepdims=True)
        grad_scores = (weights_full * (grad_weights - inner_sum)).astype(jnp.bfloat16)
        grad_query = (
            jnp.einsum("hqk,khe->qhe", grad_scores, key_block, preferred_element_type=jnp.float32)
            * score_scale
        )
        grad_key = (
            jnp.einsum("hqk,qhe->khe", grad_scores, query_block, preferred_element_type=jnp.float32)
            * score_scale
        )
        grad_value = jnp.einsum(
            "hqk,qhe->khe",
            weights_full.astype(jnp.bfloat16),
            grad_block,
            preferred_element_type=jnp.float32,
        )
        key_now = lax.dynamic_index_in_dim(key_store, group_index, 0, keepdims=False) + grad_key
        value_now = (
            lax.dynamic_index_in_dim(value_store, group_index, 0, keepdims=False) + grad_value
        )
        key_store = lax.dynamic_update_index_in_dim(key_store, key_now, group_index, 0)
        value_store = lax.dynamic_update_index_in_dim(value_store, value_now, group_index, 0)
        return ((key_store, value_store), grad_query)

    empty = jnp.zeros((groups, key_len, heads_here, head_width), jnp.float32)
    (key_store, value_store), grad_query = lax.scan(
        one_block, (empty, empty), (block_ids, query_blocks, grad_blocks, log_totals)
    )
    return (
        grad_query.reshape(queries.shape),
        key_store.reshape(key_rows.shape),
        value_store.reshape(value_rows.shape),
    )


def shards(
    latents,
    skip_input,
    condition,
    text_states,
    positions,
    cotangent,
    skip_gain,
    skip_weight,
    shift_weight,
    self_gain,
    self_weight,
    query_gain,
    key_gain,
    self_out,
    cross_gain,
    cross_query,
    cross_context,
    cross_query_gain,
    cross_key_gain,
    cross_out,
    feed_gain,
    up_weight,
    down_weight,
):
    row_tokens = latents.shape[0]
    col_tokens = cotangent.shape[0]
    col_seqs = col_tokens // LAT
    col_width = latents.shape[1]
    row_width = cotangent.shape[1]
    heads_here = col_width // HD
    col_index = lax.axis_index("col")
    row_index = lax.axis_index("row")
    row_place = positions[:, 0].astype(jnp.float32)
    col_place = positions[:, 1].astype(jnp.float32)
    block_len = min(512, LAT)
    joined = jnp.stack([latents, skip_input], axis=1).astype(jnp.float32)
    totals = col_totals(jnp.sum(joined, axis=(1, 2)), jnp.sum(joined * joined, axis=(1, 2)))
    average = totals[0] / (2 * D)
    variance = totals[1] / (2 * D) - average * average
    skip_inverse = lax.rsqrt(variance + EPSILON)
    skip_normed = (joined - average[:, None, None]) * skip_inverse[:, None, None]
    skip_low = (skip_normed * skip_gain).astype(jnp.bfloat16).reshape(row_tokens, 2 * col_width)
    skip_flat = skip_weight.reshape(2 * col_width, row_width)
    first_state, skip_rows = to_tokens(skip_low, skip_flat, False)
    cond_low = jax.nn.silu(condition.astype(jnp.float32)).astype(jnp.bfloat16)
    shift_all = shift_total(contract(cond_low, shift_weight, False))
    shift_own = lax.dynamic_slice_in_dim(shift_all, col_index * col_seqs, col_seqs, 0)
    normed_one, inverse_one = norm_across(first_state)
    first_input = (normed_one * self_gain).reshape(col_seqs, LAT, row_width) + shift_own[:, None, :]
    first_input = first_input.reshape(col_tokens, row_width).astype(jnp.bfloat16)
    self_flat = self_weight.reshape(row_width, 3 * col_width)
    mixed_raw, first_cols = to_heads(first_input, self_flat, False)
    mixed_raw = mixed_raw.reshape(row_tokens, 3, heads_here, HD)

    def shape_query(raw_part, norm_gain):
        return rotate(head_norm(raw_part, norm_gain), row_place, col_place)

    query_float, query_pull = jax.vjp(shape_query, mixed_raw[:, 0], query_gain)
    key_float, key_pull = jax.vjp(shape_query, mixed_raw[:, 1], key_gain)
    queries = query_float.astype(jnp.bfloat16)
    key_rows = key_float.astype(jnp.bfloat16)
    value_rows = mixed_raw[:, 2].astype(jnp.bfloat16)
    heads_float, log_first = attend_forward(queries, key_rows, value_rows, LAT, 0, block_len)
    heads_low = heads_float.astype(jnp.bfloat16).reshape(row_tokens, col_width)
    attn_branch, heads_rows = to_tokens(heads_low, self_out, False)
    second_state = first_state + attn_branch
    normed_two, inverse_two = norm_across(second_state)
    cross_input = (normed_two * cross_gain).astype(jnp.bfloat16)
    probe_raw, cross_cols = to_heads(cross_input, cross_query, False)
    probe_raw = probe_raw.reshape(row_tokens, heads_here, HD)
    context_flat = cross_context.reshape(cross_context.shape[0], 2 * col_width)
    memory_raw, text_cols = to_heads(text_states, context_flat, False)
    text_here = memory_raw.shape[0]
    memory_raw = memory_raw.reshape(text_here, 2, heads_here, HD)
    probe_float, probe_pull = jax.vjp(head_norm, probe_raw, cross_query_gain)
    memory_float, memory_pull = jax.vjp(head_norm, memory_raw[:, 0], cross_key_gain)
    probes = probe_float.astype(jnp.bfloat16)
    memory_keys = memory_float.astype(jnp.bfloat16)
    memory_values = memory_raw[:, 1].astype(jnp.bfloat16)
    cross_float, log_second = attend_forward(probes, memory_keys, memory_values, TXT, 0, block_len)
    cross_low = cross_float.astype(jnp.bfloat16).reshape(row_tokens, col_width)
    cross_branch, cross_rows = to_tokens(cross_low, cross_out, False)
    third_state = second_state + cross_branch
    normed_three, inverse_three = norm_across(third_state)
    feed_input = (normed_three * feed_gain).astype(jnp.bfloat16)
    hidden_raw, feed_cols = to_heads(feed_input, up_weight, False)
    hidden_float, gelu_pull = jax.vjp(gelu_tanh, hidden_raw)
    hidden_low = hidden_float.astype(jnp.bfloat16)
    feed_branch, hidden_rows = to_tokens(hidden_low, down_weight, False)
    block_out = (third_state + feed_branch).astype(jnp.bfloat16)
    grad_hidden, cotangent_cols = to_heads(cotangent, down_weight, True)
    grad_down = token_sum(hidden_rows, cotangent_cols)
    grad_pre = gelu_pull(grad_hidden)[0].astype(jnp.bfloat16)
    grad_feed_in, pre_rows = to_tokens(grad_pre, up_weight, True)
    grad_up = token_sum(feed_cols, pre_rows)
    back_three, feed_gain_part = norm_across_back(
        grad_feed_in, normed_three, inverse_three, feed_gain
    )
    grad_third = cotangent.astype(jnp.float32) + back_three
    branch_two = grad_third.astype(jnp.bfloat16)
    grad_cross_heads, branch_two_cols = to_heads(branch_two, cross_out, True)
    grad_cross_out = token_sum(cross_rows, branch_two_cols)
    grad_cross_low = grad_cross_heads.astype(jnp.bfloat16).reshape(row_tokens, heads_here, HD)
    grad_probe, grad_memory_key, grad_memory_value = attend_backward(
        probes, memory_keys, memory_values, grad_cross_low, log_second, TXT, 0, block_len
    )
    grad_probe_raw, grad_probe_gain = probe_pull(grad_probe)
    probe_low = grad_probe_raw.astype(jnp.bfloat16).reshape(row_tokens, col_width)
    grad_cross_in, probe_rows = to_tokens(probe_low, cross_query, True)
    grad_cross_query = token_sum(cross_cols, probe_rows)
    grad_memory_raw, grad_memory_gain = memory_pull(grad_memory_key)
    memory_low = jnp.stack([grad_memory_raw, grad_memory_value], axis=1).astype(jnp.bfloat16)
    memory_low = memory_low.reshape(text_here, 2 * col_width)
    grad_text_float, memory_rows = to_tokens(memory_low, context_flat, True)
    grad_cross_context = token_sum(text_cols, memory_rows).reshape(cross_context.shape)
    back_two, cross_gain_part = norm_across_back(grad_cross_in, normed_two, inverse_two, cross_gain)
    grad_second = grad_third + back_two
    branch_one = grad_second.astype(jnp.bfloat16)
    grad_heads, branch_one_cols = to_heads(branch_one, self_out, True)
    grad_self_out = token_sum(heads_rows, branch_one_cols)
    grad_heads_low = grad_heads.astype(jnp.bfloat16).reshape(row_tokens, heads_here, HD)
    grad_query, grad_key, grad_value = attend_backward(
        queries, key_rows, value_rows, grad_heads_low, log_first, LAT, 0, block_len
    )
    grad_query_raw, grad_query_gain = query_pull(grad_query)
    grad_key_raw, grad_key_gain = key_pull(grad_key)
    mixed_low = jnp.stack([grad_query_raw, grad_key_raw, grad_value], axis=1).astype(jnp.bfloat16)
    mixed_low = mixed_low.reshape(row_tokens, 3 * col_width)
    grad_first_in, mixed_rows = to_tokens(mixed_low, self_flat, True)
    grad_self_weight = token_sum(first_cols, mixed_rows).reshape(self_weight.shape)
    shift_own_grad = jnp.sum(grad_first_in.reshape(col_seqs, LAT, row_width), axis=1)
    shift_placed = lax.dynamic_update_slice_in_dim(
        jnp.zeros((condition.shape[0], row_width), jnp.float32),
        shift_own_grad,
        col_index * col_seqs,
        0,
    )
    shift_grad = shift_total(shift_placed)
    grad_shift_weight = lax.dot_general(
        cond_low.astype(jnp.float32),
        shift_grad,
        (((0,), (0,)), ((), ())),
        precision=PRECISE,
        preferred_element_type=jnp.float32,
    )
    back_one, self_gain_part = norm_across_back(grad_first_in, normed_one, inverse_one, self_gain)
    grad_first = grad_second + back_one
    grad_skip_out, first_grad_cols = to_heads(grad_first.astype(jnp.bfloat16), skip_flat, True)
    grad_skip_weight = token_sum(skip_rows, first_grad_cols).reshape(skip_weight.shape)
    grad_joined_out = grad_skip_out.reshape(row_tokens, 2, col_width)
    scaled = grad_joined_out * skip_gain
    totals_back = col_totals(
        jnp.sum(scaled, axis=(1, 2)), jnp.sum(scaled * skip_normed, axis=(1, 2))
    )
    first_mean = (totals_back[0] / (2 * D))[:, None, None]
    second_mean = (totals_back[1] / (2 * D))[:, None, None]
    grad_joined = skip_inverse[:, None, None] * (scaled - first_mean - skip_normed * second_mean)
    skip_gain_part = jnp.sum(grad_joined_out * skip_normed, axis=0)
    grad_latents = grad_joined[:, 0].astype(jnp.bfloat16)
    grad_skip_input = grad_joined[:, 1].astype(jnp.bfloat16)
    grad_text_states = grad_text_float.astype(jnp.bfloat16)

    def place_rows(partial_value):
        return lax.dynamic_update_slice_in_dim(
            jnp.zeros((D,), jnp.float32), partial_value, row_index * row_width, 0
        )

    skip_full = lax.dynamic_update_slice_in_dim(
        jnp.zeros((2, D), jnp.float32), skip_gain_part, col_index * col_width, 1
    )
    gain_sums = gain_totals(
        skip_full,
        place_rows(self_gain_part),
        place_rows(cross_gain_part),
        place_rows(feed_gain_part),
        grad_query_gain,
        grad_key_gain,
        grad_probe_gain,
        grad_memory_gain,
    )
    grad_skip_gain = lax.dynamic_slice_in_dim(gain_sums[0], col_index * col_width, col_width, 1)
    grad_self_gain = lax.dynamic_slice_in_dim(gain_sums[1], row_index * row_width, row_width, 0)
    grad_cross_gain = lax.dynamic_slice_in_dim(gain_sums[2], row_index * row_width, row_width, 0)
    grad_feed_gain = lax.dynamic_slice_in_dim(gain_sums[3], row_index * row_width, row_width, 0)
    (
        grad_skip_weight,
        grad_shift_weight,
        grad_self_weight,
        grad_self_out,
        grad_cross_query,
        grad_cross_context,
        grad_cross_out,
        grad_up,
        grad_down,
    ) = finish_weights(
        grad_skip_weight,
        grad_shift_weight,
        grad_self_weight,
        grad_self_out,
        grad_cross_query,
        grad_cross_context,
        grad_cross_out,
        grad_up,
        grad_down,
    )
    return (
        block_out,
        grad_latents,
        grad_skip_input,
        grad_text_states,
        grad_skip_gain,
        grad_skip_weight,
        grad_shift_weight,
        grad_self_gain,
        grad_self_weight,
        gain_sums[4],
        gain_sums[5],
        grad_self_out,
        grad_cross_gain,
        grad_cross_query,
        grad_cross_context,
        gain_sums[6],
        gain_sums[7],
        grad_cross_out,
        grad_feed_gain,
        grad_up,
        grad_down,
    )


def solution(mesh):
    placed = (
        P(("dp", "row"), "col"),
        P(("dp", "row"), "col"),
        P("dp", "col"),
        P(("dp", "col"), "row"),
        P(("dp", "row"), None),
        P(("dp", "col"), "row"),
        P(None, "col"),
        P(None, "col", "row"),
        P("col", "row"),
        P("row"),
        P("row", None, "col"),
        P(),
        P(),
        P("col", "row"),
        P("row"),
        P("row", "col"),
        P("row", None, "col"),
        P(),
        P(),
        P("col", "row"),
        P("row"),
        P("row", "col"),
        P("col", "row"),
    )
    return jax.shard_map(
        shards,
        mesh=mesh,
        in_specs=placed,
        out_specs=(
            P(("dp", "col"), "row"),
            P(("dp", "row"), "col"),
            P(("dp", "row"), "col"),
            P(("dp", "col"), "row"),
            P(None, "col"),
            P(None, "col", "row"),
            P("col", "row"),
            P("row"),
            P("row", None, "col"),
            P(),
            P(),
            P("col", "row"),
            P("row"),
            P("row", "col"),
            P("row", None, "col"),
            P(),
            P(),
            P("col", "row"),
            P("row"),
            P("row", "col"),
            P("col", "row"),
        ),
        check_vma=False,
    )
```

profile of v0, /device:TPU:1, one launch (start us, length us, event | category | flops | bytes accessed | tf_op | source)
XLA Modules:
  0.0 2542.6 jit_solution(5988305097701917339)
XLA Ops:
  26.5 64.9 %all-gather.18.cloned.1.call-done = bf16[2048,1152]{1,0:T(8,128)(2,1)} async-done(((bf16[1024,1152]{1,0:T(8,128)(2,1)}), bf16[2048,1152]{1,0:T(8,128)(2,1)}) %all-gather.18.cloned.1.call-update) | async-done | bytes 4718608 | tf_op jit(solution)/shard_map/all_gather | solution.py:62
  91.3 8.2 fusion.147
  99.7 13.0 reduce-scatter.19.cloned.1.call-done
  126.7 9.0 all-gather.20.cloned.1.call-done
  135.7 10.8 fusion.159
  149.8 159.1 %reduce-scatter.21.cloned.1.call-done = f32[1024,1728]{0,1:T(8,128)} async-done(((f32[2048,1728]{0,1:T(8,128)}), f32[1024,1728]{0,1:T(8,128)}) %reduce-scatter.21.cloned.1.call-update) | async-done | bytes 7077904 | tf_op jit(solution)/shard_map/reduce_scatter | solution.py:51
  333.4 25.7 %while.60 = (s32[]{:T(128)}, bf16[2,512,8,72]{1,3,2,0:T(8,128)(2,1)}, f32[2,8,512]{2,1,0:T(8,128)}, bf16[2,512,8,72]{1,3,2,0:T(8,128)(2,1)}, bf16[1,1024,8,72]{1...) while((s32[]{:T(128)}, bf16[2,512,8,72]{1,3,2,0:T(8,128)(2,1)}, f32[2,8,512]{2,1,0:T(8,128)}, ...), condition=%wide.region_18.19_spmd.clone, body=%wide.region_15.18_spmd.sunk.clone | while | flops 1241509888 | bytes 68747440 | solution.py:207
  362.9 36.2 %all-gather.22.cloned.1.call-done = bf16[2048,576]{0,1:T(8,128)(2,1)} async-done(((bf16[1024,576]{0,1:T(8,128)(2,1)}), bf16[2048,576]{0,1:T(8,128)(2,1)}) %all-gather.22.cloned.1.call-update) | async-done | bytes 2359312 | tf_op jit(solution)/shard_map/all_gather | solution.py:62
  405.1 13.1 reduce-scatter.23.cloned.1.call-done
  430.3 8.2 reduce-scatter.25.cloned.1.call-start
  458.5 75.0 %fusion = f32[336,1152]{1,0:T(8,128)} fusion(f32[666,1152]{1,0:T(8,128)} %fusion.150), kind=kCustom, calls=%all-reduce-scatter | all-reduce-scatter fusion | flops 774145 | bytes 4617728
  537.4 6.7 concatenate.43
  566.2 10.8 while.61
  581.1 39.3 %all-gather.26.cloned.1.call-done = bf16[2048,576]{0,1:T(8,128)(2,1)} async-done(((bf16[1024,576]{0,1:T(8,128)(2,1)}), bf16[2048,576]{0,1:T(8,128)(2,1)}) %all-gather.26.cloned.1.call-update) | async-done | bytes 2359312 | tf_op jit(solution)/shard_map/all_gather | solution.py:62
  627.4 12.3 reduce-scatter.27.cloned.1.call-done
  653.4 13.8 fusion.154
  667.5 12.5 fusion.152
  680.5 201.8 %reduce-scatter.33.cloned.1.call-done = f32[1024,2304]{1,0:T(8,128)} async-done(((f32[2048,2304]{1,0:T(8,128)}), f32[1024,2304]{1,0:T(8,128)}) %reduce-scatter.33.cloned.1.call-update) | async-done | bytes 9437200 | tf_op jit(solution)/shard_map/reduce_scatter | solution.py:51
  882.3 213.9 %reduce-scatter.29.cloned.1.call-done = f32[1024,2304]{1,0:T(8,128)} async-done(((f32[2048,2304]{1,0:T(8,128)}), f32[1024,2304]{1,0:T(8,128)}) %reduce-scatter.29.cloned.1.call-update) | async-done | bytes 9437200 | tf_op jit(solution)/shard_map/reduce_scatter | solution.py:51
  1096.2 14.1 fusion.95
  1110.4 118.1 %all-gather.34.cloned.1.call-done = bf16[2048,2304]{1,0:T(8,128)(2,1)} async-done(((bf16[1024,2304]{1,0:T(8,128)(2,1)}), bf16[2048,2304]{1,0:T(8,128)(2,1)}) %all-gather.34.cloned.1.call-update) | async-done | bytes 9437200 | tf_op jit(solution)/shard_map/all_gather | solution.py:62
  1228.5 9.6 fusion.155
  1238.2 13.1 reduce-scatter.35.cloned.1.call-done
  1262.1 13.3 all-gather.36.cloned.1.call-done
  1281.8 60.6 %reduce-scatter.37.cloned.1.call-done = f32[1024,576]{0,1:T(8,128)} async-done(((f32[2048,576]{0,1:T(8,128)}), f32[1024,576]{0,1:T(8,128)}) %reduce-scatter.37.cloned.1.call-update) | async-done | bytes 2359312 | tf_op jit(solution)/shard_map/reduce_scatter | solution.py:51
  1347.5 19.9 while.62
  1379.0 35.4 %all-gather.38.cloned.1.call-done = bf16[2048,576]{0,1:T(8,128)(2,1)} async-done(((bf16[1024,576]{0,1:T(8,128)(2,1)}), bf16[2048,576]{0,1:T(8,128)(2,1)}) %all-gather.38.cloned.1.call-update) | async-done | bytes 2359312 | tf_op jit(solution)/shard_map/all_gather | solution.py:62
  1420.3 113.5 %all-gather.30.cloned.1.call-done = bf16[2048,2304]{1,0:T(8,128)(2,1)} async-done(((bf16[1024,2304]{1,0:T(8,128)(2,1)}), bf16[2048,2304]{1,0:T(8,128)(2,1)}) %all-gather.30.cloned.1.call-update) | async-done | bytes 9437200 | tf_op jit(solution)/shard_map/all_gather | solution.py:62
  1533.9 9.8 fusion.153
  1572.2 12.2 all-gather.40.cloned.1.call-done
  1590.6 60.9 %reduce-scatter.41.cloned.1.call-done = f32[1024,576]{0,1:T(8,128)} async-done(((f32[2048,576]{0,1:T(8,128)}), f32[1024,576]{0,1:T(8,128)}) %reduce-scatter.41.cloned.1.call-update) | async-done | bytes 2359312 | tf_op jit(solution)/shard_map/reduce_scatter | solution.py:51
  1658.8 132.1 %while.63 = (s32[]{:T(128)}, f32[1,1024,8,72]{1,3,2,0:T(8,128)}, f32[1,1024,8,72]{1,3,2,0:T(8,128)}, f32[2,512,8,72]{1,0,3,2:T(2,128)}, bf16[2,512,8,72]{1,3,2,0...) while((s32[]{:T(128)}, f32[1,1024,8,72]{1,3,2,0:T(8,128)}, ...), condition=%wide.region_61.62_spmd.clone, body=%wide.region_59.61_spmd.sunk.clone | while | flops 3072290816 | bytes 204325104 | solution.py:264
  1669.6 9.8 multiply_reduce_fusion.43
  1679.4 10.5 multiply_convert_fusion.13
  1701.0 24.1 dynamic_update_slice.74
  1735.5 9.8 multiply_reduce_fusion.43
  1745.2 10.5 multiply_convert_fusion.13
  1766.8 24.1 dynamic_update_slice.74
  1808.6 89.3 %all-gather.42.cloned.1.call-done = bf16[2048,1728]{0,1:T(8,128)(2,1)} async-done(((bf16[1024,1728]{0,1:T(8,128)(2,1)}), bf16[2048,1728]{0,1:T(8,128)(2,1)}) %all-gather.42.cloned.1.call-update) | async-done | bytes 7077904 | tf_op jit(solution)/shard_map/all_gather | solution.py:62
  1897.9 9.7 fusion.156
  1907.7 13.1 reduce-scatter.43.cloned.1.call-done
  1937.0 8.3 all-gather.44.cloned.1.call-done
  1945.4 9.5 fusion.157
  1956.8 10.8 convolution_convert_fusion
  1967.6 10.7 convolution_convert_fusion.1
  2008.0 80.1 %reduce-scatter.45.cloned.1.call-done = f32[1024,1152]{1,0:T(8,128)} async-done(((f32[2048,1152]{1,0:T(8,128)}), f32[1024,1152]{1,0:T(8,128)}) %reduce-scatter.45.cloned.1.call-update) | async-done | bytes 4718608 | tf_op jit(solution)/shard_map/reduce_scatter | solution.py:51
  2111.7 44.1 %all-reduce.16 = (f32[2,1152]{1,0:T(2,128)S(1)}, f32[1152]{0:T(1024)S(1)}, f32[72]{0:T(128)}, f32[72]{0:T(128)}, f32[1152]{0:T(1024)S(1)}, /*index=5*/f32[72]{0:T(128)}, f32[72]{0:T(128)}, f32[1152]{0:T(1024)S(1)}) all-reduce(f32[2,1152]{1,0:T(2,128)S(1)} %dynamic_update_slice.47, ...), channel_id=1, replica_groups=mesh['dp'=8,'row'=2,'col'=2] {'dp','row','col'}, use_global_device_ids=true, to_apply=%region_80.81 | all-reduce | flops 6048 | bytes 48384 | tf_op jit(solution)/shard_map/psum | solution.py:86
  2169.6 346.8 %all-reduce.28.cloned.1.call-done = (bf16[576,3,576]{0,2,1:T(8,128)(2,1)}, bf16[2,576,576]{2,1,0:T(8,128)(2,1)}, bf16[576,576]{1,0:T(8,128)(2,1)}, bf16[576,576]...) async-done(((bf16[576,3,576]{0,2,1:T(8,128)(2,1)}, ...) | async-done | bytes 12460048 | tf_op jit(solution)/shard_map/psum | solution.py:115
  (621 shorter events, 454.3 us)
Async XLA Ops:
  7.2 660.4 %copy-start = (bf16[576,2304]{1,0:T(8,128)(2,1)S(1)}, bf16[576,2304]{1,0:T(8,128)(2,1)}, u32[]{:S(2)}) copy-start(bf16[576,2304]{1,0:T(8,128)(2,1)} %param.52) | copy-start | bytes 7962628
  7.2 84.1 %all-gather.18.cloned.1.call-start = ((), (), s32[]{:S(2)}) async-start(), calls=%async_computation.14 | async-start | bytes 7077888 | tf_op jit(solution)/shard_map/all_gather | solution.py:62
  26.4 86.3 %reduce-scatter.19.cloned.1.call-start = ((), (), s32[]{:S(2)}) async-start(), calls=%async_computation.15 | async-start | bytes 7077888 | tf_op jit(solution)/shard_map/reduce_scatter | solution.py:35
  99.6 36.1 %all-gather.20.cloned.1.call-start = ((), (), s32[]{:S(2)}) async-start(), calls=%async_computation.16 | async-start | bytes 3538944 | tf_op jit(solution)/shard_map/all_gather | solution.py:31
  122.4 186.6 %reduce-scatter.21.cloned.1.call-start = ((), (), s32[]{:S(2)}) async-start(), calls=%async_computation.17 | async-start | bytes 21233664 | tf_op jit(solution)/shard_map/reduce_scatter | solution.py:51
  146.6 252.5 %all-gather.22.cloned.1.call-start = ((), (), s32[]{:S(2)}) async-start(), calls=%async_computation.18 | async-start | bytes 3538944 | tf_op jit(solution)/shard_map/all_gather | solution.py:62
  149.8 169.9 %copy-start.39 = (f32[1024,18]{0,1:T(8,128)}, f32[1024,18]{0,1:T(8,128)S(1)}, u32[]{:S(2)}) copy-start(f32[1024,18]{0,1:T(8,128)S(1)} %get-tuple-element.582) | copy-start | bytes 221188
  149.8 169.9 %copy-start.41 = (f32[1024,18]{0,1:T(8,128)}, f32[1024,18]{0,1:T(8,128)S(1)}, u32[]{:S(2)}) copy-start(f32[1024,18]{0,1:T(8,128)S(1)} %get-tuple-element.583) | copy-start | bytes 221188
  149.8 169.9 %copy-start.43 = (f32[1024,18]{0,1:T(8,128)}, f32[1024,18]{0,1:T(8,128)S(1)}, u32[]{:S(2)}) copy-start(f32[1024,18]{0,1:T(8,128)S(1)} %get-tuple-element.594) | copy-start | bytes 221188
  149.8 169.9 %copy-start.45 = (f32[1024,18]{0,1:T(8,128)}, f32[1024,18]{0,1:T(8,128)S(1)}, u32[]{:S(2)}) copy-start(f32[1024,18]{0,1:T(8,128)S(1)} %get-tuple-element.595) | copy-start | bytes 221188
  361.5 37.6 %copy-start.145 = (bf16[576,576]{1,0:T(8,128)(2,1)S(1)}, bf16[576,576]{1,0:T(8,128)(2,1)}, u32[]{:S(2)}) copy-start(bf16[576,576]{1,0:T(8,128)(2,1)} %param.44) | copy-start | bytes 1990660
  362.9 55.3 %reduce-scatter.23.cloned.1.call-start = ((), (), s32[]{:S(2)}) async-start(), calls=%async_computation.19 | async-start | bytes 7077888 | tf_op jit(solution)/shard_map/reduce_scatter | solution.py:35
  405.0 38.6 %all-gather.24.cloned.1.call-start = ((), (), s32[]{:S(2)}) async-start(), calls=%async_computation.20 | async-start | bytes 3538944 | tf_op jit(solution)/shard_map/all_gather | solution.py:31
  430.3 123.9 %reduce-scatter.25.cloned.1.call-start = ((), (), s32[]{:S(2)}) async-start(), calls=%async_computation.21 | async-start | bytes 7077888 | tf_op jit(solution)/shard_map/reduce_scatter | solution.py:51
  449.6 170.8 %all-gather.26.cloned.1.call-start = ((), (), s32[]{:S(2)}) async-start(), calls=%async_computation.22 | async-start | bytes 3538944 | tf_op jit(solution)/shard_map/all_gather | solution.py:62
  458.5 77.6 %copy-start.131 = (u32[32]{0:T(128)S(1)}, u32[32]{0:T(128)}, u32[]{:S(2)}) copy-start(u32[32]{0:T(128)} %constant.278) | copy-start | bytes 388
  534.2 3.2 collective-permute-start
  580.9 58.8 %reduce-scatter.27.cloned.1.call-start = ((), (), s32[]{:S(2)}) async-start(), calls=%async_computation.23 | async-start | bytes 7077888 | tf_op jit(solution)/shard_map/reduce_scatter | solution.py:35
  626.6 26.8 %all-gather.32.cloned.1.call-start = ((), (), s32[]{:S(2)}) async-start(), calls=%async_computation.28 | async-start | bytes 3538944 | tf_op jit(solution)/shard_map/all_gather | solution.py:31
  627.3 40.2 %all-gather.28.cloned.1.call-start = ((), (), s32[]{:S(2)}) async-start(), calls=%async_computation.24 | async-start | bytes 3538944 | tf_op jit(solution)/shard_map/all_gather | solution.py:31
  652.7 229.6 %reduce-scatter.33.cloned.1.call-start = ((), (), s32[]{:S(2)}) async-start(), calls=%async_computation.29 | async-start | bytes 28311552 | tf_op jit(solution)/shard_map/reduce_scatter | solution.py:51
  667.2 429.0 %reduce-scatter.29.cloned.1.call-start = ((), (), s32[]{:S(2)}) async-start(), calls=%async_computation.25 | async-start | bytes 28311552 | tf_op jit(solution)/shard_map/reduce_scatter | solution.py:51
  680.1 548.4 %all-gather.34.cloned.1.call-start = ((), (), s32[]{:S(2)}) async-start(), calls=%async_computation.30 | async-start | bytes 14155776 | tf_op jit(solution)/shard_map/all_gather | solution.py:62
  1110.4 140.9 %reduce-scatter.35.cloned.1.call-start = ((), (), s32[]{:S(2)}) async-start(), calls=%async_computation.31 | async-start | bytes 7077888 | tf_op jit(solution)/shard_map/reduce_scatter | solution.py:35
  1238.2 37.3 %all-gather.36.cloned.1.call-start = ((), (), s32[]{:S(2)}) async-start(), calls=%async_computation.32 | async-start | bytes 3538944 | tf_op jit(solution)/shard_map/all_gather | solution.py:31
  1262.1 80.4 %reduce-scatter.37.cloned.1.call-start = ((), (), s32[]{:S(2)}) async-start(), calls=%async_computation.33 | async-start | bytes 7077888 | tf_op jit(solution)/shard_map/reduce_scatter | solution.py:51
  1281.5 132.9 %all-gather.38.cloned.1.call-start = ((), (), s32[]{:S(2)}) async-start(), calls=%async_computation.34 | async-start | bytes 3538944 | tf_op jit(solution)/shard_map/all_gather | solution.py:62
  1378.2 155.7 %all-gather.30.cloned.1.call-start = ((), (), s32[]{:S(2)}) async-start(), calls=%async_computation.26 | async-start | bytes 14155776 | tf_op jit(solution)/shard_map/all_gather | solution.py:62
  1378.2 36.2 %copy-start.144 = (bf16[576,576]{1,0:T(8,128)(2,1)S(1)}, bf16[576,576]{1,0:T(8,128)(2,1)}, u32[]{:S(2)}) copy-start(bf16[576,576]{1,0:T(8,128)(2,1)} %param.46) | copy-start | bytes 1990660
  1378.8 170.9 %reduce-scatter.39.cloned.1.call-start = ((), (), s32[]{:S(2)}) async-start(), calls=%async_computation.35 | async-start | bytes 7077888 | tf_op jit(solution)/shard_map/reduce_scatter | solution.py:35
  1420.3 113.6 %copy-start.132 = (bf16[2304,576]{0,1:T(8,128)(2,1)S(1)}, bf16[2304,576]{0,1:T(8,128)(2,1)}, u32[]{:S(2)}) copy-start(bf16[2304,576]{0,1:T(8,128)(2,1)} %param.53) | copy-start | bytes 7962628
  1420.3 145.6 %reduce-scatter.31.cloned.1.call-start = ((), (), s32[]{:S(2)}) async-start(), calls=%async_computation.27 | async-start | bytes 7077888 | tf_op jit(solution)/shard_map/reduce_scatter | solution.py:35
  1543.7 40.7 %all-gather.40.cloned.1.call-start = ((), (), s32[]{:S(2)}) async-start(), calls=%async_computation.36 | async-start | bytes 3538944 | tf_op jit(solution)/shard_map/all_gather | solution.py:31
  1572.1 79.3 %reduce-scatter.41.cloned.1.call-start = ((), (), s32[]{:S(2)}) async-start(), calls=%async_computation.37 | async-start | bytes 7077888 | tf_op jit(solution)/shard_map/reduce_scatter | solution.py:51
  1590.5 307.4 %all-gather.42.cloned.1.call-start = ((), (), s32[]{:S(2)}) async-start(), calls=%async_computation.38 | async-start | bytes 10616832 | tf_op jit(solution)/shard_map/all_gather | solution.py:62
  1699.7 25.3 copy-start.4
  1765.6 25.3 copy-start.4
  1808.5 89.4 %copy-start.48 = (bf16[576,3,576]{0,2,1:T(8,128)(2,1)S(1)}, bf16[576,3,576]{0,2,1:T(8,128)(2,1)}, u32[]{:S(2)}) copy-start(bf16[576,3,576]{0,2,1:T(8,128)(2,1)} %copy.81) | copy-start | bytes 5971972
  1808.5 112.3 %reduce-scatter.43.cloned.1.call-start = ((), (), s32[]{:S(2)}) async-start(), calls=%async_computation.39 | async-start | bytes 7077888 | tf_op jit(solution)/shard_map/reduce_scatter | solution.py:35
  1907.7 37.7 %all-gather.44.cloned.1.call-start = ((), (), s32[]{:S(2)}) async-start(), calls=%async_computation.40 | async-start | bytes 3538944 | tf_op jit(solution)/shard_map/all_gather | solution.py:31
  1932.0 49.4 %all-gather.46.cloned.1.call-start = ((), (), s32[]{:S(2)}) async-start(), calls=%async_computation.42 | async-start | bytes 2322432 | tf_op jit(solution)/shard_map/all_gather | solution.py:62
  1937.0 151.1 %reduce-scatter.45.cloned.1.call-start = ((), (), s32[]{:S(2)}) async-start(), calls=%async_computation.41 | async-start | bytes 14155776 | tf_op jit(solution)/shard_map/reduce_scatter | solution.py:51
  1954.9 561.5 %all-reduce.28.cloned.1.call-start = ((), (), s32[]{:S(2)}) async-start(), calls=%async_computation.43 | async-start | bytes 26247168 | tf_op jit(solution)/shard_map/psum | solution.py:115
  2006.3 81.8 %copy-start.97 = (f32[1152]{0:T(1024)S(1)}, f32[1152]{0:T(1024)}, u32[]{:S(2)}) copy-start(f32[1152]{0:T(1024)} %copy-done.96) | copy-start | bytes 13828
  2006.4 81.8 %copy-start.99 = (f32[1024]{0:T(1024)S(1)}, f32[1024]{0:T(1024)}, u32[]{:S(2)}) copy-start(f32[1024]{0:T(1024)} %copy-done.98) | copy-start | bytes 12292
  2006.4 81.8 %copy-start.101 = (f32[1024]{0:T(1024)S(1)}, f32[1024]{0:T(1024)}, u32[]{:S(2)}) copy-start(f32[1024]{0:T(1024)} %copy-done.100) | copy-start | bytes 12292
  2008.0 88.6 %copy-start.120 = (bf16[2,576]{1,0:T(2,128)(2,1)S(1)}, bf16[2,576]{1,0:T(2,128)(2,1)}, u32[]{:S(2)}) copy-start(bf16[2,576]{1,0:T(2,128)(2,1)} %param.33) | copy-start | bytes 6916
  2106.3 3.1 collective-permute-start.1
  (150 other events, 678.7 us)
Sparse Core Ops, SparseCore 0:
  26.5 64.7 all-gather.17
  99.7 12.9 reduce-scatter.18
  122.5 13.2 all-gather.19
  146.7 162.2 reduce-scatter.20
  363.0 36.0 all-gather.21
  405.2 12.9 reduce-scatter.22
  430.4 13.1 all-gather.23
  449.7 93.9 reduce-scatter.24
  581.0 39.4 all-gather.25
  626.7 12.9 reduce-scatter.26
  641.2 12.1 all-gather.31
  655.4 12.1 all-gather.27
  669.8 212.4 reduce-scatter.32
  884.5 211.6 reduce-scatter.28
  1110.5 117.9 all-gather.33
  1238.3 12.9 reduce-scatter.34
  1262.2 13.2 all-gather.35
  1281.7 60.7 reduce-scatter.36
  1378.3 36.0 all-gather.37
  1415.8 117.9 all-gather.29
  1536.7 12.9 reduce-scatter.38
  1552.1 13.7 reduce-scatter.30
  1572.2 12.1 all-gather.39
  1590.6 60.7 reduce-scatter.40
  1808.6 89.2 all-gather.41
  1907.8 12.9 reduce-scatter.42
  1932.1 13.2 all-gather.43
  1947.5 27.7 all-gather.45
  1977.5 110.5 reduce-scatter.44
  2098.5 417.9 all-reduce.27
where the time goes:
time: 2560 us; the launch traced here: 2540 us
  waiting for transfers between devices  1750 us (68%)
  matrix products  262 us (10%)
  other arithmetic  177 us (7%)
  local copies, waits for them, and re-layouts  166 us (6%)
  blocking collectives  158 us (6%)
    reduce_scatter x7, waiting for transfers between devices, to_heads(): lax.psum_scatter(partial_term(jnp.int32(0), own_rows * lax.axis_size('row...  776 us
    all_gather x8, waiting for transfers between devices, to_tokens(): gathered = lax.all_gather(values, 'row', axis=0, tiled=True)  497 us
    psum x1, waiting for transfers between devices, finish_weights(): lax.psum(grad_self.astype(jnp.bfloat16), 'dp').astype(jnp.float32)  347 us
    dot_general x17, matrix products, contract(): lax.dot_general(left_side, right_side, numbers, preferred_element_type=jn...  127 us
    unnamed x2, blocking collectives  79.2 us
    reduce_scatter x7, waiting for transfers between devices, spread_cols(): lax.psum_scatter(term_fn(jnp.int32(0), own_rows * lax.axis_size('col')),...  75.8 us
  transfers between devices with their start and end apart: 32, of which 29 were waited for; matrix products, arithmetic and copies ran while one was open for 10% of the time, Pallas kernels for 0%

commit v1 on v0

v1 whole, which is shorter than its diff:
```python
import jax
import jax.numpy as jnp
from jax import lax
from jax.sharding import PartitionSpec as P

D = 1152
HD = 72
TXT = 333
LAT = 1024


EPSILON = 1e-06
PRECISE = lax.Precision.HIGHEST
SWAP = [(0, 1), (1, 0)]
BF16 = jnp.bfloat16
F32 = jnp.float32


def other_core(values):
    return lax.ppermute(values, "col", SWAP)


def other_chip(values):
    return lax.ppermute(values, "row", SWAP)


def contract(left_side, right_side, transposed=False):
    numbers = (((1,), (1 if transposed else 0,)), ((), ()))
    return lax.dot_general(left_side, right_side, numbers, preferred_element_type=F32)


def token_sum(left_side, right_side):
    return lax.dot_general(
        left_side, right_side, (((0,), (0,)), ((), ())), preferred_element_type=F32
    )


def both_halves(own, weight, transposed=False):
    other = other_core(own)
    product = jnp.concatenate(
        [contract(own, weight, transposed), contract(other, weight, transposed)]
    )
    return product, jnp.concatenate([own, other])


def own_half(values, weight, transposed=False):
    half = values.shape[0] // 2
    sent = contract(values[half:], weight, transposed)
    return contract(values[:half], weight, transposed) + other_core(sent)


def after(values, earlier):
    return lax.optimization_barrier((values, earlier))[0]


def head_norm(values, norm_gain):
    average = jnp.mean(values, axis=-1, keepdims=True)
    variance = jnp.mean(values * values, axis=-1, keepdims=True) - average * average
    return (values - average) * lax.rsqrt(variance + EPSILON) * norm_gain


def gelu_tanh(values):
    return jax.nn.gelu(values, approximate=True)


def rotate(values, row_place, col_place):
    half_width = values.shape[-1] // 2
    quarter = half_width // 2
    frequency = 10000.0 ** (-jnp.arange(quarter, dtype=jnp.float32) / quarter)

    def turn_half(portion, place):
        angles = place[:, None] * frequency[None, :]
        cosine = jnp.cos(angles)[:, None, :]
        sine_value = jnp.sin(angles)[:, None, :]
        leading = portion[..., :quarter]
        trailing = portion[..., quarter:]
        return jnp.concatenate(
            [leading * cosine - trailing * sine_value, trailing * cosine + leading * sine_value],
            axis=-1,
        )

    return jnp.concatenate(
        [
            turn_half(values[..., :half_width], row_place),
            turn_half(values[..., half_width:], col_place),
        ],
        axis=-1,
    )


def norm_rows(values):
    average = jnp.mean(values, axis=1, keepdims=True)
    variance = jnp.mean(values * values, axis=1, keepdims=True) - average * average
    inverse = lax.rsqrt(variance + EPSILON)
    return ((values - average) * inverse, inverse)


def norm_rows_back(grad_normed, normed, inverse, norm_gain):
    scaled = grad_normed * norm_gain
    first_mean = jnp.mean(scaled, axis=1, keepdims=True)
    second_mean = jnp.mean(scaled * normed, axis=1, keepdims=True)
    grad_input = inverse * (scaled - first_mean - normed * second_mean)
    return (grad_input, jnp.sum(grad_normed * normed, axis=0))


def attend_forward(queries, key_rows, value_rows, key_len, first_row, block_len):
    heads_here = queries.shape[1]
    head_width = queries.shape[2]
    score_scale = head_width ** (-0.5)
    groups = key_rows.shape[0] // key_len
    key_groups = key_rows.reshape(groups, key_len, heads_here, head_width)
    value_groups = value_rows.reshape(groups, key_len, heads_here, head_width)
    block_count = queries.shape[0] // block_len
    query_blocks = queries.reshape(block_count, block_len, heads_here, head_width)
    block_ids = jnp.arange(block_count, dtype=jnp.int32)

    def one_block(packed):
        block_id, query_block = packed
        group_index = (first_row + block_id * block_len) // LAT
        key_block = lax.dynamic_index_in_dim(key_groups, group_index, 0, keepdims=False)
        value_block = lax.dynamic_index_in_dim(value_groups, group_index, 0, keepdims=False)
        scores = (
            jnp.einsum("qhe,khe->hqk", query_block, key_block, preferred_element_type=jnp.float32)
            * score_scale
        )
        row_top = jnp.max(scores, axis=-1, keepdims=True)
        row_total = jnp.sum(jnp.exp(scores - row_top), axis=-1, keepdims=True)
        log_total = row_top + jnp.log(row_total)
        weights_low = jnp.exp(scores - log_total).astype(jnp.bfloat16)
        output = jnp.einsum(
            "hqk,khe->qhe", weights_low, value_block, preferred_element_type=jnp.float32
        )
        return (output, log_total[..., 0])

    outputs, log_totals = lax.map(one_block, (block_ids, query_blocks))
    return (outputs.reshape(queries.shape), log_totals)


def attend_backward(
    queries, key_rows, value_rows, grad_heads, log_totals, key_len, first_row, block_len
):
    heads_here = queries.shape[1]
    head_width = queries.shape[2]
    score_scale = head_width ** (-0.5)
    groups = key_rows.shape[0] // key_len
    key_groups = key_rows.reshape(groups, key_len, heads_here, head_width)
    value_groups = value_rows.reshape(groups, key_len, heads_here, head_width)
    block_count = queries.shape[0] // block_len
    query_blocks = queries.reshape(block_count, block_len, heads_here, head_width)
    grad_blocks = grad_heads.reshape(block_count, block_len, heads_here, head_width)
    block_ids = jnp.arange(block_count, dtype=jnp.int32)

    def one_block(carry, packed):
        key_store, value_store = carry
        block_id, query_block, grad_block, log_block = packed
        group_index = (first_row + block_id * block_len) // LAT
        key_block = lax.dynamic_index_in_dim(key_groups, group_index, 0, keepdims=False)
        value_block = lax.dynamic_index_in_dim(value_groups, group_index, 0, keepdims=False)
        scores = (
            jnp.einsum("qhe,khe->hqk", query_block, key_block, preferred_element_type=jnp.float32)
            * score_scale
        )
        weights_full = jnp.exp(scores - log_block[..., None])
        grad_weights = jnp.einsum(
            "qhe,khe->hqk", grad_block, value_block, preferred_element_type=jnp.float32
        )
        inner_sum = jnp.sum(weights_full * grad_weights, axis=-1, keepdims=True)
        grad_scores = (weights_full * (grad_weights - inner_sum)).astype(jnp.bfloat16)
        grad_query = (
            jnp.einsum("hqk,khe->qhe", grad_scores, key_block, preferred_element_type=jnp.float32)
            * score_scale
        )
        grad_key = (
            jnp.einsum("hqk,qhe->khe", grad_scores, query_block, preferred_element_type=jnp.float32)
            * score_scale
        )
        grad_value = jnp.einsum(
            "hqk,qhe->khe",
            weights_full.astype(jnp.bfloat16),
            grad_block,
            preferred_element_type=jnp.float32,
        )
        key_now = lax.dynamic_index_in_dim(key_store, group_index, 0, keepdims=False) + grad_key
        value_now = (
            lax.dynamic_index_in_dim(value_store, group_index, 0, keepdims=False) + grad_value
        )
        key_store = lax.dynamic_update_index_in_dim(key_store, key_now, group_index, 0)
        value_store = lax.dynamic_update_index_in_dim(value_store, value_now, group_index, 0)
        return ((key_store, value_store), grad_query)

    empty = jnp.zeros((groups, key_len, heads_here, head_width), jnp.float32)
    (key_store, value_store), grad_query = lax.scan(
        one_block, (empty, empty), (block_ids, query_blocks, grad_blocks, log_totals)
    )
    return (
        grad_query.reshape(queries.shape),
        key_store.reshape(key_rows.shape),
        value_store.reshape(value_rows.shape),
    )


def shards(
    latents,
    skip_input,
    condition,
    text_states,
    positions,
    cotangent,
    skip_gain,
    skip_weight,
    shift_weight,
    self_gain,
    self_weight,
    query_gain,
    key_gain,
    self_out,
    cross_gain,
    cross_query,
    cross_context,
    cross_query_gain,
    cross_key_gain,
    cross_out,
    feed_gain,
    up_weight,
    down_weight,
):
    tokens, width = latents.shape
    half = tokens // 2
    heads_here = width // HD
    core = lax.axis_index("col")
    chip = lax.axis_index("row")
    straight = core == chip

    def own_first(values):
        return (
            lax.dynamic_slice_in_dim(values, core * half, half, 0),
            lax.dynamic_slice_in_dim(values, (1 - core) * half, half, 0),
        )

    def in_order(own, other):
        return jnp.where(
            core == 0, jnp.concatenate([own, other]), jnp.concatenate([other, own])
        )

    skip_flat = skip_weight.reshape(2 * width, -1)
    self_flat = self_weight.reshape(-1, 3 * width)
    context_flat = cross_context.reshape(-1, 2 * width)

    def whole(weight, axis):
        return jnp.concatenate([weight, other_chip(weight)], axis=axis)

    skip_all = whole(skip_flat, 1)
    self_all = whole(self_flat, 0)
    self_out_all = whole(self_out, 1)
    context_all = whole(context_flat, 0)
    query_all = whole(cross_query, 0)
    cross_out_all = whole(cross_out, 1)
    up_all = whole(up_weight, 0)
    down_all = whole(down_weight, 1)
    norm_gains = jnp.stack([self_gain, cross_gain, feed_gain])
    norm_gains = jnp.concatenate([norm_gains, other_chip(norm_gains)], axis=1)
    self_gain_all, cross_gain_all, feed_gain_all = norm_gains[0], norm_gains[1], norm_gains[2]

    text_near = other_core(text_states)
    text_mine = jnp.where(straight, text_states, text_near)
    text_far = other_chip(jnp.where(straight, text_near, text_states))
    text_all = jnp.concatenate([text_mine, text_far], axis=1)
    kept, handed = own_first(cotangent)
    handed = other_core(handed)
    cot_mine = jnp.where(straight, kept, handed)
    cot_far = other_chip(jnp.where(straight, handed, kept))
    cot_own = jnp.concatenate([cot_mine, cot_far], axis=1)

    place_own, place_other = own_first(positions)
    places = jnp.concatenate([place_own, place_other]).astype(F32)
    row_place = places[:, 0]
    col_place = places[:, 1]
    block_len = min(512, LAT)

    lat_own, lat_other = own_first(latents)
    skip_own, skip_other = own_first(skip_input)
    joined = jnp.stack(
        [jnp.concatenate([lat_own, lat_other]), jnp.concatenate([skip_own, skip_other])], axis=1
    ).astype(F32)
    sums = jnp.stack([jnp.sum(joined, axis=(1, 2)), jnp.sum(joined * joined, axis=(1, 2))])

    def swap_halves(values):
        return jnp.concatenate([values[:, half:], values[:, :half]], axis=1)

    sums = sums + swap_halves(other_core(sums))
    average = sums[0] / (2 * D)
    variance = sums[1] / (2 * D) - average * average
    skip_inverse = lax.rsqrt(variance + EPSILON)
    skip_normed = (joined - average[:, None, None]) * skip_inverse[:, None, None]
    skip_low = (skip_normed * skip_gain).astype(BF16).reshape(tokens, 2 * width)
    first_state = own_half(skip_low, skip_all)

    cond_low = jax.nn.silu(condition.astype(F32)).astype(BF16)
    shift_part = contract(cond_low, shift_weight)
    shift_part = shift_part + other_core(shift_part)
    shift_mine = lax.dynamic_slice_in_dim(shift_part, chip, 1, 0)
    shift_far = other_chip(lax.dynamic_slice_in_dim(shift_part, 1 - chip, 1, 0))
    shift_row = jnp.concatenate([shift_mine, shift_far], axis=1)

    normed_one, inverse_one = norm_rows(first_state)
    first_input = (normed_one * self_gain_all + shift_row).astype(BF16)
    mixed_raw, first_all = both_halves(first_input, self_all)
    mixed_raw = mixed_raw.reshape(tokens, 3, heads_here, HD)

    def shape_query(raw_part, norm_gain):
        return rotate(head_norm(raw_part, norm_gain), row_place, col_place)

    query_float, query_pull = jax.vjp(shape_query, mixed_raw[:, 0], query_gain)
    key_float, key_pull = jax.vjp(shape_query, mixed_raw[:, 1], key_gain)
    queries = query_float.astype(BF16)
    key_rows = key_float.astype(BF16)
    value_rows = mixed_raw[:, 2].astype(BF16)
    heads_float, log_first = attend_forward(queries, key_rows, value_rows, LAT, 0, block_len)
    heads_low = heads_float.astype(BF16).reshape(tokens, width)
    second_state = first_state + own_half(heads_low, self_out_all)

    normed_two, inverse_two = norm_rows(second_state)
    cross_input = (normed_two * cross_gain_all).astype(BF16)
    probe_raw, cross_all = both_halves(cross_input, query_all)
    probe_raw = probe_raw.reshape(tokens, heads_here, HD)
    memory_raw = contract(text_all, context_all)
    text_here = memory_raw.shape[0]
    memory_raw = memory_raw.reshape(text_here, 2, heads_here, HD)
    probe_float, probe_pull = jax.vjp(head_norm, probe_raw, cross_query_gain)
    memory_float, memory_pull = jax.vjp(head_norm, memory_raw[:, 0], cross_key_gain)
    probes = probe_float.astype(BF16)
    memory_keys = memory_float.astype(BF16)
    memory_values = memory_raw[:, 1].astype(BF16)
    cross_float, log_second = attend_forward(probes, memory_keys, memory_values, TXT, 0, block_len)
    cross_low = cross_float.astype(BF16).reshape(tokens, width)
    third_state = second_state + own_half(cross_low, cross_out_all)

    normed_three, inverse_three = norm_rows(third_state)
    feed_input = (normed_three * feed_gain_all).astype(BF16)
    hidden_raw, feed_all = both_halves(feed_input, up_all)
    hidden_float, gelu_pull = jax.vjp(gelu_tanh, hidden_raw)
    hidden_low = hidden_float.astype(BF16)
    out_own = (third_state + own_half(hidden_low, down_all)).astype(BF16)
    row_width = up_weight.shape[0]
    out_mine = out_own[:, :row_width]
    out_far = other_chip(out_own[:, row_width:])
    out_kept = jnp.where(straight, out_mine, out_far)
    out_got = other_core(jnp.where(straight, out_far, out_mine))
    block_out = in_order(out_kept, out_got)

    grad_hidden, cot_all = both_halves(cot_own, down_all, True)
    grad_down = token_sum(hidden_low, cot_all)
    grad_pre = gelu_pull(grad_hidden)[0].astype(BF16)
    grad_up = token_sum(feed_all, grad_pre)
    grad_feed_in = own_half(grad_pre, up_all, True)
    back_three, feed_gain_part = norm_rows_back(
        grad_feed_in, normed_three, inverse_three, feed_gain_all
    )
    grad_third = cot_own.astype(F32) + back_three

    branch_two = grad_third.astype(BF16)
    grad_cross_heads, branch_two_all = both_halves(branch_two, cross_out_all, True)
    grad_cross_out = token_sum(cross_low, branch_two_all)
    grad_cross_low = grad_cross_heads.astype(BF16).reshape(tokens, heads_here, HD)
    grad_probe, grad_memory_key, grad_memory_value = attend_backward(
        probes, memory_keys, memory_values, grad_cross_low, log_second, TXT, 0, block_len
    )
    grad_probe_raw, grad_probe_gain = probe_pull(grad_probe)
    probe_low = grad_probe_raw.astype(BF16).reshape(tokens, width)
    grad_cross_query = token_sum(cross_all, probe_low)
    grad_cross_in = own_half(probe_low, query_all, True)
    grad_memory_raw, grad_memory_gain = memory_pull(grad_memory_key)
    memory_low = jnp.stack([grad_memory_raw, grad_memory_value], axis=1).astype(BF16)
    memory_low = memory_low.reshape(text_here, 2 * width)
    grad_context = token_sum(text_all, memory_low)
    text_part = contract(memory_low, context_all, True)
    text_width = text_states.shape[1]
    text_one, text_two = text_part[:, :text_width], text_part[:, text_width:]
    text_sum = jnp.where(straight, text_one, text_two) + other_core(
        jnp.where(straight, text_two, text_one)
    )
    text_sum = text_sum.astype(BF16)
    text_back = lax.ppermute(text_sum, ("row", "col"), [(1, 2), (2, 1)])
    grad_text_states = jnp.where(straight, text_sum, text_back)

    back_two, cross_gain_part = norm_rows_back(
        grad_cross_in, normed_two, inverse_two, cross_gain_all
    )
    grad_second = grad_third + back_two
    branch_one = grad_second.astype(BF16)
    grad_heads, branch_one_all = both_halves(branch_one, self_out_all, True)
    grad_self_out = token_sum(heads_low, branch_one_all)
    grad_heads_low = grad_heads.astype(BF16).reshape(tokens, heads_here, HD)
    grad_query, grad_key, grad_value = attend_backward(
        queries, key_rows, value_rows, grad_heads_low, log_first, LAT, 0, block_len
    )
    grad_query_raw, grad_query_gain = query_pull(grad_query)
    grad_key_raw, grad_key_gain = key_pull(grad_key)
    mixed_low = jnp.stack([grad_query_raw, grad_key_raw, grad_value], axis=1).astype(BF16)
    mixed_low = mixed_low.reshape(tokens, 3 * width)
    grad_self_weight = token_sum(first_all, mixed_low)
    grad_first_in = own_half(mixed_low, self_all, True)

    shift_grad = jnp.sum(grad_first_in, axis=0, keepdims=True)
    shift_grad = shift_grad + other_core(shift_grad)
    shift_here = shift_grad[:, :row_width]
    shift_there = other_chip(shift_grad[:, row_width:])
    shift_pair = jnp.where(
        chip == 0,
        jnp.concatenate([shift_here, shift_there]),
        jnp.concatenate([shift_there, shift_here]),
    )
    cond_every = lax.all_gather(cond_low, "dp", axis=0, tiled=True)
    shift_every = lax.all_gather(shift_pair, "dp", axis=0, tiled=True)
    grad_shift_weight = lax.dot_general(
        cond_every.astype(F32),
        shift_every,
        (((0,), (0,)), ((), ())),
        precision=PRECISE,
        preferred_element_type=F32,
    )

    back_one, self_gain_part = norm_rows_back(grad_first_in, normed_one, inverse_one, self_gain_all)
    grad_first = grad_second + back_one
    grad_skip_out, grad_first_all = both_halves(grad_first.astype(BF16), skip_all, True)
    grad_skip_weight = token_sum(skip_low, grad_first_all)
    grad_joined_out = grad_skip_out.reshape(tokens, 2, width)
    scaled = grad_joined_out * skip_gain
    sums_back = jnp.stack(
        [jnp.sum(scaled, axis=(1, 2)), jnp.sum(scaled * skip_normed, axis=(1, 2))]
    )
    sums_back = sums_back + swap_halves(other_core(sums_back))
    first_mean = (sums_back[0] / (2 * D))[:, None, None]
    second_mean = (sums_back[1] / (2 * D))[:, None, None]
    grad_joined = skip_inverse[:, None, None] * (scaled - first_mean - skip_normed * second_mean)
    skip_gain_part = jnp.sum(grad_joined_out * skip_normed, axis=0)
    grad_joined = grad_joined.astype(BF16)
    grad_latents = in_order(grad_joined[:half, 0], grad_joined[half:, 0])
    grad_skip_input = in_order(grad_joined[:half, 1], grad_joined[half:, 1])

    wide = jnp.stack([self_gain_part, cross_gain_part, feed_gain_part])
    wide = wide + other_core(wide)
    narrow = jnp.stack([grad_query_gain, grad_key_gain, grad_probe_gain, grad_memory_gain])
    narrow = narrow + other_core(narrow)

    def flat(*pieces):
        return jnp.concatenate([piece.reshape(-1) for piece in pieces])

    kept_gains = flat(wide[:, :row_width], narrow, skip_gain_part)
    sent_gains = flat(wide[:, row_width:], narrow, skip_gain_part)
    gain_sums = lax.psum(kept_gains + other_chip(sent_gains), "dp")
    wide_sum = gain_sums[: 3 * row_width].reshape(3, row_width)
    narrow_sum = gain_sums[3 * row_width : 3 * row_width + 4 * HD].reshape(4, HD)
    grad_skip_gain = gain_sums[3 * row_width + 4 * HD :].reshape(2, width)

    def chip_sum(grad, axis):
        size = grad.shape[axis] // 2
        own = lax.slice_in_dim(grad, 0, size, axis=axis)
        sent = lax.slice_in_dim(grad, size, 2 * size, axis=axis).astype(BF16)
        return (own + other_chip(sent).astype(F32)).astype(BF16)

    pieces = [
        chip_sum(grad_down, 1),
        chip_sum(grad_up, 0),
        chip_sum(grad_cross_out, 1),
        chip_sum(grad_cross_query, 0),
        chip_sum(grad_context, 0),
        chip_sum(grad_self_out, 1),
        chip_sum(grad_self_weight, 0),
        chip_sum(grad_skip_weight, 1),
    ]
    totals = []
    for piece in pieces:
        if totals:
            piece = after(piece, totals[-1])
        totals.append(lax.psum(piece, "dp"))
    (
        grad_down,
        grad_up,
        grad_cross_out,
        grad_cross_query,
        grad_context,
        grad_self_out,
        grad_self_weight,
        grad_skip_weight,
    ) = [total.astype(F32) for total in totals]
    return (
        block_out,
        grad_latents,
        grad_skip_input,
        grad_text_states,
        grad_skip_gain,
        grad_skip_weight.reshape(skip_weight.shape),
        grad_shift_weight,
        wide_sum[0],
        grad_self_weight.reshape(self_weight.shape),
        narrow_sum[0],
        narrow_sum[1],
        grad_self_out,
        wide_sum[1],
        grad_cross_query,
        grad_context.reshape(cross_context.shape),
        narrow_sum[2],
        narrow_sum[3],
        grad_cross_out,
        wide_sum[2],
        grad_up,
        grad_down,
    )


def solution(mesh):
    placed = (
        P(("dp", "row"), "col"),
        P(("dp", "row"), "col"),
        P("dp", "col"),
        P(("dp", "col"), "row"),
        P(("dp", "row"), None),
        P(("dp", "col"), "row"),
        P(None, "col"),
        P(None, "col", "row"),
        P("col", "row"),
        P("row"),
        P("row", None, "col"),
        P(),
        P(),
        P("col", "row"),
        P("row"),
        P("row", "col"),
        P("row", None, "col"),
        P(),
        P(),
        P("col", "row"),
        P("row"),
        P("row", "col"),
        P("col", "row"),
    )
    return jax.shard_map(
        shards,
        mesh=mesh,
        in_specs=placed,
        out_specs=(
            P(("dp", "col"), "row"),
            P(("dp", "row"), "col"),
            P(("dp", "row"), "col"),
            P(("dp", "col"), "row"),
            P(None, "col"),
            P(None, "col", "row"),
            P("col", "row"),
            P("row"),
            P("row", None, "col"),
            P(),
            P(),
            P("col", "row"),
            P("row"),
            P("row", "col"),
            P("row", None, "col"),
            P(),
            P(),
            P("col", "row"),
            P("row"),
            P("row", "col"),
            P("col", "row"),
        ),
        check_vma=False,
    )
```

time: 2560 us -> 1450 us (0.57)
  waiting for transfers between devices: 1750 us -> 638 us
  local copies, waits for them, and re-layouts: 166 us -> 253 us
  blocking collectives: 158 us -> 79.5 us
  other arithmetic: 177 us -> 146 us
    reduce_scatter x14 -> x0, waiting for transfers between devices: 852 us -> none  [the longest x7 776 us: to_heads(): lax.psum_scatter(partial_term(jnp.int32(0), own_rows * lax.axis_size('row...]
    all_gather x15 -> x0, waiting for transfers between devices: 546 us -> none  [the longest x8 497 us: to_tokens(): gathered = lax.all_gather(values, 'row', axis=0, tiled=True)]
    ppermute x0 -> x48, waiting for transfers between devices: none -> 338 us  [the longest x23 310 us: other_chip(): return lax.ppermute(values, 'row', SWAP)]
    unnamed x2 -> x0, blocking collectives: 79.2 us -> none
    psum x1 -> x8, waiting for transfers between devices: 347 us -> 300 us  [shards(): totals.append(lax.psum(piece, 'dp'))]
    all_gather x1 -> x2, blocking collectives: 2.42 us -> 48.7 us  [the longest x1 24.5 us: shards(): cond_every = lax.all_gather(cond_low, 'dp', axis=0, tiled=True)]
    psum x9 -> x1, blocking collectives: 76.4 us -> 30.8 us  [shards(): gain_sums = lax.psum(kept_gains + other_chip(sent_gains), 'dp')]
    ppermute x0 -> x48, starting transfers between devices: none -> 35.9 us  [the longest x24 17.7 us: other_core(): return lax.ppermute(values, 'col', SWAP)]
  transfers between devices with their start and end apart: 32 -> 56, of which waited for: 29 -> 17; matrix products, arithmetic and copies ran while one was open for 10% -> 40% of each run, Pallas kernels for 0% -> 0%
where the time goes in v1:
time: 1450 us; the launch traced here: 1430 us
  waiting for transfers between devices  638 us (44%)
  matrix products  260 us (18%)
  local copies, waits for them, and re-layouts  253 us (17%)
  other arithmetic  146 us (10%)
  blocking collectives  79.5 us (5%)
  starting transfers between devices  37.5 us (3%)
  between operations  17.1 us (1%)
    ppermute x23, waiting for transfers between devices, other_chip(): return lax.ppermute(values, 'row', SWAP)  310 us
    psum x8, waiting for transfers between devices, shards(): totals.append(lax.psum(piece, 'dp'))  300 us
    dot_general x31, matrix products, contract(): lax.dot_general(left_side, right_side, numbers, preferred_element_type=F32)  133 us
    unnamed x380, local copies, waits for them, and re-layouts  61.3 us
    dynamic_update_slice x4, local copies, waits for them, and re-layouts, attend_forward(): outputs, log_totals = lax.map(one_block, (block_ids, query_blocks))  52.8 us
    dot_general x8, matrix products, token_sum(): lax.dot_general(left_side, right_side, (((0,), (0,)), ((), ())), preferre...  37.5 us
    psum x1, blocking collectives, shards(): gain_sums = lax.psum(kept_gains + other_chip(sent_gains), 'dp')  30.8 us
  transfers between devices with their start and end apart: 56, of which 17 were waited for; matrix products, arithmetic and copies ran while one was open for 40% of the time, Pallas kernels for 0%

profile of v1, /device:TPU:1, one launch (start us, length us, event | category | flops | bytes accessed | tf_op | source)
XLA Modules:
  0.0 1432.2 jit_solution(10121360733983694589)
XLA Ops:
  26.0 25.3 %collective-permute-done.1 = bf16[1152,576]{0,1:T(8,128)(2,1)} collective-permute-done((bf16[1152,576]{0,1:T(8,128)(2,1)}, bf16[1152,576]{0,1:T(8,128)(2,1)}, u32[]{:S(2)}, u32[]{:S(2)}) %collective-permute-start.1) | collective-permute-done | bytes 1327136 | tf_op jit(solution)/shard_map/ppermute | solution.py:24
  66.2 54.4 %collective-permute-done.5 = f32[1,576]{1,0:T(1,128)S(1)} collective-permute-done((f32[1,576]{1,0:T(1,128)S(1)}, f32[1,576]{1,0:T(1,128)S(1)}, u32[]{:S(2)}, u32[]{:S(2)}) %collective-permute-start.5) | collective-permute-done | bytes 2336 | tf_op jit(solution)/shard_map/ppermute | solution.py:24
  158.7 24.2 %while.60 = (s32[]{:T(128)}, bf16[2,512,8,72]{1,3,2,0:T(8,128)(2,1)}, f32[2,8,512]{2,1,0:T(8,128)S(1)}, bf16[2,512,8,72]{1,3,2,0:T(8,128)(2,1)}, bf16[1,1024,8,7...) while((s32[]{:T(128)}, bf16[2,512,8,72]{1,3,2,0:T(8,128)(2,1)}, ...), condition=%wide.region_11.12_spmd.clone, body=%wide.region_8.11_spmd.sunk.clone | while | flops 1241509888 | bytes 64028816 | solution.py:135
  198.4 24.5 %all-gather = bf16[8,2,576]{2,1,0:T(2,128)(2,1)S(1)} all-gather(bf16[1,2,576]{2,1,0:T(2,128)(2,1)S(1)} %fusion.200), channel_id=1, replica_groups=mesh['dp'=8,'row'=2,'col'=2] {'dp'}, dimensions={0}, use_global_device_ids=true | all-gather | bytes 20736 | tf_op jit(solution)/shard_map/all_gather | solution.py:413
  229.7 11.7 collective-permute-done.13
  263.8 6.0 while.61
  270.7 43.4 %collective-permute-done.15 = bf16[576,576]{1,0:T(8,128)(2,1)} collective-permute-done((bf16[576,576]{1,0:T(8,128)(2,1)}, bf16[576,576]{1,0:T(8,128)(2,1)}, u32[]{:S(2)}, u32[]{:S(2)}) %collective-permute-start.15) | collective-permute-done | bytes 663584 | tf_op jit(solution)/shard_map/ppermute | solution.py:24
  327.5 5.8 copy.145
  333.3 6.5 copy.146
  343.3 40.3 %collective-permute-done.24 = bf16[512,576]{0,1:T(8,128)(2,1)} collective-permute-done((bf16[512,576]{0,1:T(8,128)(2,1)}, bf16[512,576]{0,1:T(8,128)(2,1)}, u32[]{:S(2)}, u32[]{:S(2)}) %collective-permute-start.24) | collective-permute-done | bytes 589856 | tf_op jit(solution)/shard_map/ppermute | solution.py:24
  391.7 5.9 fusion.235
  423.9 8.9 fusion.93
  432.9 10.4 fusion.112
  443.3 7.2 fusion.115
  451.0 5.8 fusion.137
  462.6 7.7 fusion.141
  472.5 9.5 fusion.100
  484.6 8.2 multiply_reduce_fusion.11
  500.0 74.8 %collective-permute-done.45 = bf16[2304,576]{0,1:T(8,128)(2,1)} collective-permute-done((bf16[2304,576]{0,1:T(8,128)(2,1)}, bf16[2304,576]{0,1:T(8,128)(2,1)}, u32[]{:S(2)}, u32[]{:S(2)}) %collective-permute-start.45) | collective-permute-done | bytes 2654240 | tf_op jit(solution)/shard_map/ppermute | solution.py:24
  579.1 8.4 collective-permute-done.21
  613.5 20.0 %while.62 = (s32[]{:T(128)}, f32[1,333,8,72]{1,3,2,0:T(8,128)S(1)}, f32[1,333,8,72]{1,3,2,0:T(8,128)}, f32[2,512,8,72]{1,3,2,0:T(8,128)}, bf16[2,512,8,72]{1,3,2...) while((s32[]{:T(128)}, f32[1,333,8,72]{1,3,2,0:T(8,128)S(1)}, ...), condition=%wide.region_28.29_spmd.clone, body=%wide.region_26.28_spmd.sunk.clone | while | flops 999290816 | bytes 79082248 | solution.py:192
  678.4 9.7 collective-permute-done.42
  690.3 26.9 %collective-permute-done.34 = bf16[333,512]{1,0:T(8,128)(2,1)S(1)} collective-permute-done((bf16[333,512]{1,0:T(8,128)(2,1)S(1)}, bf16[333,512]{1,0:T(8,128)(2,1)S(1)}, u32[]{:S(2)}, u32[]{:S(2)}) %collective-permute-start.34) | collective-permute-done | bytes 341024 | tf_op jit(solution)/shard_map/ppermute | solution.py:383
  729.0 133.6 %while.63 = (s32[]{:T(128)}, f32[1,1024,8,72]{1,3,2,0:T(8,128)}, f32[1,1024,8,72]{1,3,2,0:T(8,128)}, f32[2,512,8,72]{1,0,3,2:T(2,128)}, bf16[2,512,8,72]{1,3,2,0...) while((s32[]{:T(128)}, f32[1,1024,8,72]{1,3,2,0:T(8,128)}, ...), condition=%wide.region_35.36_spmd.clone, body=%wide.region_33.35_spmd.sunk.clone | while | flops 3072290816 | bytes 204325104 | solution.py:192
  739.1 9.9 multiply_reduce_fusion.43
  749.0 10.6 multiply_convert_fusion.15
  759.6 6.7 fusion.373
  772.0 24.2 %dynamic_update_slice.54 = f32[2,512,8,72]{1,0,3,2:T(2,128)} dynamic-update-slice(f32[2,512,8,72]{1,0,3,2:T(2,128)} %get-tuple-element.1016, f32[1,512,8,72]{1,0,3,2:T(1,128)} %copy.242, s32[]{:T(128)S(6)} %copy.286, s32[]{:T(128)} %constant.232.clone.1..sunk.1, s32[]{:T(128)} %constant.232.clone.1..sunk.1, s32[]{:T(128)} %constant.232.clone.1..sunk.1) | dynamic-update-slice | bytes 2359300 | tf_op jit(solution)/shard_map/while/body/jit(dynamic_update_index_in_dim)/dynamic_update_slice | solution.py:135
  800.1 5.7 fusion.372
  805.9 9.9 multiply_reduce_fusion.43
  815.7 10.6 multiply_convert_fusion.15
  826.3 6.5 fusion.373
  838.5 24.1 %dynamic_update_slice.54 = f32[2,512,8,72]{1,0,3,2:T(2,128)} dynamic-update-slice(f32[2,512,8,72]{1,0,3,2:T(2,128)} %get-tuple-element.1016, f32[1,512,8,72]{1,0,3,2:T(1,128)} %copy.242, s32[]{:T(128)S(6)} %copy.286, s32[]{:T(128)} %constant.232.clone.1..sunk.1, s32[]{:T(128)} %constant.232.clone.1..sunk.1, s32[]{:T(128)} %constant.232.clone.1..sunk.1) | dynamic-update-slice | bytes 2359300 | tf_op jit(solution)/shard_map/while/body/jit(dynamic_update_index_in_dim)/dynamic_update_slice | solution.py:135
  878.5 6.4 fusion.121
  895.9 6.3 fusion.208
  916.9 41.8 %collective-permute-done.40 = bf16[576,576]{1,0:T(8,128)(2,1)S(1)} collective-permute-done((bf16[576,576]{1,0:T(8,128)(2,1)}, bf16[576,576]{1,0:T(8,128)(2,1)S(1)}, u32[]{:S(2)}, u32[]{:S(2)}) %collective-permute-start.40) | collective-permute-done | bytes 663584 | tf_op jit(solution)/shard_map/ppermute | solution.py:24
  963.9 20.4 %all-reduce.25.cloned.1.call-done = bf16[576,576]{1,0:T(8,128)(2,1)} async-done(((bf16[576,576]{1,0:T(8,128)(2,1)}), bf16[576,576]{1,0:T(8,128)(2,1)}) %all-reduce.25.cloned.1.call-update) | async-done | bytes 663568 | tf_op jit(solution)/shard_map/psum | solution.py:476
  994.2 67.1 %all-reduce.27.cloned.1.call-done = bf16[576,576]{0,1:T(8,128)(2,1)} async-done(((bf16[576,576]{0,1:T(8,128)(2,1)}), bf16[576,576]{0,1:T(8,128)(2,1)}) %all-reduce.27.cloned.1.call-update) | async-done | bytes 663568 | tf_op jit(solution)/shard_map/psum | solution.py:476
  1064.2 7.1 multiply_reduce_fusion.13
  1086.0 24.2 %all-gather.1 = f32[8,2,576]{2,1,0:T(2,128)S(1)} all-gather(f32[1,2,576]{2,1,0:T(2,128)S(1)} %fusion.185), channel_id=1, replica_groups=mesh['dp'=8,'row'=2,'col'=2] {'dp'}, dimensions={0}, use_global_device_ids=true | all-gather | bytes 41472 | tf_op jit(solution)/shard_map/all_gather | solution.py:414
  1112.2 32.9 %all-reduce.29.cloned.1.call-done = bf16[512,1152]{1,0:T(8,128)(2,1)} async-done(((bf16[512,1152]{1,0:T(8,128)(2,1)}), bf16[512,1152]{1,0:T(8,128)(2,1)}) %all-reduce.29.cloned.1.call-update) | async-done | bytes 1179664 | tf_op jit(solution)/shard_map/psum | solution.py:476
  1145.6 6.7 fusion.110
  1165.4 56.3 %all-reduce.31.cloned.1.call-done = bf16[576,576]{1,0:T(8,128)(2,1)} async-done(((bf16[576,576]{1,0:T(8,128)(2,1)}), bf16[576,576]{1,0:T(8,128)(2,1)}) %all-reduce.31.cloned.1.call-update) | async-done | bytes 663568 | tf_op jit(solution)/shard_map/psum | solution.py:476
  1235.7 6.1 copy.139
  1241.7 5.9 copy.140
  1251.1 78.8 %all-reduce.33.cloned.1.call-done = bf16[576,1728]{0,1:T(8,128)(2,1)} async-done(((bf16[576,1728]{0,1:T(8,128)(2,1)}), bf16[576,1728]{0,1:T(8,128)(2,1)}) %all-reduce.33.cloned.1.call-update) | async-done | bytes 1990672 | tf_op jit(solution)/shard_map/psum | solution.py:476
  1340.3 30.8 %psum.63 = f32[3168]{0:T(1024)S(1)} all-reduce(f32[3168]{0:T(1024)S(1)} %add.411), channel_id=1, replica_groups=mesh['dp'=8,'row'=2,'col'=2] {'dp'}, use_global_device_ids=true, to_apply=%region_54.55 | all-reduce | flops 3168 | bytes 25344 | tf_op jit(solution)/shard_map/psum | solution.py:451
  1377.2 44.7 %all-reduce.35.cloned.1.call-done = bf16[2,576,576]{2,1,0:T(8,128)(2,1)} async-done(((bf16[2,576,576]{2,1,0:T(8,128)(2,1)}), bf16[2,576,576]{2,1,0:T(8,128)(2,1)}) %all-reduce.35.cloned.1.call-update) | async-done | bytes 1327120 | tf_op jit(solution)/shard_map/psum | solution.py:476
  (805 shorter events, 474.7 us)
Async XLA Ops:
  7.2 710.7 %all-reduce.21.cloned.1.call-start = ((), (), s32[]{:S(2)}) async-start(), calls=%async_computation | async-start | bytes 5308416 | tf_op jit(solution)/shard_map/psum | solution.py:476
  18.8 32.5 %collective-permute-start.1 = (bf16[1152,576]{0,1:T(8,128)(2,1)}, bf16[1152,576]{0,1:T(8,128)(2,1)}, u32[]{:S(2)}, u32[]{:S(2)}) collective-permute-start(bf16[1152,576]{0,1:T(8,128)(2,1)} %copy.160), channel_id=1, source_target_pairs={{0,2},{2,0},{1,3},{3,1},{4,6},{6,4},{5,7},{7,5},{8,10},{10,8},{9,1... | collective-permute-start | bytes 3981320 | tf_op jit(solution)/shard_map/ppermute | solution.py:24
  56.3 66.6 %collective-permute-start.2 = (f32[512,1152]{1,0:T(8,128)}, f32[512,1152]{1,0:T(8,128)}, u32[]{:S(2)}, u32[]{:S(2)}) collective-permute-start(f32[512,1152]{1,0:T(8,128)} %fusion.205), channel_id=1, source_target_pairs={{0,1},{1,0},{2,3},{3,2},{4,5},{5,4},{6,7},{7,6},{8,9},{9,8},{10,11... | collective-permute-start | bytes 7077896 | tf_op jit(solution)/shard_map/ppermute | solution.py:20
  57.2 63.5 %collective-permute-start.3 = (f32[3,576]{1,0:T(4,128)S(1)}, f32[3,576]{1,0:T(4,128)S(1)}, u32[]{:S(2)}, u32[]{:S(2)}) collective-permute-start(f32[3,576]{1,0:T(4,128)S(1)} %pad_maximum_fusion.24), channel_id=1, source_target_pairs={{0,2},{2,0},{1,3},{3,1},{4,6},{6,4},{5,7},{7,5},{8,10},{10,8},{9,1... | collective-permute-start | bytes 20744 | tf_op jit(solution)/shard_map/ppermute | solution.py:24
  58.8 126.9 %collective-permute-start.8 = (bf16[576,576]{1,0:T(8,128)(2,1)}, bf16[576,576]{1,0:T(8,128)(2,1)}, u32[]{:S(2)}, u32[]{:S(2)}) collective-permute-start(bf16[576,576]{1,0:T(8,128)(2,1)} %param.44), channel_id=1, source_target_pairs={{0,2},{2,0},{1,3},{3,1},{4,6},{6,4},{5,7},{7,5},{8,10},{10,8},{9,1... | collective-permute-start | bytes 1990664 | tf_op jit(solution)/shard_map/ppermute | solution.py:24
  64.6 69.4 %collective-permute-start.6 = (bf16[576,1728]{1,0:T(8,128)(2,1)}, bf16[576,1728]{1,0:T(8,128)(2,1)}, u32[]{:S(2)}, u32[]{:S(2)}) collective-permute-start(bf16[576,1728]{1,0:T(8,128)(2,1)} %copy.114), channel_id=1, source_target_pairs={{0,2},{2,0},{1,3},{3,1},{4,6},{6,4},{5,7},{7,5},{8,10},{10,8},{9,1... | collective-permute-start | bytes 5971976 | tf_op jit(solution)/shard_map/ppermute | solution.py:24
  66.0 54.6 %collective-permute-start.5 = (f32[1,576]{1,0:T(1,128)S(1)}, f32[1,576]{1,0:T(1,128)S(1)}, u32[]{:S(2)}, u32[]{:S(2)}) collective-permute-start(f32[1,576]{1,0:T(1,128)S(1)} %get-tuple-element.629), channel_id=1, source_target_pairs={{0,2},{2,0},{1,3},{3,1},{4,6},{6,4},{5,7},{7,5},{8,10},{10,8},{9,1... | collective-permute-start | bytes 6920 | tf_op jit(solution)/shard_map/ppermute | solution.py:24
  130.4 12.6 collective-permute-start.7
  189.9 55.1 %collective-permute-start.9 = (f32[512,1152]{1,0:T(8,128)}, f32[512,1152]{1,0:T(8,128)}, u32[]{:S(2)}, u32[]{:S(2)}) collective-permute-start(f32[512,1152]{1,0:T(8,128)} %fusion.207), channel_id=1, source_target_pairs={{0,1},{1,0},{2,3},{3,2},{4,5},{5,4},{6,7},{7,6},{8,9},{9,8},{10,11... | collective-permute-start | bytes 7077896 | tf_op jit(solution)/shard_map/ppermute | solution.py:20
  190.4 38.8 %collective-permute-start.10 = (bf16[576,576]{1,0:T(8,128)(2,1)}, bf16[576,576]{1,0:T(8,128)(2,1)S(1)}, u32[]{:S(2)}, u32[]{:S(2)}) collective-permute-start(bf16[576,576]{1,0:T(8,128)(2,1)} %param.46), channel_id=1, source_target_pairs={{0,2},{2,0},{1,3},{3,1},{4,6},{6,4},{5,7},{7,5},{8,10},{10,8},{9,1... | collective-permute-start | bytes 1990664 | tf_op jit(solution)/shard_map/ppermute | solution.py:24
  190.6 51.0 %collective-permute-start.14 = (bf16[512,1152]{0,1:T(8,128)(2,1)}, bf16[512,1152]{0,1:T(8,128)(2,1)}, u32[]{:S(2)}, u32[]{:S(2)}) collective-permute-start(bf16[512,1152]{0,1:T(8,128)(2,1)} %bitcast.63), channel_id=1, source_target_pairs={{0,2},{2,0},{1,3},{3,1},{4,6},{6,4},{5,7},{7,5},{8,10},{10,8},{9,1... | collective-permute-start | bytes 3538952 | tf_op jit(solution)/shard_map/ppermute | solution.py:24
  192.8 33.0 %collective-permute-start.23 = (bf16[512,576]{0,1:T(8,128)(2,1)}, bf16[512,576]{0,1:T(8,128)(2,1)}, u32[]{:S(2)}, u32[]{:S(2)}) collective-permute-start(bf16[512,576]{0,1:T(8,128)(2,1)} %get-tuple-element.581), channel_id=1, source_target_pairs={{0,1},{1,0},{2,3},{3,2},{4,5},{5,4},{6,7},{7,6},{8,9},{9,8},{10,11... | collective-permute-start | bytes 1769480 | tf_op jit(solution)/shard_map/ppermute | solution.py:20
  196.9 44.5 %collective-permute-start.13 = (bf16[333,512]{1,0:T(8,128)(2,1)}, bf16[333,512]{1,0:T(8,128)(2,1)}, u32[]{:S(2)}, u32[]{:S(2)}) collective-permute-start(bf16[333,512]{1,0:T(8,128)(2,1)} %get-tuple-element.591), channel_id=1, source_target_pairs={{0,2},{2,0},{1,3},{3,1},{4,6},{6,4},{5,7},{7,5},{8,10},{10,8},{9,1... | collective-permute-start | bytes 1022984 | tf_op jit(solution)/shard_map/ppermute | solution.py:24
  225.9 180.0 %collective-permute-start.17 = (bf16[576,2304]{1,0:T(8,128)(2,1)}, bf16[576,2304]{1,0:T(8,128)(2,1)}, u32[]{:S(2)}, u32[]{:S(2)}) collective-permute-start(bf16[576,2304]{1,0:T(8,128)(2,1)} %param.52), channel_id=1, source_target_pairs={{0,2},{2,0},{1,3},{3,1},{4,6},{6,4},{5,7},{7,5},{8,10},{10,8},{9,1... | collective-permute-start | bytes 7962632 | tf_op jit(solution)/shard_map/ppermute | solution.py:24
  229.2 84.9 %collective-permute-start.15 = (bf16[576,576]{1,0:T(8,128)(2,1)}, bf16[576,576]{1,0:T(8,128)(2,1)}, u32[]{:S(2)}, u32[]{:S(2)}) collective-permute-start(bf16[576,576]{1,0:T(8,128)(2,1)} %param.50), channel_id=1, source_target_pairs={{0,2},{2,0},{1,3},{3,1},{4,6},{6,4},{5,7},{7,5},{8,10},{10,8},{9,1... | collective-permute-start | bytes 1990664 | tf_op jit(solution)/shard_map/ppermute | solution.py:24
  241.4 146.9 %collective-permute-start.19 = (bf16[2304,576]{0,1:T(8,128)(2,1)}, bf16[2304,576]{0,1:T(8,128)(2,1)}, u32[]{:S(2)}, u32[]{:S(2)}) collective-permute-start(bf16[2304,576]{0,1:T(8,128)(2,1)} %param.53), channel_id=1, source_target_pairs={{0,2},{2,0},{1,3},{3,1},{4,6},{6,4},{5,7},{7,5},{8,10},{10,8},{9,1... | collective-permute-start | bytes 7962632 | tf_op jit(solution)/shard_map/ppermute | solution.py:24
  318.2 79.5 %collective-permute-start.16 = (f32[512,1152]{1,0:T(8,128)}, f32[512,1152]{1,0:T(8,128)}, u32[]{:S(2)}, u32[]{:S(2)}) collective-permute-start(f32[512,1152]{1,0:T(8,128)} %fusion.206), channel_id=1, source_target_pairs={{0,1},{1,0},{2,3},{3,2},{4,5},{5,4},{6,7},{7,6},{8,9},{9,8},{10,11... | collective-permute-start | bytes 7077896 | tf_op jit(solution)/shard_map/ppermute | solution.py:20
  322.8 60.8 %collective-permute-start.24 = (bf16[512,576]{0,1:T(8,128)(2,1)}, bf16[512,576]{0,1:T(8,128)(2,1)}, u32[]{:S(2)}, u32[]{:S(2)}) collective-permute-start(bf16[512,576]{0,1:T(8,128)(2,1)} %copy.132), channel_id=1, source_target_pairs={{0,2},{2,0},{1,3},{3,1},{4,6},{6,4},{5,7},{7,5},{8,10},{10,8},{9,1... | collective-permute-start | bytes 1769480 | tf_op jit(solution)/shard_map/ppermute | solution.py:24
  387.4 15.2 %collective-permute-start.25 = (bf16[512,1152]{1,0:T(8,128)(2,1)S(1)}, bf16[512,1152]{1,0:T(8,128)(2,1)S(1)}, u32[]{:S(2)}, u32[]{:S(2)}) collective-permute-start(bf16[512,1152]{1,0:T(8,128)(2,1)S(1)} %pad_maximum_fusion.16), channel_id=1, source_target_pairs={{0,1},{1,0},{2,3},{3,2},{4,5},{5,4},{6,7},{7,6},{8,9},{9,8},{10,11... | collective-permute-start | bytes 3538952 | tf_op jit(solution)/shard_map/ppermute | solution.py:20
  402.1 16.0 %collective-permute-start.18 = (bf16[512,1152]{1,0:T(8,128)(2,1)S(1)}, bf16[512,1152]{1,0:T(8,128)(2,1)S(1)}, u32[]{:S(2)}, u32[]{:S(2)}) collective-permute-start(bf16[512,1152]{1,0:T(8,128)(2,1)S(1)} %multiply_convert_fusion.7), channel_id=1, source_target_pairs={{0,1},{1,0},{2,3},{3,2},{4,5},{5,4},{6,7},{7,6},{8,9},{9,8},{10,11... | collective-permute-start | bytes 3538952 | tf_op jit(solution)/shard_map/ppermute | solution.py:20
  450.5 22.0 %collective-permute-start.20 = (f32[512,1152]{1,0:T(8,128)}, f32[512,1152]{1,0:T(8,128)}, u32[]{:S(2)}, u32[]{:S(2)}) collective-permute-start(f32[512,1152]{1,0:T(8,128)} %fusion.115), channel_id=1, source_target_pairs={{0,1},{1,0},{2,3},{3,2},{4,5},{5,4},{6,7},{7,6},{8,9},{9,8},{10,11... | collective-permute-start | bytes 7077896 | tf_op jit(solution)/shard_map/ppermute | solution.py:20
  450.7 34.0 %collective-permute-start.26 = (f32[512,1152]{1,0:T(8,128)}, f32[512,1152]{1,0:T(8,128)}, u32[]{:S(2)}, u32[]{:S(2)}) collective-permute-start(f32[512,1152]{1,0:T(8,128)} %fusion.112), channel_id=1, source_target_pairs={{0,1},{1,0},{2,3},{3,2},{4,5},{5,4},{6,7},{7,6},{8,9},{9,8},{10,11... | collective-permute-start | bytes 7077896 | tf_op jit(solution)/shard_map/ppermute | solution.py:20
  458.6 134.8 %collective-permute-start.44 = (bf16[576,2304]{1,0:T(8,128)(2,1)}, bf16[576,2304]{1,0:T(8,128)(2,1)}, u32[]{:S(2)}, u32[]{:S(2)}) collective-permute-start(bf16[576,2304]{1,0:T(8,128)(2,1)} %slice.578), channel_id=1, source_target_pairs={{0,2},{2,0},{1,3},{3,1},{4,6},{6,4},{5,7},{7,5},{8,10},{10,8},{9,1... | collective-permute-start | bytes 7962632 | tf_op jit(solution)/shard_map/ppermute | solution.py:24
  472.3 102.5 %collective-permute-start.45 = (bf16[2304,576]{0,1:T(8,128)(2,1)}, bf16[2304,576]{0,1:T(8,128)(2,1)}, u32[]{:S(2)}, u32[]{:S(2)}) collective-permute-start(bf16[2304,576]{0,1:T(8,128)(2,1)} %slice.577), channel_id=1, source_target_pairs={{0,2},{2,0},{1,3},{3,1},{4,6},{6,4},{5,7},{7,5},{8,10},{10,8},{9,1... | collective-permute-start | bytes 7962632 | tf_op jit(solution)/shard_map/ppermute | solution.py:24
  484.5 103.0 %collective-permute-start.21 = (bf16[512,576]{0,1:T(8,128)(2,1)}, bf16[512,576]{0,1:T(8,128)(2,1)}, u32[]{:S(2)}, u32[]{:S(2)}) collective-permute-start(bf16[512,576]{0,1:T(8,128)(2,1)} %copy.123), channel_id=1, source_target_pairs={{0,2},{2,0},{1,3},{3,1},{4,6},{6,4},{5,7},{7,5},{8,10},{10,8},{9,1... | collective-permute-start | bytes 1769480 | tf_op jit(solution)/shard_map/ppermute | solution.py:24
  496.1 109.3 %collective-permute-start.27 = (bf16[512,1152]{1,0:T(8,128)(2,1)}, bf16[512,1152]{1,0:T(8,128)(2,1)}, u32[]{:S(2)}, u32[]{:S(2)}) collective-permute-start(bf16[512,1152]{1,0:T(8,128)(2,1)} %get-tuple-element.520), channel_id=1, source_target_pairs={{0,1},{1,0},{2,3},{3,2},{4,5},{5,4},{6,7},{7,6},{8,9},{9,8},{10,11... | collective-permute-start | bytes 3538952 | tf_op jit(solution)/shard_map/ppermute | solution.py:20
  578.6 332.0 %all-reduce.23.cloned.1.call-start = ((), (), s32[]{:S(2)}) async-start(), calls=%async_computation.1 | async-start | bytes 5308416 | tf_op jit(solution)/shard_map/psum | solution.py:476
  644.5 23.8 %collective-permute-start.28 = (f32[512,1152]{1,0:T(8,128)S(1)}, f32[512,1152]{1,0:T(8,128)S(1)}, u32[]{:S(2)}, u32[]{:S(2)}) collective-permute-start(f32[512,1152]{1,0:T(8,128)S(1)} %fusion.237), channel_id=1, source_target_pairs={{0,1},{1,0},{2,3},{3,2},{4,5},{5,4},{6,7},{7,6},{8,9},{9,8},{10,11... | collective-permute-start | bytes 7077896 | tf_op jit(solution)/shard_map/ppermute | solution.py:20
  649.9 24.6 %collective-permute-start.33 = (f32[333,512]{1,0:T(8,128)S(1)}, f32[333,512]{1,0:T(8,128)S(1)}, u32[]{:S(2)}, u32[]{:S(2)}) collective-permute-start(f32[333,512]{1,0:T(8,128)S(1)} %slice_select_fusion), channel_id=1, source_target_pairs={{0,1},{1,0},{2,3},{3,2},{4,5},{5,4},{6,7},{7,6},{8,9},{9,8},{10,11... | collective-permute-start | bytes 2045960 | tf_op jit(solution)/shard_map/ppermute | solution.py:20
  654.1 23.3 %collective-permute-start.43 = (bf16[576,576]{1,0:T(8,128)(2,1)S(1)}, bf16[576,576]{1,0:T(8,128)(2,1)S(1)}, u32[]{:S(2)}, u32[]{:S(2)}) collective-permute-start(bf16[576,576]{1,0:T(8,128)(2,1)S(1)} %slice.582), channel_id=1, source_target_pairs={{0,2},{2,0},{1,3},{3,1},{4,6},{6,4},{5,7},{7,5},{8,10},{10,8},{9,1... | collective-permute-start | bytes 1990664 | tf_op jit(solution)/shard_map/ppermute | solution.py:24
  660.9 27.3 %collective-permute-start.42 = (bf16[576,576]{0,1:T(8,128)(2,1)}, bf16[576,576]{0,1:T(8,128)(2,1)}, u32[]{:S(2)}, u32[]{:S(2)}) collective-permute-start(bf16[576,576]{0,1:T(8,128)(2,1)} %slice.583), channel_id=1, source_target_pairs={{0,2},{2,0},{1,3},{3,1},{4,6},{6,4},{5,7},{7,5},{8,10},{10,8},{9,1... | collective-permute-start | bytes 1990664 | tf_op jit(solution)/shard_map/ppermute | solution.py:24
  667.9 242.8 %collective-permute-start.41 = (bf16[512,1152]{1,0:T(8,128)(2,1)}, bf16[512,1152]{1,0:T(8,128)(2,1)}, u32[]{:S(2)}, u32[]{:S(2)}) collective-permute-start(bf16[512,1152]{1,0:T(8,128)(2,1)} %slice.581), channel_id=1, source_target_pairs={{0,2},{2,0},{1,3},{3,1},{4,6},{6,4},{5,7},{7,5},{8,10},{10,8},{9,1... | collective-permute-start | bytes 3538952 | tf_op jit(solution)/shard_map/ppermute | solution.py:24
  673.9 46.8 %collective-permute-start.29 = (bf16[512,1152]{1,0:T(8,128)(2,1)}, bf16[512,1152]{1,0:T(8,128)(2,1)}, u32[]{:S(2)}, u32[]{:S(2)}) collective-permute-start(bf16[512,1152]{1,0:T(8,128)(2,1)} %get-tuple-element.518), channel_id=1, source_target_pairs={{0,1},{1,0},{2,3},{3,2},{4,5},{5,4},{6,7},{7,6},{8,9},{9,8},{10,11... | collective-permute-start | bytes 3538952 | tf_op jit(solution)/shard_map/ppermute | solution.py:20
  674.8 42.4 %collective-permute-start.34 = (bf16[333,512]{1,0:T(8,128)(2,1)S(1)}, bf16[333,512]{1,0:T(8,128)(2,1)S(1)}, u32[]{:S(2)}, u32[]{:S(2)}) collective-permute-start(bf16[333,512]{1,0:T(8,128)(2,1)S(1)} %add_convert_fusion.6), channel_id=1, source_target_pairs={{1,2},{2,1},{5,6},{6,5},{9,10},{10,9},{13,14},{14,13},{17,18},{18,... | collective-permute-start | bytes 1022984 | tf_op jit(solution)/shard_map/ppermute | solution.py:383
  718.0 266.3 %all-reduce.25.cloned.1.call-start = ((), (), s32[]{:S(2)}) async-start(), calls=%async_computation.2 | async-start | bytes 1474560 | tf_op jit(solution)/shard_map/psum | solution.py:476
  895.8 90.9 %collective-permute-start.39 = (bf16[576,1728]{1,0:T(8,128)(2,1)}, bf16[576,1728]{1,0:T(8,128)(2,1)}, u32[]{:S(2)}, u32[]{:S(2)}) collective-permute-start(bf16[576,1728]{1,0:T(8,128)(2,1)} %copy.147), channel_id=1, source_target_pairs={{0,2},{2,0},{1,3},{3,1},{4,6},{6,4},{5,7},{7,5},{8,10},{10,8},{9,1... | collective-permute-start | bytes 5971976 | tf_op jit(solution)/shard_map/ppermute | solution.py:24
  902.2 161.9 %collective-permute-start.30 = (f32[512,1152]{1,0:T(8,128)}, f32[512,1152]{1,0:T(8,128)}, u32[]{:S(2)}, u32[]{:S(2)}) collective-permute-start(f32[512,1152]{1,0:T(8,128)} %fusion.208), channel_id=1, source_target_pairs={{0,1},{1,0},{2,3},{3,2},{4,5},{5,4},{6,7},{7,6},{8,9},{9,8},{10,11... | collective-permute-start | bytes 7077896 | tf_op jit(solution)/shard_map/ppermute | solution.py:20
  909.6 49.1 %collective-permute-start.40 = (bf16[576,576]{1,0:T(8,128)(2,1)}, bf16[576,576]{1,0:T(8,128)(2,1)S(1)}, u32[]{:S(2)}, u32[]{:S(2)}) collective-permute-start(bf16[576,576]{1,0:T(8,128)(2,1)} %slice.584), channel_id=1, source_target_pairs={{0,2},{2,0},{1,3},{3,1},{4,6},{6,4},{5,7},{7,5},{8,10},{10,8},{9,1... | collective-permute-start | bytes 1990664 | tf_op jit(solution)/shard_map/ppermute | solution.py:24
  910.6 150.7 %all-reduce.27.cloned.1.call-start = ((), (), s32[]{:S(2)}) async-start(), calls=%async_computation.3 | async-start | bytes 1474560 | tf_op jit(solution)/shard_map/psum | solution.py:476
  984.3 160.8 %all-reduce.29.cloned.1.call-start = ((), (), s32[]{:S(2)}) async-start(), calls=%async_computation.4 | async-start | bytes 2359296 | tf_op jit(solution)/shard_map/psum | solution.py:476
  1061.3 160.4 %all-reduce.31.cloned.1.call-start = ((), (), s32[]{:S(2)}) async-start(), calls=%async_computation.5 | async-start | bytes 1474560 | tf_op jit(solution)/shard_map/psum | solution.py:476
  1073.3 38.9 %collective-permute-start.35 = (f32[3,1152]{1,0:T(4,128)S(1)}, f32[3,1152]{1,0:T(4,128)S(1)}, u32[]{:S(2)}, u32[]{:S(2)}) collective-permute-start(f32[3,1152]{1,0:T(4,128)S(1)} %pad_maximum_fusion.23), channel_id=1, source_target_pairs={{0,1},{1,0},{2,3},{3,2},{4,5},{5,4},{6,7},{7,6},{8,9},{9,8},{10,11... | collective-permute-start | bytes 41480 | tf_op jit(solution)/shard_map/ppermute | solution.py:20
  1075.2 70.4 %collective-permute-start.31 = (bf16[512,1152]{1,0:T(8,128)(2,1)}, bf16[512,1152]{1,0:T(8,128)(2,1)}, u32[]{:S(2)}, u32[]{:S(2)}) collective-permute-start(bf16[512,1152]{1,0:T(8,128)(2,1)} %add_convert_fusion), channel_id=1, source_target_pairs={{0,1},{1,0},{2,3},{3,2},{4,5},{5,4},{6,7},{7,6},{8,9},{9,8},{10,11... | collective-permute-start | bytes 3538952 | tf_op jit(solution)/shard_map/ppermute | solution.py:20
  1145.1 184.8 %all-reduce.33.cloned.1.call-start = ((), (), s32[]{:S(2)}) async-start(), calls=%async_computation.6 | async-start | bytes 4423680 | tf_op jit(solution)/shard_map/psum | solution.py:476
  1155.2 92.5 %collective-permute-start.38 = (bf16[1152,576]{0,1:T(8,128)(2,1)}, bf16[1152,576]{0,1:T(8,128)(2,1)}, u32[]{:S(2)}, u32[]{:S(2)}) collective-permute-start(bf16[1152,576]{0,1:T(8,128)(2,1)} %slice.580), channel_id=1, source_target_pairs={{0,2},{2,0},{1,3},{3,1},{4,6},{6,4},{5,7},{7,5},{8,10},{10,8},{9,1... | collective-permute-start | bytes 3981320 | tf_op jit(solution)/shard_map/ppermute | solution.py:24
  1221.8 200.2 %all-reduce.35.cloned.1.call-start = ((), (), s32[]{:S(2)}) async-start(), calls=%async_computation.7 | async-start | bytes 2949120 | tf_op jit(solution)/shard_map/psum | solution.py:476
  1229.3 18.3 %collective-permute-start.32 = (f32[2,1024]{1,0:T(2,128)S(1)}, f32[2,1024]{1,0:T(2,128)S(1)}, u32[]{:S(2)}, u32[]{:S(2)}) collective-permute-start(f32[2,1024]{1,0:T(2,128)S(1)} %pad_maximum_fusion.26), channel_id=1, source_target_pairs={{0,1},{1,0},{2,3},{3,2},{4,5},{5,4},{6,7},{7,6},{8,9},{9,8},{10,11... | collective-permute-start | bytes 24584 | tf_op jit(solution)/shard_map/ppermute | solution.py:20
  1234.4 105.9 %collective-permute-start.37 = (f32[3168]{0:T(1024)S(1)}, f32[3168]{0:T(1024)S(1)}, u32[]{:S(2)}, u32[]{:S(2)}) collective-permute-start(f32[3168]{0:T(1024)S(1)} %concatenate.209), channel_id=1, source_target_pairs={{0,2},{2,0},{1,3},{3,1},{4,6},{6,4},{5,7},{7,5},{8,10},{10,8},{9,1... | collective-permute-start | bytes 38024 | tf_op jit(solution)/shard_map/ppermute | solution.py:24
  (210 other events, 2379.4 us)
Sparse Core Ops, SparseCore 0:
  578.8 116.2 all-reduce.20
  718.1 115.5 all-reduce.22
  910.7 73.4 all-reduce.24
  988.0 73.2 all-reduce.26
  1065.2 79.7 all-reduce.28
  1148.8 72.9 all-reduce.30
  1225.4 104.4 all-reduce.32
  1334.6 87.3 all-reduce.34

commit v2 on v1

v2 whole, which is shorter than its diff:
```python
import functools

import jax
import jax.numpy as jnp
from jax import lax
from jax.experimental import pallas as pl
from jax.experimental.pallas import tpu as pltpu
from jax.sharding import PartitionSpec as P

D = 1152
HD = 72
TXT = 333
LAT = 1024


EPSILON = 1e-06
PRECISE = lax.Precision.HIGHEST
SWAP = [(0, 1), (1, 0)]
BF16 = jnp.bfloat16
F32 = jnp.float32
MESH = pl.DeviceIdType.MESH
LOG2E = 1.4426950408889634
FREE = pl.CostEstimate(flops=0, bytes_accessed=0, transcendentals=0)


def other_core(values):
    return lax.ppermute(values, "col", SWAP)


def other_chip(values):
    return lax.ppermute(values, "row", SWAP)


def contract(left_side, right_side):
    return jnp.dot(left_side, right_side, preferred_element_type=F32)


def pair(own):
    return jnp.concatenate([own, other_core(own)])


def after(values, earlier):
    return lax.optimization_barrier((values, earlier))[0]


def dot_nn(a, b):
    return lax.dot_general(a, b, (((1,), (0,)), ((), ())), preferred_element_type=F32)


def dot_tn(a, b):
    return lax.dot_general(a, b, (((0,), (0,)), ((), ())), preferred_element_type=F32)


def dot_nt(a, b):
    return lax.dot_general(a, b, (((1,), (1,)), ((), ())), preferred_element_type=F32)


def lane_norm(values):
    average = jnp.mean(values, axis=0, keepdims=True)
    variance = jnp.mean(values * values, axis=0, keepdims=True) - average * average
    inverse = lax.rsqrt(variance + EPSILON)
    return (values - average) * inverse, inverse


def lane_norm_back(grad, normed, inverse, gain):
    scaled = grad * gain
    first = jnp.mean(scaled, axis=0, keepdims=True)
    second = jnp.mean(scaled * normed, axis=0, keepdims=True)
    return inverse * (scaled - first - normed * second)


def turn(values, cosine, sine):
    quarter = HD // 4
    place = lax.broadcasted_iota(jnp.int32, values.shape, 0)
    leading = (place < quarter) | ((place >= 2 * quarter) & (place < 3 * quarter))
    partner = jnp.where(
        leading,
        pltpu.roll(values, HD - quarter, 0),
        pltpu.roll(values, quarter, 0),
    )
    return values * cosine + partner * sine


def attend_kernel(turned, valid, q_ref, k_ref, v_ref, qg_ref, kg_ref, *rest):
    if turned:
        cos_ref, sin_ref, out_ref, lse_ref = rest
    else:
        out_ref, lse_ref = rest
    query = lane_norm(q_ref[0])[0] * qg_ref[...]
    key = lane_norm(k_ref[0])[0] * kg_ref[...]
    if turned:
        query = turn(query, cos_ref[...], sin_ref[...])
        key = turn(key, cos_ref[...], sin_ref[...])
    query = query.astype(BF16)
    key_rows = key.astype(BF16).T
    value = v_ref[0].astype(BF16)
    keys = value.shape[1]
    ones = jnp.ones((8, keys), BF16)
    if valid < keys:
        ones = jnp.where(lax.broadcasted_iota(jnp.int32, (8, keys), 1) < valid, 1.0, 0.0).astype(BF16)
    tokens = query.shape[1]
    block = 256
    for start in range(0, tokens, block):
        scores = dot_nn(key_rows, query[:, start : start + block])
        weights = jnp.exp2(scores * (LOG2E * HD**-0.5)).astype(BF16)
        total = dot_nn(ones, weights)[:1]
        out = dot_nn(value, weights)
        out_ref[0, :, start : start + block] = (out * (1.0 / total)).astype(BF16)
        lse_ref[0, :, start : start + block] = jnp.log2(total)


def attend_back_kernel(turned, valid, q_ref, k_ref, v_ref, qg_ref, kg_ref, *rest):
    if turned:
        cos_ref, sin_ref, out_ref, lse_ref, grad_ref, grads_ref, gain_ref, dk_acc, dv_acc, dq_acc = rest
    else:
        out_ref, lse_ref, grad_ref, dq_ref, grads_ref, gain_ref, dk_acc, dv_acc, dq_acc = rest
    q_hat, q_inverse = lane_norm(q_ref[0])
    k_hat, k_inverse = lane_norm(k_ref[0])
    query = q_hat * qg_ref[...]
    key = k_hat * kg_ref[...]
    if turned:
        query = turn(query, cos_ref[...], sin_ref[...])
        key = turn(key, cos_ref[...], sin_ref[...])
    query = query.astype(BF16)
    key = key.astype(BF16)
    key_rows = key.T
    value_rows = v_ref[0].astype(BF16).T
    grad = grad_ref[0]
    inner = jnp.sum(grad.astype(F32) * out_ref[0].astype(F32), axis=0, keepdims=True)
    tokens = query.shape[1]
    block = 256
    for start in range(0, tokens, block):
        at = slice(start, start + block)
        scores = dot_nn(key_rows, query[:, at])
        weights = jnp.exp2(scores * (LOG2E * HD**-0.5) - lse_ref[0, :, at])
        grad_weights = dot_nn(value_rows, grad[:, at])
        grad_scores = (weights * (grad_weights - inner[:, at])).astype(BF16)
        weights = weights.astype(BF16)
        dq_acc[:, at] = dot_nn(key, grad_scores)
        grad_value = dot_nt(grad[:, at], weights)
        grad_key = dot_nt(query[:, at], grad_scores)
        if start == 0:
            dk_acc[...] = grad_key
            dv_acc[...] = grad_value
        else:
            dk_acc[...] += grad_key
            dv_acc[...] += grad_value
    grad_query = dq_acc[...] * HD**-0.5
    grad_key = dk_acc[...] * HD**-0.5
    grad_value = dv_acc[...]
    if turned:
        grad_query = turn(grad_query, cos_ref[...], -sin_ref[...])
        grad_key = turn(grad_key, cos_ref[...], -sin_ref[...])
    keys = grad_key.shape[1]
    if valid < keys:
        real = lax.broadcasted_iota(jnp.int32, grad_key.shape, 1) < valid
        grad_key = jnp.where(real, grad_key, 0.0)
        grad_value = jnp.where(real, grad_value, 0.0)
    gain_ref[0, 0] = jnp.sum(grad_query * q_hat, axis=1, keepdims=True)
    gain_ref[0, 1] = jnp.sum(grad_key * k_hat, axis=1, keepdims=True)
    grad_query = lane_norm_back(grad_query, q_hat, q_inverse, qg_ref[...]).astype(BF16)
    grad_key = lane_norm_back(grad_key, k_hat, k_inverse, kg_ref[...]).astype(BF16)
    grads = [grad_key, grad_value.astype(BF16)]
    if turned:
        grads = [grad_query] + grads
    else:
        dq_ref[0] = grad_query
    for index, value in enumerate(grads):
        grads_ref[index, 0] = value


def head_block(array, first):
    return pl.BlockSpec((1,) + array.shape[1:], lambda h: (first + h, 0, 0))


def fixed(array):
    return pl.BlockSpec(array.shape, lambda h: (0,) * array.ndim)


def attend(q, k, v, starts, heads, qg, kg, angles, valid):
    tokens, keys = q.shape[2], k.shape[2]
    extra = list(angles)
    return pl.pallas_call(
        functools.partial(attend_kernel, bool(extra), valid),
        grid=(heads,),
        in_specs=[head_block(q, starts[0]), head_block(k, starts[1]), head_block(v, starts[2])]
        + [fixed(a) for a in [qg, kg] + extra],
        out_specs=[
            pl.BlockSpec((1, HD, tokens), lambda h: (h, 0, 0)),
            pl.BlockSpec((1, 1, tokens), lambda h: (h, 0, 0)),
        ],
        out_shape=[
            jax.ShapeDtypeStruct((heads, HD, tokens), BF16),
            jax.ShapeDtypeStruct((heads, 1, tokens), F32),
        ],
        compiler_params=pltpu.CompilerParams(vmem_limit_bytes=48 * 2**20),
        cost_estimate=FREE,
        name="attend",
    )(q, k, v, qg, kg, *extra)


def attend_back(q, k, v, starts, heads, qg, kg, angles, valid, out, lse, grad):
    tokens, keys = q.shape[2], k.shape[2]
    extra = list(angles)
    parts = 3 if extra else 2
    out_specs = [
        pl.BlockSpec((parts, 1, HD, keys), lambda h: (0, h, 0, 0)),
        pl.BlockSpec((1, 2, HD, 1), lambda h: (h, 0, 0, 0)),
    ]
    out_shape = [
        jax.ShapeDtypeStruct((parts, heads, HD, keys), BF16),
        jax.ShapeDtypeStruct((heads, 2, HD, 1), F32),
    ]
    if not extra:
        out_specs = [pl.BlockSpec((1, HD, tokens), lambda h: (h, 0, 0))] + out_specs
        out_shape = [jax.ShapeDtypeStruct((heads, HD, tokens), BF16)] + out_shape
    return pl.pallas_call(
        functools.partial(attend_back_kernel, bool(extra), valid),
        grid=(heads,),
        in_specs=[head_block(q, starts[0]), head_block(k, starts[1]), head_block(v, starts[2])]
        + [fixed(a) for a in [qg, kg] + extra]
        + [head_block(out, 0), head_block(lse, 0), head_block(grad, 0)],
        out_specs=out_specs,
        out_shape=out_shape,
        scratch_shapes=[
            pltpu.VMEM((HD, keys), F32),
            pltpu.VMEM((HD, keys), F32),
            pltpu.VMEM((HD, tokens), F32),
        ],
        compiler_params=pltpu.CompilerParams(vmem_limit_bytes=48 * 2**20),
        cost_estimate=FREE,
        name="attend_back",
    )(q, k, v, qg, kg, *extra, out, lse, grad)


CHUNK = 256


def core_pair(with_chip=False):
    group, chip, core = (lax.axis_index(axis) for axis in ("dp", "row", "col"))
    other, across = (group, chip, 1 - core), (group, 1 - chip, core)
    barrier = pltpu.get_barrier_semaphore()
    greeted = (other, across) if with_chip else (other,)
    for device in greeted:
        pl.semaphore_signal(barrier, inc=1, device_id=device, device_id_type=MESH)
    pl.semaphore_wait(barrier, len(greeted))
    return (other, across) if with_chip else other


def rows_at(step, base=0):
    return pl.ds(pl.multiple_of(base + step * CHUNK, CHUNK), CHUNK)


def send(src, dst, sems, step, other):
    return pltpu.make_async_remote_copy(
        src_ref=src,
        dst_ref=dst,
        send_sem=sems.at[0, step],
        recv_sem=sems.at[1, step],
        device_id=other,
        device_id_type=MESH,
    )


def join_rows(dst, own, far):
    size = own.shape[0]
    dst[:size] = own[...]
    dst[size:] = far[...]


def join_columns(dst, own, far):
    size = own.shape[1]
    dst[:, :size] = own[...]
    dst[:, size:] = far[...]


def row_norm(values):
    average = jnp.mean(values, axis=1, keepdims=True)
    variance = jnp.mean(values * values, axis=1, keepdims=True) - average * average
    inverse = lax.rsqrt(variance + EPSILON)
    return (values - average) * inverse, inverse


def row_norm_back(grad, normed, inverse, gain):
    scaled = grad * gain
    first = jnp.mean(scaled, axis=1, keepdims=True)
    second = jnp.mean(scaled * normed, axis=1, keepdims=True)
    return inverse * (scaled - first - normed * second)


GELU_A = 0.7978845608028654
GELU_B = 0.044715


def gelu_parts(pre):
    square = pre * pre
    angle = jnp.tanh(GELU_A * pre * (1.0 + GELU_B * square))
    value = 0.5 * pre * (1.0 + angle)
    slope = 0.5 * (1.0 + angle) + 0.5 * pre * (1.0 - angle * angle) * GELU_A * (
        1.0 + 3.0 * GELU_B * square
    )
    return value, slope


def steps(body, half):
    def one(step, carry):
        body(step)
        return carry

    lax.fori_loop(0, half // CHUNK, one, 0)


def forward_kernel(tokens_last, residual, shifted, feed, fetch, *refs):
    refs = list(refs)
    take = lambda: refs.pop(0)
    a_ref, w1o = take(), take()
    w1f = None if fetch else take()
    gain = take()
    res_ref = take() if residual else None
    shift = take() if shifted else None
    w2o = take()
    w2f = None if fetch else take()
    if feed:
        w3o, w3f = take(), take()
    state_ref, x_ref, out_ref = take(), take(), take()
    w1, w2, sent, got, sems, x_sems = take(), take(), take(), take(), take(), take()
    if feed:
        w3, sent_out, got_out, out_sems = take(), take(), take(), take()
    half = state_ref.shape[0]
    if fetch:
        w1f, w2f, far_sems = take(), take(), take()
        other, across = core_pair(True)
        fetches = [
            send(own, far, far_sems, step, across)
            for step, (own, far) in enumerate(((w1o, w1f), (w2o, w2f)))
        ]
        for copy in fetches:
            copy.start()
        fetches[0].wait_recv()
    else:
        other = core_pair()
    join_columns(w1, w1o, w1f)

    def rows_of(step, base):
        if tokens_last:
            return a_ref[:, rows_at(step, base)].T
        return a_ref[rows_at(step, base)]

    def give(step):
        at = rows_at(step)
        sent[at] = dot_nn(rows_of(step, half), w1[...])
        send(sent.at[at], got.at[at], sems, step, other).start()

    steps(give, half)
    if not fetch:
        join_rows(w2, w2o, w2f)
    if feed:
        join_columns(w3, w3o, w3f)

    def keep(step):
        at = rows_at(step)
        state = dot_nn(rows_of(step, 0), w1[...])
        if residual:
            state = state + res_ref[at]
        send(sent.at[at], got.at[at], sems, step, other).wait_recv()
        state = state + got[at]
        state_ref[at] = state
        x = row_norm(state)[0] * gain[...]
        if shifted:
            x = x + shift[...]
        x_ref[at] = x.astype(BF16)
        send(x_ref.at[at], x_ref.at[rows_at(step, half)], x_sems, step, other).start()

    steps(keep, half)
    if fetch:
        fetches[1].wait_recv()
        join_rows(w2, w2o, w2f)

    def arrive(step):
        at = rows_at(step)
        send(x_ref.at[at], x_ref.at[rows_at(step, half)], x_sems, step, other).wait_recv()

    if feed:

        def hidden(step, base):
            pre = dot_nn(x_ref[rows_at(step, base)], w2[...])
            return dot_nn(gelu_parts(pre)[0].astype(BF16), w3[...])

        def give_out(step):
            at = rows_at(step)
            arrive(step)
            sent_out[at] = hidden(step, half)
            send(sent_out.at[at], got_out.at[at], out_sems, step, other).start()

        steps(give_out, half)

        def keep_out(step):
            at = rows_at(step)
            value = hidden(step, 0) + state_ref[at]
            send(sent_out.at[at], got_out.at[at], out_sems, step, other).wait_recv()
            out_ref[at] = (value + got_out[at]).astype(BF16)

        steps(keep_out, half)
    else:

        def near_out(step):
            at = rows_at(step)
            out_ref[:, at] = dot_nn(x_ref[at], w2[...]).T

        steps(near_out, half)

        def far_out(step):
            arrive(step)
            at = rows_at(step, half)
            out_ref[:, at] = dot_nn(x_ref[at], w2[...]).T

        steps(far_out, half)

    def drain(step):
        at = rows_at(step)
        send(sent.at[at], got.at[at], sems, step, other).wait_send()
        send(x_ref.at[at], x_ref.at[rows_at(step, half)], x_sems, step, other).wait_send()
        if feed:
            send(sent_out.at[at], got_out.at[at], out_sems, step, other).wait_send()

    steps(drain, half)
    if fetch:
        for copy in fetches:
            copy.wait_send()


def whole_call(kernel, operands, out_shape, scratch_shapes, collective, name):
    vmem = pl.BlockSpec(memory_space=pltpu.VMEM)
    return pl.pallas_call(
        kernel,
        in_specs=[vmem] * len(operands),
        out_specs=[vmem] * len(out_shape),
        out_shape=[jax.ShapeDtypeStruct(shape, dtype) for shape, dtype in out_shape],
        scratch_shapes=scratch_shapes,
        compiler_params=pltpu.CompilerParams(
            collective_id=collective, has_side_effects=True, vmem_limit_bytes=60 * 2**20
        ),
        cost_estimate=FREE,
        name=name,
    )(*operands)


def pair_sems(half):
    return pltpu.SemaphoreType.DMA((2, half // CHUNK))


def forward_bridge(a, tokens_last, w1, gain, res, shift, w2, w3, collective, name):
    tokens = a.shape[1] if tokens_last else a.shape[0]
    half = tokens // 2
    feed = w3 is not None
    operands = [a, *w1, gain]
    operands += [res] if res is not None else []
    operands += [shift] if shift is not None else []
    operands += [*w2] + ([*w3] if feed else [])
    depth, wide = w1[0].shape[0], w2[0].shape[1]
    out_shape = [((half, D), F32), ((tokens, D), BF16)]
    out_shape += [((half, D), BF16)] if feed else [((wide, tokens), F32)]
    part = pltpu.VMEM((half, D), F32)
    joined = [(depth, D), (D, wide)]
    scratch = [part, part, pair_sems(half), pair_sems(half)]
    if len(w1) == 1:
        out_shape += [(shape, BF16) for shape in joined]
    else:
        scratch = [pltpu.VMEM(shape, BF16) for shape in joined] + scratch
    if feed:
        scratch += [pltpu.VMEM((wide, D), BF16), part, part, pair_sems(half)]
    fetch = len(w1) == 1
    if fetch:
        scratch += [
            pltpu.VMEM(w1[0].shape, BF16),
            pltpu.VMEM(w2[0].shape, BF16),
            pltpu.SemaphoreType.DMA((2, 2)),
        ]
    return whole_call(
        functools.partial(
            forward_kernel, tokens_last, res is not None, shift is not None, feed, fetch
        ),
        operands,
        out_shape,
        scratch,
        collective,
        name,
    )


def backward_kernel(feed, summed, tokens_last, whole, *refs):
    refs = list(refs)
    take = lambda: refs.pop(0)
    if feed:
        cot_ref, feed_ref, w3o, w3f = take(), take(), take(), take()
    else:
        g_ref, res_ref = take(), take()
    if whole:
        w2, state_ref, gain, w1 = take(), take(), take(), take()
    else:
        w2o, w2f, state_ref, gain, w1o, w1f = (take() for _ in range(6))
    if feed:
        hidden_ref, pre_ref = take(), take()
    total_ref, b_ref, out_ref, gain_ref = take(), take(), take(), take()
    if summed:
        sum_ref = take()
    if not whole:
        w1, w2 = take(), take()
    sent, got, sems, x_sems = take(), take(), take(), take()
    if feed:
        w3 = take()
    half = state_ref.shape[0]
    other = core_pair()
    if not whole:
        join_rows(w2, w2o, w2f)
    if feed:
        join_columns(w3, w3o, w3f)

    def part(step, base):
        at = rows_at(step, base)
        if feed:
            value, slope = gelu_parts(dot_nn(feed_ref[at], w2[...]))
            hidden_ref[at] = value.astype(BF16)
            rows = (dot_nt(cot_ref[at], w3[...]) * slope).astype(BF16)
            pre_ref[at] = rows
        else:
            rows = g_ref[:, at].T
        return dot_nt(rows, w2[...])

    def give(step):
        at = rows_at(step)
        sent[at] = part(step, half)
        send(sent.at[at], got.at[at], sems, step, other).start()

    steps(give, half)
    if not whole:
        join_columns(w1, w1o, w1f)
    gain_ref[...] = jnp.zeros_like(gain_ref)
    if summed:
        sum_ref[...] = jnp.zeros_like(sum_ref)

    def keep(step):
        at = rows_at(step)
        grad = part(step, 0)
        send(sent.at[at], got.at[at], sems, step, other).wait_recv()
        grad = grad + got[at]
        normed, inverse = row_norm(state_ref[at])
        gain_ref[...] += jnp.sum(grad * normed, axis=0, keepdims=True)
        if summed:
            sum_ref[...] += jnp.sum(grad, axis=0, keepdims=True)
        back = row_norm_back(grad, normed, inverse, gain[...])
        total = back + (cot_ref[at].astype(F32) if feed else res_ref[at])
        total_ref[at] = total
        b_ref[at] = total.astype(BF16)
        send(b_ref.at[at], b_ref.at[rows_at(step, half)], x_sems, step, other).start()

    steps(keep, half)

    def product(at):
        value = dot_nt(b_ref[at], w1[...])
        if tokens_last:
            out_ref[:, at] = value.T.astype(out_ref.dtype)
        else:
            out_ref[at] = value.astype(out_ref.dtype)

    def near_out(step):
        product(rows_at(step))

    steps(near_out, half)

    def far_out(step):
        at = rows_at(step)
        send(b_ref.at[at], b_ref.at[rows_at(step, half)], x_sems, step, other).wait_recv()
        product(rows_at(step, half))

    steps(far_out, half)

    def drain(step):
        at = rows_at(step)
        send(sent.at[at], got.at[at], sems, step, other).wait_send()
        send(b_ref.at[at], b_ref.at[rows_at(step, half)], x_sems, step, other).wait_send()

    steps(drain, half)


def backward_bridge(g, res, feed, w2, state, gain, w1, summed, tokens_last, collective, name):
    half = state.shape[0]
    tokens = 2 * half
    depth, wide = w2[0].shape[1], w1[0].shape[0]
    if feed:
        operands = [feed[0], feed[1], *feed[2]]
    else:
        operands = [g, res]
    operands += [*w2, state, gain, *w1]
    out_shape = [((tokens, depth), BF16)] * 2 if feed else []
    out_shape += [((half, D), F32), ((tokens, D), BF16)]
    out_shape += [((wide, tokens), BF16)] if tokens_last else [((tokens, wide), F32)]
    out_shape += [((1, D), F32)] * (2 if summed else 1)
    part = pltpu.VMEM((half, D), F32)
    scratch = [part, part, pair_sems(half), pair_sems(half)]
    whole = len(w1) == 1
    if not whole:
        scratch = [pltpu.VMEM((wide, D), BF16), pltpu.VMEM((D, depth), BF16)] + scratch
    if feed:
        scratch += [pltpu.VMEM((depth, D), BF16)]
    return whole_call(
        functools.partial(backward_kernel, bool(feed), summed, tokens_last, whole),
        operands,
        out_shape,
        scratch,
        collective,
        name,
    )


def product_kernel(by_rows, left_last, left_ref, right_ref, own_ref, far_ref):
    left, right = left_ref[...], right_ref[...]
    if by_rows:
        if left_last:
            value = dot_nn(left, right).T
        else:
            value = dot_tn(right, left)
        value = value.astype(BF16)
        size = value.shape[0] // 2
        parts = (value[:size], value[size:])
    else:
        value = dot_nn(left, right) if left_last else dot_tn(left, right)
        value = value.astype(BF16)
        size = value.shape[1] // 2
        parts = (value[:, :size], value[:, size:])
    for part, ref in zip(parts, (own_ref, far_ref)):
        rows, columns = ref.shape
        if part.shape == ref.shape:
            ref[...] = part
        else:
            ref[:, : columns // 2] = part[:rows]
            ref[:, columns // 2 :] = part[rows:]


def weight_product(left, left_last, right, by_rows, tile, name):
    wide = left.shape[0] if left_last else left.shape[1]
    tokens, across = right.shape
    if left_last:
        left_spec = pl.BlockSpec((tile, tokens), lambda i: (i, 0))
    else:
        left_spec = pl.BlockSpec((tokens, tile), lambda i: (0, i))
    rows = tile * across // 2 // D
    out_spec = pl.BlockSpec((rows, D), lambda i: (i, 0))
    out_shape = jax.ShapeDtypeStruct((rows * (wide // tile), D), BF16)
    return pl.pallas_call(
        functools.partial(product_kernel, by_rows, left_last),
        grid=(wide // tile,),
        in_specs=[left_spec, pl.BlockSpec((tokens, across), lambda i: (0, 0))],
        out_specs=[out_spec, out_spec],
        out_shape=[out_shape, out_shape],
        compiler_params=pltpu.CompilerParams(vmem_limit_bytes=48 * 2**20),
        cost_estimate=FREE,
        name=name,
    )(left, right)


def pieces_of(rows):
    for pieces in (3, 2, 5):
        if rows % (16 * pieces) == 0:
            return pieces
    return 1


def ring_kernel(size, plan, *refs):
    refs = list(refs)
    sections = len(plan)

    def take(count):
        return [refs.pop(0) for _ in range(count)]

    own_refs = [take(len(parts)) for _, parts in plan]
    far_refs = [take(len(parts)) for _, parts in plan]
    out_refs = take(sections)
    work_refs = take(sections)
    slot_refs = take(sections)
    sends, arrivals, far_sems = take(3)
    index = lax.axis_index("dp")
    chip = lax.axis_index("row")
    core = lax.axis_index("col")
    across = size // 2
    side = lax.rem(index, 2)
    level = index // 2
    place = (1 - side) * level + side * (size - 1 - level)

    def device_at(where):
        where = lax.rem(where + size, size)
        turned = where // across
        high = (1 - turned) * where + turned * (size - 1 - where)
        return (high * 2 + turned, chip, core)

    neighbours = (device_at(place + 1), device_at(place - 1))
    partner = (index, 1 - chip, core)
    barrier = pltpu.get_barrier_semaphore()
    for device in neighbours + (partner,):
        pl.semaphore_signal(barrier, inc=1, device_id=device, device_id_type=MESH)
    pl.semaphore_wait(barrier, 3)

    exchanges = []
    for section in range(sections):
        exchanges.append([])
        if plan[section][0]:
            base = 0
            for number, far in enumerate(far_refs[section]):
                rows = far.shape[0]
                exchange = pltpu.make_async_remote_copy(
                    src_ref=far,
                    dst_ref=work_refs[section].at[base : base + rows],
                    send_sem=far_sems.at[0, section, number],
                    recv_sem=far_sems.at[1, section, number],
                    device_id=partner,
                    device_id_type=MESH,
                )
                exchange.start()
                exchanges[section].append(exchange)
                base += rows

    def ring(which, source, total, slots):
        half = source.shape[0] // 2
        rows = half // size
        pieces = pieces_of(rows)
        piece = rows // pieces

        def span(way, chunk, part):
            chunk = lax.rem(chunk + 2 * size, size)
            return pl.ds(pl.multiple_of(way * half + chunk * rows + part * piece, 16), piece)

        def chunk_of(way, step):
            return place - step if way == 0 else place + step

        def within(part):
            return pl.ds(part * piece, piece)

        def copy(way, part, step, src, dst, phase):
            return pltpu.make_async_remote_copy(
                src_ref=src,
                dst_ref=dst,
                send_sem=sends.at[which, phase, way, part, step],
                recv_sem=arrivals.at[which, phase, way, part, step],
                device_id=neighbours[way],
                device_id_type=MESH,
            )

        def first(way, part):
            src = source.at[span(way, chunk_of(way, 0), part)]
            return copy(way, part, 0, src, slots.at[way, 0, within(part)], 0)

        def reduced(way, part, step):
            src = slots.at[way, step - 1, within(part)]
            return copy(way, part, step, src, slots.at[way, step, within(part)], 0)

        def spread(way, part, step):
            at = span(way, chunk_of(way, step) + (1 if way == 0 else -1), part)
            return copy(way, part, step, total.at[at], total.at[at], 1)

        def arrival(way, part, step):
            return first(way, part) if isinstance(step, int) else reduced(way, part, step)

        def added(way, part, step):
            at = span(way, chunk_of(way, step + 1), part)
            got = slots[way, step, within(part)]
            return at, (source[at].astype(F32) + got.astype(F32)).astype(BF16)

        each = [(way, part) for part in range(pieces) for way in range(2)]
        for way, part in each:
            first(way, part).start()

        def reduce_step(step, carry):
            for way, part in each:
                arrival(way, part, step).wait_recv()
                _, value = added(way, part, step)
                slots[way, step, within(part)] = value
                reduced(way, part, step + 1).start()
            return carry

        reduce_step(0, 0)
        lax.fori_loop(1, size - 2, reduce_step, 0)
        for way, part in each:
            reduced(way, part, size - 2).wait_recv()
            at, value = added(way, part, size - 2)
            total[at] = value
            spread(way, part, 0).start()

        def gather_step(step, carry):
            for way, part in each:
                spread(way, part, step).wait_recv()
                spread(way, part, step + 1).start()
            return carry

        lax.fori_loop(0, size - 2, gather_step, 0)
        for way, part in each:
            spread(way, part, size - 2).wait_recv()
            first(way, part).wait_send()
            spread(way, part, 0).wait_send()

        def drain(step, carry):
            for way, part in each:
                reduced(way, part, step).wait_send()
                spread(way, part, step).wait_send()
            return carry

        lax.fori_loop(1, size - 1, drain, 0)

    for section in range(sections):
        exchanged, parts = plan[section]
        work = work_refs[section]
        base = 0
        for number, rows in enumerate(parts):
            own = own_refs[section][number][...]
            if exchanged:
                exchanges[section][number].wait()
                near = work[base : base + rows]
            else:
                near = far_refs[section][number][...]
            work[base : base + rows] = (own.astype(F32) + near.astype(F32)).astype(BF16)
            base += rows
        if base < work.shape[0]:
            work[base:] = jnp.zeros((work.shape[0] - base, work.shape[1]), BF16)
        ring(section, work, out_refs[section], slot_refs[section])


def ring_sum(size, sections):
    vmem = pl.BlockSpec(memory_space=pltpu.VMEM)
    plan = tuple((exchanged, tuple(own.shape[0] for own in owns)) for exchanged, owns, _ in sections)
    owns = [own for _, parts, _ in sections for own in parts]
    fars = [far for _, _, parts in sections for far in parts]
    totals = [sum(parts) for _, parts in plan]
    totals = [rows + -rows % (32 * size) for rows in totals]
    whole = [pltpu.VMEM((rows, D), BF16) for rows in totals]
    slots = [pltpu.VMEM((2, size - 1, rows // 2 // size, D), BF16) for rows in totals]
    pieces = max(pieces_of(rows // 2 // size) for rows in totals)
    sems = pltpu.SemaphoreType.DMA((len(sections), 2, 2, pieces, size - 1))
    most = max(len(parts) for _, parts in plan)
    return pl.pallas_call(
        functools.partial(ring_kernel, size, plan),
        in_specs=[vmem] * (len(owns) + len(fars)),
        out_specs=[vmem] * len(sections),
        out_shape=[jax.ShapeDtypeStruct((rows, D), BF16) for rows in totals],
        scratch_shapes=whole
        + slots
        + [sems, sems, pltpu.SemaphoreType.DMA((2, len(sections), most))],
        compiler_params=pltpu.CompilerParams(
            collective_id=0, has_side_effects=True, vmem_limit_bytes=62 * 2**20
        ),
        cost_estimate=FREE,
        name="ring_sum",
    )(*owns, *fars)


def shards(
    latents,
    skip_input,
    condition,
    text_states,
    positions,
    cotangent,
    skip_gain,
    skip_weight,
    shift_weight,
    self_gain,
    self_weight,
    query_gain,
    key_gain,
    self_out,
    cross_gain,
    cross_query,
    cross_context,
    cross_query_gain,
    cross_key_gain,
    cross_out,
    feed_gain,
    up_weight,
    down_weight,
):
    tokens, width = latents.shape
    half = tokens // 2
    heads_here = width // HD
    core = lax.axis_index("col")
    chip = lax.axis_index("row")
    straight = core == chip

    def own_first(values):
        return (
            lax.dynamic_slice_in_dim(values, core * half, half, 0),
            lax.dynamic_slice_in_dim(values, (1 - core) * half, half, 0),
        )

    def in_order(own, other):
        return jnp.where(
            core == 0, jnp.concatenate([own, other]), jnp.concatenate([other, own])
        )

    skip_flat = skip_weight.reshape(2 * width, -1)
    self_flat = self_weight.reshape(-1, 3 * width)
    context_flat = cross_context.reshape(-1, 2 * width)

    rows = up_weight.shape[0]
    norm_far = other_chip(jnp.stack([self_gain, cross_gain, feed_gain]))

    def near_and_far(weight):
        return (weight, other_chip(weight))

    def share_of(weight):
        share = weight.shape[0] // lax.axis_size("dp")
        piece = lax.dynamic_slice_in_dim(weight, lax.axis_index("dp") * share, share, 0)
        return other_chip(piece)

    up_share, down_share = share_of(up_weight), share_of(down_weight)
    up_pair = (up_weight, lax.all_gather(up_share, "dp", axis=0, tiled=True))
    down_pair = (down_weight, lax.all_gather(down_share, "dp", axis=0, tiled=True))
    norm_gains = jnp.concatenate([jnp.stack([self_gain, cross_gain, feed_gain]), norm_far], axis=1)
    self_gain_all, cross_gain_all, feed_gain_all = norm_gains[0:1], norm_gains[1:2], norm_gains[2:3]

    text_near = other_core(text_states)
    text_mine = jnp.where(straight, text_states, text_near)
    text_here = text_states.shape[0]
    kept, handed = own_first(cotangent)
    handed = other_core(handed)
    cot_mine = jnp.where(straight, kept, handed)

    place_own, place_other = own_first(positions)
    places = jnp.concatenate([place_own, place_other]).astype(F32)
    quarter = HD // 4
    frequency = 10000.0 ** (-jnp.arange(quarter, dtype=F32) / quarter)
    angles = frequency[:, None] * places.T[:, None, :]
    cosine = jnp.cos(angles)
    sine = jnp.sin(angles)
    cosine = jnp.stack([cosine, cosine], axis=1).reshape(HD, tokens)
    sine = jnp.stack([-sine, sine], axis=1).reshape(HD, tokens)

    lat_own, lat_other = own_first(latents)
    skip_own, skip_other = own_first(skip_input)
    lat = jnp.concatenate([lat_own, lat_other]).astype(F32)
    joint = jnp.concatenate([skip_own, skip_other]).astype(F32)
    sums = jnp.stack(
        [jnp.sum(lat, axis=1) + jnp.sum(joint, axis=1), jnp.sum(lat * lat, axis=1) + jnp.sum(joint * joint, axis=1)]
    )

    def swap_halves(values):
        return jnp.concatenate([values[:, half:], values[:, :half]], axis=1)

    sums = sums + swap_halves(other_core(sums))
    average = (sums[0] / (2 * D))[:, None]
    skip_inverse = lax.rsqrt((sums[1] / (2 * D))[:, None] - average * average + EPSILON)
    skip_low = jnp.concatenate(
        [
            (lat - average) * skip_inverse * skip_gain[0],
            (joint - average) * skip_inverse * skip_gain[1],
        ],
        axis=1,
    ).astype(BF16)

    cond_low = jax.nn.silu(condition.astype(F32)).astype(BF16)
    shift_part = contract(cond_low, shift_weight)
    shift_part = shift_part + other_core(shift_part)
    shift_mine = lax.dynamic_slice_in_dim(shift_part, chip, 1, 0)
    shift_far = other_chip(lax.dynamic_slice_in_dim(shift_part, 1 - chip, 1, 0))
    shift_row = jnp.concatenate([shift_mine, shift_far], axis=1)

    first_state, first_all, mixed_raw, skip_whole, self_whole = forward_bridge(
        skip_low, False, (skip_flat,), self_gain_all, None, shift_row, (self_flat,), None, 1, "into_self"
    )
    mixed_raw = mixed_raw.reshape(3 * heads_here, HD, tokens)

    def near_and_later(weight):
        return (weight, other_chip(after(weight, first_all)))

    out_pair = near_and_later(self_out)
    query_pair = near_and_later(cross_query)
    text_far = other_chip(after(jnp.where(straight, text_near, text_states), first_all))
    context_pair = near_and_later(context_flat)
    context_far = context_pair[1]
    cross_pair = near_and_later(cross_out)
    cot_far = other_chip(after(jnp.where(straight, handed, kept), context_far))
    text_all = jnp.concatenate([text_mine, text_far], axis=1)
    text_all = jnp.pad(text_all, ((0, -text_here % 128), (0, 0)))
    context_all = jnp.concatenate([context_flat, context_far])
    self_args = (
        (mixed_raw, mixed_raw, mixed_raw),
        (0, heads_here, 2 * heads_here),
        heads_here,
        query_gain[:, None],
        key_gain[:, None],
        (cosine, sine),
        tokens,
    )
    heads_low, log_first = attend(*self_args[0], *self_args[1:])
    heads_flat = heads_low.reshape(width, tokens)
    second_state, cross_all, probe_raw = forward_bridge(
        heads_flat, True, out_pair, cross_gain_all, first_state, None, query_pair, None, 2, "into_cross"
    )
    probe_raw = probe_raw.reshape(heads_here, HD, tokens)
    memory_raw = lax.dot_general(
        context_all, text_all, (((0,), (1,)), ((), ())), preferred_element_type=F32
    ).reshape(2 * heads_here, HD, -1)
    cross_args = (
        (probe_raw, memory_raw, memory_raw),
        (0, 0, heads_here),
        heads_here,
        cross_query_gain[:, None],
        cross_key_gain[:, None],
        (),
        text_here,
    )
    cross_low, log_second = attend(*cross_args[0], *cross_args[1:])
    cross_flat = cross_low.reshape(width, tokens)
    third_state, feed_all, out_own = forward_bridge(
        cross_flat, True, cross_pair, feed_gain_all, second_state, None, up_pair, down_pair, 3, "into_feed"
    )
    row_width = up_weight.shape[0]
    out_mine = out_own[:, :row_width]
    out_far = other_chip(out_own[:, row_width:])

    cot_own = jnp.concatenate([cot_mine, after(cot_far, cross_all)], axis=1)
    cot_all = pair(cot_own)
    (
        hidden_low,
        grad_pre,
        grad_third,
        branch_two_all,
        grad_cross_heads,
        feed_gain_part,
    ) = backward_bridge(
        None,
        None,
        (cot_all, feed_all, down_pair),
        up_pair,
        third_state,
        feed_gain_all,
        cross_pair,
        False,
        True,
        4,
        "from_feed",
    )
    down_own, down_far = weight_product(hidden_low, False, cot_all, False, 768, "grad_down")
    up_own, up_far = weight_product(grad_pre, False, feed_all, True, 1152, "grad_up")
    cross_own, cross_far = weight_product(
        cross_flat, True, branch_two_all, False, 576, "grad_cross_out"
    )
    down_far_here = other_chip(down_far)
    up_far_here = other_chip(up_far)
    grad_cross_heads = after(grad_cross_heads, (down_far, up_far))
    grad_probe, grad_memory, grad_cross_gains = attend_back(
        *cross_args[0],
        *cross_args[1:],
        cross_low,
        log_second,
        grad_cross_heads.reshape(heads_here, HD, tokens),
    )
    probe_low = grad_probe.reshape(width, tokens)
    query_own, query_far = weight_product(probe_low, True, cross_all, True, 576, "grad_cross_query")
    memory_low = grad_memory.reshape(2 * width, -1)
    context_own, context_far = weight_product(
        memory_low, True, text_all, True, 576, "grad_context"
    )
    text_part = lax.dot_general(
        memory_low, context_all, (((0,), (1,)), ((), ())), preferred_element_type=F32
    )[:text_here]
    text_width = text_states.shape[1]
    text_one, text_two = text_part[:, :text_width], text_part[:, text_width:]
    text_sum = jnp.where(straight, text_one, text_two) + other_core(
        jnp.where(straight, text_two, text_one)
    )
    text_sum = text_sum.astype(BF16)
    text_back = lax.ppermute(text_sum, ("row", "col"), [(1, 2), (2, 1)])
    grad_text_states = jnp.where(straight, text_sum, text_back)

    grad_second, branch_one_all, grad_heads, cross_gain_part = backward_bridge(
        probe_low,
        grad_third,
        None,
        query_pair,
        second_state,
        cross_gain_all,
        out_pair,
        False,
        True,
        5,
        "from_cross",
    )
    out_grad_own, out_grad_far = weight_product(
        heads_flat, True, branch_one_all, False, 576, "grad_self_out"
    )
    grad_heads_in = after(grad_heads, down_far_here)
    grad_mixed, grad_self_gains = attend_back(
        *self_args[0],
        *self_args[1:],
        heads_low,
        log_first,
        grad_heads_in.reshape(heads_here, HD, tokens),
    )
    mixed_low = grad_mixed.reshape(3 * width, tokens)
    self_own, self_far = weight_product(mixed_low, True, first_all, True, 576, "grad_self")
    _, grad_first_all, grad_skip_out, self_gain_part, shift_grad = backward_bridge(
        mixed_low,
        grad_second,
        None,
        (self_whole,),
        first_state,
        self_gain_all,
        (skip_whole,),
        True,
        False,
        6,
        "from_self",
    )
    skip_own, skip_far = weight_product(skip_low, False, grad_first_all, False, 384, "grad_skip")
    shift_grad = shift_grad + other_core(shift_grad)
    shift_here = shift_grad[:, :row_width]
    shift_there = other_chip(shift_grad[:, row_width:])
    shift_pair = jnp.where(
        chip == 0,
        jnp.concatenate([shift_here, shift_there]),
        jnp.concatenate([shift_there, shift_here]),
    )
    out_far = after(out_far, grad_skip_out)
    out_kept = jnp.where(straight, out_mine, out_far)
    out_got = other_core(jnp.where(straight, out_far, out_mine))
    block_out = in_order(out_kept, out_got)
    lat_normed = (lat - average) * skip_inverse
    joint_normed = (joint - average) * skip_inverse
    grad_lat, grad_joint = grad_skip_out[:, :width], grad_skip_out[:, width:]
    lat_scaled, joint_scaled = grad_lat * skip_gain[0], grad_joint * skip_gain[1]
    sums_back = jnp.stack(
        [
            jnp.sum(lat_scaled, axis=1) + jnp.sum(joint_scaled, axis=1),
            jnp.sum(lat_scaled * lat_normed, axis=1) + jnp.sum(joint_scaled * joint_normed, axis=1),
        ]
    )
    sums_back = sums_back + swap_halves(other_core(sums_back))
    first_mean = (sums_back[0] / (2 * D))[:, None]
    second_mean = (sums_back[1] / (2 * D))[:, None]
    skip_gain_part = jnp.stack(
        [jnp.sum(grad_lat * lat_normed, axis=0), jnp.sum(grad_joint * joint_normed, axis=0)]
    )
    grad_lat = (skip_inverse * (lat_scaled - first_mean - lat_normed * second_mean)).astype(BF16)
    grad_joint = (skip_inverse * (joint_scaled - first_mean - joint_normed * second_mean)).astype(BF16)
    grad_latents = in_order(grad_lat[:half], grad_lat[half:])
    grad_skip_input = in_order(grad_joint[:half], grad_joint[half:])

    wide = jnp.concatenate([self_gain_part, cross_gain_part, feed_gain_part])
    wide = wide + other_core(wide)
    narrow = jnp.concatenate([jnp.sum(grad_self_gains, axis=0), jnp.sum(grad_cross_gains, axis=0)])
    narrow = narrow[:, :, 0]
    narrow = narrow + other_core(narrow)

    def flat(*pieces):
        return jnp.concatenate([piece.reshape(-1) for piece in pieces])

    kept_gains = flat(wide[:, :row_width], narrow, skip_gain_part)
    sent_gains = flat(wide[:, row_width:], narrow, skip_gain_part)
    small = flat(
        kept_gains + other_chip(sent_gains), cond_low.astype(F32), shift_pair
    )
    groups = lax.axis_size("dp")
    smalls = [small] + [
        lax.ppermute(small, "dp", [(i, (i + k) % groups) for i in range(groups)])
        for k in range(1, groups)
    ]
    down_sum = (down_own.astype(F32) + down_far_here.astype(F32)).astype(BF16)
    up_far_here = after(up_far_here, down_sum)
    high, middle, inner, last = ring_sum(
        groups,
        [
            (False, [up_own], [up_far_here]),
            (
                True,
                [cross_own, out_grad_own, query_own, context_own],
                [cross_far, out_grad_far, query_far, context_far],
            ),
            (True, [self_own], [self_far]),
            (True, [skip_own], [skip_far]),
        ],
    )
    grad_down = lax.psum(down_sum, "dp")

    def unpack(block, count):
        rows = block.shape[0] // count
        pieces = [block[i * rows : (i + 1) * rows] for i in range(count)]
        return [
            jnp.concatenate([piece[:, :width], piece[:, width:]]).astype(F32) for piece in pieces
        ]

    grad_down = jnp.concatenate(unpack(grad_down, 3))
    grad_up = jnp.concatenate([high[:row_width], high[row_width : 2 * row_width]], axis=1)
    grad_up = grad_up.astype(F32)
    place = width // 2
    grad_cross_out, grad_self_out, grad_cross_query = unpack(middle[: 3 * place], 3)
    grad_context = unpack(middle[3 * place : 3 * place + text_width], 2)
    grad_context = jnp.concatenate([grad_context[0], grad_context[1]], axis=1)
    grad_self_weight = jnp.stack(unpack(inner[: 3 * place], 3), axis=1)
    grad_skip_weight = jnp.concatenate(unpack(last[: 2 * place], 3))

    smalls = [after(value, last) for value in smalls[1:]] + smalls[:1]
    gain_count = kept_gains.shape[0]
    gain_sums = sum(value[:gain_count] for value in smalls)
    images = condition.shape[0]
    conds = [
        value[gain_count : gain_count + images * width].reshape(images, width) for value in smalls
    ]
    shifts = [value[gain_count + images * width :].reshape(images, row_width) for value in smalls]
    grad_shift_weight = lax.dot_general(
        jnp.concatenate(conds),
        jnp.concatenate(shifts),
        (((0,), (0,)), ((), ())),
        precision=PRECISE,
        preferred_element_type=F32,
    )
    wide_sum = gain_sums[: 3 * row_width].reshape(3, row_width)
    narrow_sum = gain_sums[3 * row_width : 3 * row_width + 4 * HD].reshape(4, HD)
    grad_skip_gain = gain_sums[3 * row_width + 4 * HD :].reshape(2, width)

    return (
        block_out,
        grad_latents,
        grad_skip_input,
        grad_text_states,
        grad_skip_gain,
        grad_skip_weight.reshape(skip_weight.shape),
        grad_shift_weight,
        wide_sum[0],
        grad_self_weight.reshape(self_weight.shape),
        narrow_sum[0],
        narrow_sum[1],
        grad_self_out,
        wide_sum[1],
        grad_cross_query,
        grad_context.reshape(cross_context.shape),
        narrow_sum[2],
        narrow_sum[3],
        grad_cross_out,
        wide_sum[2],
        grad_up,
        grad_down,
    )


def solution(mesh):
    placed = (
        P(("dp", "row"), "col"),
        P(("dp", "row"), "col"),
        P("dp", "col"),
        P(("dp", "col"), "row"),
        P(("dp", "row"), None),
        P(("dp", "col"), "row"),
        P(None, "col"),
        P(None, "col", "row"),
        P("col", "row"),
        P("row"),
        P("row", None, "col"),
        P(),
        P(),
        P("col", "row"),
        P("row"),
        P("row", "col"),
        P("row", None, "col"),
        P(),
        P(),
        P("col", "row"),
        P("row"),
        P("row", "col"),
        P("col", "row"),
    )
    return jax.shard_map(
        shards,
        mesh=mesh,
        in_specs=placed,
        out_specs=(
            P(("dp", "col"), "row"),
            P(("dp", "row"), "col"),
            P(("dp", "row"), "col"),
            P(("dp", "col"), "row"),
            P(None, "col"),
            P(None, "col", "row"),
            P("col", "row"),
            P("row"),
            P("row", None, "col"),
            P(),
            P(),
            P("col", "row"),
            P("row"),
            P("row", "col"),
            P("row", None, "col"),
            P(),
            P(),
            P("col", "row"),
            P("row"),
            P("row", "col"),
            P("col", "row"),
        ),
        check_vma=False,
    )
```

time: 1450 us -> 933 us (0.64)
  Pallas kernels: 0 us -> 590 us
  waiting for transfers between devices: 638 us -> 101 us
  matrix products: 260 us -> 9.68 us
  local copies, waits for them, and re-layouts: 253 us -> 101 us
  other arithmetic: 146 us -> 58.1 us
  blocking collectives: 79.5 us -> 0 us
    pallas_call x0 -> x19, Pallas kernels: none -> 590 us  [the longest x1 263 us: ring_sum(): pl.pallas_call(functools.partial(ring_kernel, size, plan), in_specs=[vmem...]
    psum x8 -> x1, waiting for transfers between devices: 300 us -> 0.01 us  [shards(): grad_down = lax.psum(down_sum, 'dp')]
    ppermute x23 -> x15, waiting for transfers between devices: 310 us -> 52.2 us  [other_chip(): return lax.ppermute(values, 'row', SWAP)]
    dot_general x68 -> x4, matrix products: 260 us -> 9.68 us  [the longest x1 3.77 us: shards(): lax.dot_general(memory_low, context_all, (((0,), (1,)), ((), ())), prefer...]
    convert_element_type x32 -> x7, other arithmetic: 90.4 us -> 19.4 us  [the longest x1 6.47 us: shards(): (skip_inverse * (joint_scaled - first_mean - joint_normed * second_mean))...]
    dynamic_update_slice x4 -> x0, local copies, waits for them, and re-layouts: 52.8 us -> none  [attend_forward(): outputs, log_totals = lax.map(one_block, (block_ids, query_blocks))]
    all_gather x2 -> x0, blocking collectives: 48.7 us -> none  [the longest x1 24.5 us: shards(): cond_every = lax.all_gather(cond_low, 'dp', axis=0, tiled=True)]
    psum x1 -> x0, blocking collectives: 30.8 us -> none  [shards(): gain_sums = lax.psum(kept_gains + other_chip(sent_gains), 'dp')]
  transfers between devices with their start and end apart: 56 -> 37, of which waited for: 17 -> 11; matrix products, arithmetic and copies ran while one was open for 40% -> 13% of each run, Pallas kernels for 0% -> 55%
where the time goes in v2:
time: 933 us; the launch traced here: 928 us
  Pallas kernels  590 us (63%)
  local copies, waits for them, and re-layouts  101 us (11%)
  waiting for transfers between devices  101 us (11%)
  other arithmetic  58.1 us (6%)
  starting transfers between devices  51.4 us (6%)
  between operations  15.7 us (2%)
  matrix products  9.68 us (1%)
    pallas_call x1, Pallas kernels, ring_sum(): pl.pallas_call(functools.partial(ring_kernel, size, plan), in_specs=[vmem...  263 us
    pallas_call x6, Pallas kernels, whole_call(): pl.pallas_call(kernel, in_specs=[vmem] * len(operands), out_specs=[vmem]...  221 us
    unnamed x262, local copies, waits for them, and re-layouts  62.9 us
    ppermute x15, waiting for transfers between devices, other_chip(): return lax.ppermute(values, 'row', SWAP)  52.2 us
    ppermute x1, waiting for transfers between devices, shards(): text_back = lax.ppermute(text_sum, ('row', 'col'), [(1, 2), (2, 1)])  48.1 us
    pallas_call x2, Pallas kernels, attend_back(): pl.pallas_call(functools.partial(attend_back_kernel, bool(extra), valid),...  44.4 us
    pallas_call x8, Pallas kernels, weight_product(): pl.pallas_call(functools.partial(product_kernel, by_rows, left_last), gri...  40.1 us
    ppermute x11, starting transfers between devices, other_core(): return lax.ppermute(values, 'col', SWAP)  28.2 us
  transfers between devices with their start and end apart: 37, of which 11 were waited for; matrix products, arithmetic and copies ran while one was open for 13% of the time, Pallas kernels for 55%

profile of v2, /device:TPU:1, one launch (start us, length us, event | category | flops | bytes accessed | tf_op | source)
XLA Modules:
  0.0 927.9 jit_solution(13030071732721587956)
XLA Ops:
  7.3 4.6 copy.102.refs_7_.refs_2_
  12.8 2.1 collective-permute-start.11
  15.0 8.3 collective-permute-done.11
  24.1 2.6 constant_dynamic-slice_fusion.9
  36.5 4.2 copy.95
  40.7 4.1 copy.96.refs_4_
  50.8 2.2 pad_maximum_fusion.refs_0_.left_ref
  53.0 96.3 %into_self.1 = (f32[512,1152]{1,0:T(8,128)}, bf16[1024,1152]{1,0:T(8,128)(2,1)}, f32[1728,1024]{1,0:T(8,128)}, bf16[1152,1152]{1,0:T(8,128)(2,1)}, bf16[1152,1728]{1,0:T(8,128)(2,1)}) custom-call(bf16[1024,1152]{1,0:T(8,128)(2,1)} %pad_maximum_fusion.refs_0_.left_ref, bf16[1152,576]{1,0:T(8,128)(2,1)} %bitcast.85, ...), custom_call_target="tpu_custom_call" | custom-call | tf_op jit(solution)/shard_map/into_self/pallas_call | solution.py:434
  154.7 2.0 broadcast_select_fusion.3
  156.8 19.8 %collective-permute-done.6 = bf16[512,1152]{0,1:T(8,128)(2,1)} collective-permute-done((bf16[512,1152]{0,1:T(8,128)(2,1)}, bf16[512,1152]{0,1:T(8,128)(2,1)}, u32[]{:S(2)}, u32[]{:S(2)}) %collective-permute-start.6) | collective-permute-done | bytes 1179680 | tf_op jit(solution)/shard_map/ppermute | solution.py:31
  180.6 15.3 %attend.2 = (bf16[8,72,1024]{2,1,0:T(8,128)(2,1)S(1)}, f32[8,1,1024]{2,1,0:T(1,128)S(1)}) custom-call(f32[24,72,1024]{2,1,0:T(8,128)} %bitcast.75, f32[24,72,1024]{2,1,0:T(8,128)} %bitcast.76, f32[24,72,1024]{2,1,0:T(8,128)} %bitcast.77, f32[72,1]{1,0:T(8,128)S(1)} %copy.97.qg_ref, f32[72,1]{1,0:T(8,128)S(1)} %copy.98.kg_ref, ...), custom_call_target="tpu_custom_call" | custom-call | tf_op jit(solution)/shard_map/attend/pallas_call | solution.py:183
  197.5 10.6 %collective-permute-done.5.refs_6_.refs_3_ = bf16[576,576]{1,0:T(8,128)(2,1)} collective-permute-done((bf16[576,576]{1,0:T(8,128)(2,1)S(1)}, bf16[576,576]{1,0:T(8,128)(2,1)}, u32[]{:S(2)}, u32[]{:S(2)}) %collective-permute-start.5) | collective-permute-done | bytes 663584 | tf_op jit(solution)/shard_map/ppermute | solution.py:31
  208.2 17.5 %into_cross.1 = (f32[512,1152]{1,0:T(8,128)}, bf16[1024,1152]{1,0:T(8,128)(2,1)}, f32[576,1024]{1,0:T(8,128)}) custom-call(bf16[576,1024]{1,0:T(8,128)(2,1)} %bitcast.63, bf16[576,576]{1,0:T(8,128)(2,1)} %refs_6_.1, bf16[576,576]{1,0:T(8,128)(2,1)} %copy-done.67, f32[1,1152]{1,0:T(1,128)} %get-tuple-element.295.refs_3_.refs_5_, ...), custom_call_target="tpu_custom_call" | custom-call | tf_op jit(solution)/shard_map/into_cross/pallas_call | solution.py:434
  230.9 8.0 collective-permute-done.8
  239.6 3.2 fusion.29
  242.9 6.9 attend.3
  249.9 3.3 pad_maximum_fusion.2.refs_0_.right_ref
  254.8 28.8 %into_feed.1 = (f32[512,1152]{1,0:T(8,128)}, bf16[1024,1152]{1,0:T(8,128)(2,1)}, bf16[512,1152]{1,0:T(8,128)(2,1)}) custom-call(bf16[576,1024]{1,0:T(8,128)(2,1)} %bitcast.65, bf16[576,576]{1,0:T(8,128)(2,1)} %refs_8_.1, bf16[576,576]{1,0:T(8,128)(2,1)} %collective-permute-done.9.refs_2_.refs_9_, f32[1,1152]{1,0:T(1,128)} %get-tuple-element.294.refs_3_.refs_7_, ...), custom_call_target="tpu_custom_call" | custom-call | tf_op jit(solution)/shard_map/into_feed/pallas_call | solution.py:434
  283.6 40.2 %from_feed.1 = (bf16[1024,2304]{1,0:T(8,128)(2,1)}, bf16[1024,2304]{1,0:T(8,128)(2,1)}, f32[512,1152]{1,0:T(8,128)}, bf16[1024,1152]{1,0:T(8,128)(2,1)}, bf16[576,1024]{1,0:T(8,128)(2,1)}, /*index=5*/f32[1,1152]{1,0:T(1,128)}) custom-call(bf16[1024,1152]{1,0:T(8,128)(2,1)} %pad_maximum_fusion.2.refs_0_.right_ref, ...), custom_call_target="tpu_custom_call" | custom-call | tf_op jit(solution)/shard_map/from_feed/pallas_call | solution.py:434
  323.9 9.2 grad_down.1
  334.6 9.4 %grad_up.1 = (bf16[1152,1152]{1,0:T(8,128)(2,1)S(1)}, bf16[1152,1152]{1,0:T(8,128)(2,1)}) custom-call(bf16[1024,2304]{1,0:T(8,128)(2,1)} %get-tuple-element.116.left_ref, bf16[1024,1152]{1,0:T(8,128)(2,1)S(1)} %copy-done.9), custom_call_target="tpu_custom_call" | custom-call | tf_op jit(solution)/shard_map/grad_up/pallas_call | solution.py:650
  345.6 15.8 %attend_back.2 = (bf16[8,72,1024]{2,1,0:T(8,128)(2,1)S(1)}, bf16[2,8,72,384]{3,2,1,0:T(8,128)(2,1)S(1)}, f32[8,2,72,1]{3,2,1,0:T(8,128)S(1)}) custom-call(f32[8,72,1024]{2,1,0:T(8,128)} %bitcast.67, f32[16,72,384]{2,1,0:T(8,128)} %bitcast.61, f32[16,72,384]{2,1,0:T(8,128)} %bitcast.62, f32[72,1]{1,0:T(8,128)S(1)} %copy-done.43, f32[72,1]{1,0:T(8,128)S(1)} %copy-done.41, ...), custom_call_target="tpu_custom_call" | custom-call | tf_op jit(solution)/shard_map/attend_back/pallas_call | solution.py:217
  361.4 3.8 fusion.28
  368.7 2.5 add_convert_fusion.1
  371.2 3.5 collective-permute-start.20
  381.8 15.9 %from_cross.1 = (f32[512,1152]{1,0:T(8,128)}, bf16[1024,1152]{1,0:T(8,128)(2,1)}, bf16[576,1024]{1,0:T(8,128)(2,1)}, f32[1,1152]{1,0:T(1,128)}) custom-call(bf16[576,1024]{1,0:T(8,128)(2,1)} %bitcast.70, f32[512,1152]{1,0:T(8,128)} %get-tuple-element.120.refs_1_, bf16[576,576]{1,0:T(8,128)(2,1)} %refs_2_.2, ...), custom_call_target="tpu_custom_call" | custom-call | tf_op jit(solution)/shard_map/from_cross/pallas_call | solution.py:434
  402.9 2.2 grad_context.1
  410.7 48.1 %collective-permute-done.20 = bf16[333,512]{1,0:T(8,128)(2,1)} collective-permute-done((bf16[333,512]{1,0:T(8,128)(2,1)}, bf16[333,512]{1,0:T(8,128)(2,1)}, u32[]{:S(2)}, u32[]{:S(2)}) %collective-permute-start.20) | collective-permute-done | bytes 341024 | tf_op jit(solution)/shard_map/ppermute | solution.py:1070
  460.6 4.7 add_convert_fusion
  469.0 28.6 %attend_back.3 = (bf16[3,8,72,1024]{3,2,1,0:T(8,128)(2,1)}, f32[8,2,72,1]{3,2,1,0:T(8,128)S(1)}) custom-call(f32[24,72,1024]{2,1,0:T(8,128)} %bitcast.78, f32[24,72,1024]{2,1,0:T(8,128)} %bitcast.79, f32[24,72,1024]{2,1,0:T(8,128)} %bitcast.80, f32[72,1]{1,0:T(8,128)S(1)} %copy-done.45, f32[72,1]{1,0:T(8,128)S(1)} %copy-done.47, f32[72,1024]{1,0:T(8,128)S(1)} %copy-done.16, ...), custom_call_target="tpu_custom_call" | custom-call | tf_op jit(solution)/shard_map/attend_back/pallas_call | solution.py:217
  497.6 8.2 grad_self.1
  508.4 21.8 %from_self.1 = (f32[512,1152]{1,0:T(8,128)}, bf16[1024,1152]{1,0:T(8,128)(2,1)}, f32[1024,1152]{1,0:T(8,128)}, f32[1,1152]{1,0:T(1,128)}, f32[1,1152]{1,0:T(1,128)}) custom-call(bf16[1728,1024]{1,0:T(8,128)(2,1)} %bitcast.82, f32[512,1152]{1,0:T(8,128)} %get-tuple-element.124.refs_1_, bf16[1152,1728]{1,0:T(8,128)(2,1)} %get-tuple-element.125.refs_2_, ...), custom_call_target="tpu_custom_call" | custom-call | tf_op jit(solution)/shard_map/from_self/pallas_call | solution.py:434
  530.3 5.7 grad_skip.1
  538.1 262.8 %ring_sum.1 = (bf16[1280,1152]{1,0:T(8,128)(2,1)}, bf16[1536,1152]{1,0:T(8,128)(2,1)}, bf16[1024,1152]{1,0:T(8,128)(2,1)}, bf16[768,1152]{1,0:T(8,128)(2,1)}) custom-call(bf16[1152,1152]{1,0:T(8,128)(2,1)} %copy-done.13, bf16[288,1152]{1,0:T(8,128)(2,1)} %copy-done.36, bf16[288,1152]{1,0:T(8,128)(2,1)} %copy-done.34, bf16[288,1152]{1,0:T(8,128)(2,1)} %copy-done.32, ...), custom_call_target="tpu_custom_call" | custom-call | tf_op jit(solution)/shard_map/ring_sum/pallas_call | solution.py:838
  800.9 3.3 fusion.44
  808.1 3.6 slice_bitcast_fusion.5
  811.6 20.0 %collective-permute-start.24 = (f32[1,1152]{1,0:T(1,128)}, f32[1,1152]{1,0:T(1,128)}, u32[]{:S(2)}, u32[]{:S(2)}) collective-permute-start(f32[1,1152]{1,0:T(1,128)} %get-tuple-element.135), channel_id=1, source_target_pairs={{0,1},{1,0},{2,3},{3,2},{4,5},{5,4},{6,7},{7,6},{8,9},{9,8},{10,11... | collective-permute-start | bytes 13832 | tf_op jit(solution)/shard_map/ppermute | solution.py:27
  831.7 6.1 fusion.11
  850.9 4.6 maximum_convert_fusion
  859.3 3.0 maximum_convert_fusion.1
  863.5 2.1 copy.116
  866.7 2.2 collective-permute-done.25
  869.1 6.5 fusion.22
  887.6 2.3 collective-permute-start.33
  894.1 4.4 collective-permute-start.17
  902.3 2.5 fusion.61
  909.1 2.1 slice_dynamic-update-slice_fusion.4
  915.9 5.0 copy.123
  (446 shorter events, 122.1 us)
Async XLA Ops:
  7.2 26.3 %copy-start = (bf16[576,576]{1,0:T(8,128)(2,1)S(1)}, bf16[576,576]{1,0:T(8,128)(2,1)}, u32[]{:S(2)}) copy-start(bf16[576,576]{1,0:T(8,128)(2,1)} %param.31) | copy-start | bytes 1990660
  7.2 247.6 %all-gather.5.cloned.1.call-start = ((), (), s32[]{:S(2)}) async-start(), calls=%async_computation.1 | async-start | bytes 3317760 | tf_op jit(solution)/shard_map/all_gather | solution.py:914
  12.8 10.4 %collective-permute-start.11 = (bf16[288,576]{1,0:T(8,128)(2,1)S(1)}, bf16[288,576]{1,0:T(8,128)(2,1)S(1)}, u32[]{:S(2)}, u32[]{:S(2)}) collective-permute-start(bf16[288,576]{1,0:T(8,128)(2,1)S(1)} %constant_dynamic-slice_fusion.2), channel_id=1, source_target_pairs={{0,2},{2,0},{1,3},{3,1},{4,6},{6,4},{5,7},{7,5},{8,10},{10,8},{9,1... | collective-permute-start | bytes 995336 | tf_op jit(solution)/shard_map/ppermute | solution.py:31
  24.1 230.7 %all-gather.3.cloned.1.call-start = ((), (), s32[]{:S(2)}) async-start(), calls=%async_computation | async-start | bytes 2985984 | tf_op jit(solution)/shard_map/all_gather | solution.py:913
  32.2 16.2 %collective-permute-start = (f32[2,1024]{1,0:T(2,128)S(1)}, f32[2,1024]{1,0:T(2,128)S(1)}, u32[]{:S(2)}, u32[]{:S(2)}) collective-permute-start(f32[2,1024]{1,0:T(2,128)S(1)} %pad_maximum_fusion.12), channel_id=1, source_target_pairs={{0,1},{1,0},{2,3},{3,2},{4,5},{5,4},{6,7},{7,6},{8,9},{9,8},{10,11... | collective-permute-start | bytes 24584 | tf_op jit(solution)/shard_map/ppermute | solution.py:27
  33.7 11.1 %collective-permute-start.2 = (f32[2,576]{1,0:T(2,128)S(1)}, f32[2,576]{1,0:T(2,128)S(1)}, u32[]{:S(2)}, u32[]{:S(2)}) collective-permute-start(f32[2,576]{1,0:T(2,128)S(1)} %fusion.41), channel_id=1, source_target_pairs={{0,1},{1,0},{2,3},{3,2},{4,5},{5,4},{6,7},{7,6},{8,9},{9,8},{10,11... | collective-permute-start | bytes 13832 | tf_op jit(solution)/shard_map/ppermute | solution.py:27
  33.8 12.5 %collective-permute-start.1 = (f32[3,576]{1,0:T(4,128)S(1)}, f32[3,576]{1,0:T(4,128)S(1)}, u32[]{:S(2)}, u32[]{:S(2)}) collective-permute-start(f32[3,576]{1,0:T(4,128)S(1)} %pad_maximum_fusion.11), channel_id=1, source_target_pairs={{0,2},{2,0},{1,3},{3,1},{4,6},{6,4},{5,7},{7,5},{8,10},{10,8},{9,1... | collective-permute-start | bytes 20744 | tf_op jit(solution)/shard_map/ppermute | solution.py:31
  36.3 12.1 %collective-permute-start.10 = (bf16[72,2304]{1,0:T(8,128)(2,1)S(1)}, bf16[72,2304]{1,0:T(8,128)(2,1)}, u32[]{:S(2)}, u32[]{:S(2)}) collective-permute-start(bf16[72,2304]{1,0:T(8,128)(2,1)S(1)} %constant_dynamic-slice_fusion.3), channel_id=1, source_target_pairs={{0,2},{2,0},{1,3},{3,1},{4,6},{6,4},{5,7},{7,5},{8,10},{10,8},{9,1... | collective-permute-start | bytes 995336 | tf_op jit(solution)/shard_map/ppermute | solution.py:31
  36.5 795.2 %copy-start.92 = (f32[576]{0:T(1024)}, f32[576]{0:T(1024)S(1)}, u32[]{:S(2)}) copy-start(f32[576]{0:T(1024)S(1)} %get-tuple-element.240) | copy-start | bytes 6916
  36.5 795.1 %copy-start.94 = (f32[576]{0:T(1024)}, f32[576]{0:T(1024)S(1)}, u32[]{:S(2)}) copy-start(f32[576]{0:T(1024)S(1)} %get-tuple-element.241) | copy-start | bytes 6916
  44.8 2.9 collective-permute-start.3
  48.5 858.6 %all-reduce.3.cloned.1.call-start = ((), (), s32[]{:S(2)}) async-start(), calls=%async_computation.2 | async-start | bytes 5308416 | tf_op jit(solution)/shard_map/psum | solution.py:1180
  53.0 96.5 %copy-start.87 = (bf16[1024,576]{0,1:T(8,128)(2,1)S(1)}, bf16[1024,576]{0,1:T(8,128)(2,1)}, u32[]{:S(2)}) copy-start(bf16[1024,576]{0,1:T(8,128)(2,1)} %param.28) | copy-start | bytes 3538948
  149.3 27.2 %collective-permute-start.6 = (bf16[512,1152]{0,1:T(8,128)(2,1)}, bf16[512,1152]{0,1:T(8,128)(2,1)}, u32[]{:S(2)}, u32[]{:S(2)}) collective-permute-start(bf16[512,1152]{0,1:T(8,128)(2,1)} %bitcast.12), channel_id=1, source_target_pairs={{0,2},{2,0},{1,3},{3,1},{4,6},{6,4},{5,7},{7,5},{8,10},{10,8},{9,1... | collective-permute-start | bytes 3538952 | tf_op jit(solution)/shard_map/ppermute | solution.py:31
  150.4 3.3 collective-permute-start.13
  151.3 76.7 %collective-permute-start.7 = (bf16[333,512]{1,0:T(8,128)(2,1)}, bf16[333,512]{1,0:T(8,128)(2,1)}, u32[]{:S(2)}, u32[]{:S(2)}) collective-permute-start(bf16[333,512]{1,0:T(8,128)(2,1)} %param.26), channel_id=1, source_target_pairs={{0,1},{1,0},{2,3},{3,2},{4,5},{5,4},{6,7},{7,6},{8,9},{9,8},{10,11... | collective-permute-start | bytes 1022984 | tf_op jit(solution)/shard_map/ppermute | solution.py:27
  151.7 45.8 %collective-permute-start.4 = (bf16[576,576]{1,0:T(8,128)(2,1)S(1)}, bf16[576,576]{1,0:T(8,128)(2,1)S(1)}, u32[]{:S(2)}, u32[]{:S(2)}) collective-permute-start(bf16[576,576]{1,0:T(8,128)(2,1)S(1)} %copy-done.65), channel_id=1, source_target_pairs={{0,2},{2,0},{1,3},{3,1},{4,6},{6,4},{5,7},{7,5},{8,10},{10,8},{9,1... | collective-permute-start | bytes 1990664 | tf_op jit(solution)/shard_map/ppermute | solution.py:31
  153.2 55.0 %collective-permute-start.5 = (bf16[576,576]{1,0:T(8,128)(2,1)S(1)}, bf16[576,576]{1,0:T(8,128)(2,1)}, u32[]{:S(2)}, u32[]{:S(2)}) collective-permute-start(bf16[576,576]{1,0:T(8,128)(2,1)S(1)} %copy-done.66), channel_id=1, source_target_pairs={{0,2},{2,0},{1,3},{3,1},{4,6},{6,4},{5,7},{7,5},{8,10},{10,8},{9,1... | collective-permute-start | bytes 1990664 | tf_op jit(solution)/shard_map/ppermute | solution.py:31
  156.8 23.6 %copy-start.116 = (f32[72]{0:T(128)S(1)}, f32[72]{0:T(128)}, u32[]{:S(2)}) copy-start(f32[72]{0:T(128)} %param.34) | copy-start | bytes 868
  156.8 23.7 %copy-start.117 = (f32[72]{0:T(128)S(1)}, f32[72]{0:T(128)}, u32[]{:S(2)}) copy-start(f32[72]{0:T(128)} %param.35) | copy-start | bytes 868
  177.6 48.1 %collective-permute-start.14 = (bf16[512,576]{0,1:T(8,128)(2,1)}, bf16[512,576]{0,1:T(8,128)(2,1)}, u32[]{:S(2)}, u32[]{:S(2)}) collective-permute-start(bf16[512,576]{0,1:T(8,128)(2,1)} %copy.107), channel_id=1, source_target_pairs={{0,2},{2,0},{1,3},{3,1},{4,6},{6,4},{5,7},{7,5},{8,10},{10,8},{9,1... | collective-permute-start | bytes 1769480 | tf_op jit(solution)/shard_map/ppermute | solution.py:31
  227.4 22.5 %collective-permute-start.15 = (bf16[512,1152]{1,0:T(8,128)(2,1)S(1)}, bf16[512,1152]{1,0:T(8,128)(2,1)}, u32[]{:S(2)}, u32[]{:S(2)}) collective-permute-start(bf16[512,1152]{1,0:T(8,128)(2,1)S(1)} %pad_maximum_fusion.7), channel_id=1, source_target_pairs={{0,1},{1,0},{2,3},{3,2},{4,5},{5,4},{6,7},{7,6},{8,9},{9,8},{10,11... | collective-permute-start | bytes 3538952 | tf_op jit(solution)/shard_map/ppermute | solution.py:27
  229.1 9.7 %collective-permute-start.8 = (bf16[333,512]{1,0:T(8,128)(2,1)S(1)}, bf16[333,512]{1,0:T(8,128)(2,1)S(1)}, u32[]{:S(2)}, u32[]{:S(2)}) collective-permute-start(bf16[333,512]{1,0:T(8,128)(2,1)S(1)} %get-tuple-element.101), channel_id=1, source_target_pairs={{0,2},{2,0},{1,3},{3,1},{4,6},{6,4},{5,7},{7,5},{8,10},{10,8},{9,1... | collective-permute-start | bytes 1022984 | tf_op jit(solution)/shard_map/ppermute | solution.py:31
  229.2 25.6 %collective-permute-start.9 = (bf16[576,576]{1,0:T(8,128)(2,1)}, bf16[576,576]{1,0:T(8,128)(2,1)}, u32[]{:S(2)}, u32[]{:S(2)}) collective-permute-start(bf16[576,576]{1,0:T(8,128)(2,1)} %refs_8_.1), channel_id=1, source_target_pairs={{0,2},{2,0},{1,3},{3,1},{4,6},{6,4},{5,7},{7,5},{8,10},{10,8},{9,1... | collective-permute-start | bytes 1990664 | tf_op jit(solution)/shard_map/ppermute | solution.py:31
  283.6 40.3 %copy-start.3 = (bf16[1024,1152]{1,0:T(8,128)(2,1)S(1)}, bf16[1024,1152]{1,0:T(8,128)(2,1)}, u32[]{:S(2)}) copy-start(bf16[1024,1152]{1,0:T(8,128)(2,1)} %pad_maximum_fusion.2.refs_0_.right_ref) | copy-start | bytes 7077892
  334.6 126.0 %collective-permute-start.16 = (bf16[1152,1152]{1,0:T(8,128)(2,1)}, bf16[1152,1152]{1,0:T(8,128)(2,1)}, u32[]{:S(2)}, u32[]{:S(2)}) collective-permute-start(bf16[1152,1152]{1,0:T(8,128)(2,1)} %get-tuple-element.115), channel_id=1, source_target_pairs={{0,2},{2,0},{1,3},{3,1},{4,6},{6,4},{5,7},{7,5},{8,10},{10,8},{9,1... | collective-permute-start | bytes 7962632 | tf_op jit(solution)/shard_map/ppermute | solution.py:31
  366.5 2.3 collective-permute-start.19
  366.7 98.6 %collective-permute-start.27 = (bf16[1152,1152]{1,0:T(8,128)(2,1)}, bf16[1152,1152]{1,0:T(8,128)(2,1)}, u32[]{:S(2)}, u32[]{:S(2)}) collective-permute-start(bf16[1152,1152]{1,0:T(8,128)(2,1)} %get-tuple-element.117), channel_id=1, source_target_pairs={{0,2},{2,0},{1,3},{3,1},{4,6},{6,4},{5,7},{7,5},{8,10},{10,8},{9,1... | collective-permute-start | bytes 7962632 | tf_op jit(solution)/shard_map/ppermute | solution.py:31
  371.2 87.6 %collective-permute-start.20 = (bf16[333,512]{1,0:T(8,128)(2,1)}, bf16[333,512]{1,0:T(8,128)(2,1)}, u32[]{:S(2)}, u32[]{:S(2)}) collective-permute-start(bf16[333,512]{1,0:T(8,128)(2,1)} %add_convert_fusion.1), channel_id=1, source_target_pairs={{1,2},{2,1},{5,6},{6,5},{9,10},{10,9},{13,14},{14,13},{17,18},{18,... | collective-permute-start | bytes 1022984 | tf_op jit(solution)/shard_map/ppermute | solution.py:1070
  410.0 439.5 %collective-permute-start.12 = (bf16[512,576]{0,1:T(8,128)(2,1)}, bf16[512,576]{0,1:T(8,128)(2,1)}, u32[]{:S(2)}, u32[]{:S(2)}) collective-permute-start(bf16[512,576]{0,1:T(8,128)(2,1)} %copy.103), channel_id=1, source_target_pairs={{0,2},{2,0},{1,3},{3,1},{4,6},{6,4},{5,7},{7,5},{8,10},{10,8},{9,1... | collective-permute-start | bytes 1769480 | tf_op jit(solution)/shard_map/ppermute | solution.py:31
  808.1 23.6 %copy-start.53 = (bf16[512,576]{1,0:T(8,128)(2,1)S(1)}, bf16[512,576]{1,0:T(8,128)(2,1)}, u32[]{:S(2)}) copy-start(bf16[512,576]{1,0:T(8,128)(2,1)} %copy-done.52) | copy-start | bytes 1769476
  808.1 23.6 %copy-start.55 = (bf16[512,576]{1,0:T(8,128)(2,1)S(1)}, bf16[512,576]{1,0:T(8,128)(2,1)}, u32[]{:S(2)}) copy-start(bf16[512,576]{1,0:T(8,128)(2,1)} %copy-done.54) | copy-start | bytes 1769476
  808.1 23.6 %copy-start.57 = (bf16[512,576]{1,0:T(8,128)(2,1)S(1)}, bf16[512,576]{1,0:T(8,128)(2,1)}, u32[]{:S(2)}) copy-start(bf16[512,576]{1,0:T(8,128)(2,1)} %copy-done.56) | copy-start | bytes 1769476
  808.1 23.6 %copy-start.59 = (bf16[512,576]{1,0:T(8,128)(2,1)S(1)}, bf16[512,576]{1,0:T(8,128)(2,1)}, u32[]{:S(2)}) copy-start(bf16[512,576]{1,0:T(8,128)(2,1)} %copy.125) | copy-start | bytes 1769476
  811.6 54.1 %collective-permute-start.24 = (f32[1,1152]{1,0:T(1,128)}, f32[1,1152]{1,0:T(1,128)}, u32[]{:S(2)}, u32[]{:S(2)}) collective-permute-start(f32[1,1152]{1,0:T(1,128)} %get-tuple-element.135), channel_id=1, source_target_pairs={{0,1},{1,0},{2,3},{3,2},{4,5},{5,4},{6,7},{7,6},{8,9},{9,8},{10,11... | collective-permute-start | bytes 13832 | tf_op jit(solution)/shard_map/ppermute | solution.py:27
  838.1 28.5 %collective-permute-start.22 = (f32[4,72]{1,0:T(4,128)S(1)}, f32[4,72]{1,0:T(4,128)S(1)}, u32[]{:S(2)}, u32[]{:S(2)}) collective-permute-start(f32[4,72]{1,0:T(4,128)S(1)} %maximum_bitcast_fusion), channel_id=1, source_target_pairs={{0,1},{1,0},{2,3},{3,2},{4,5},{5,4},{6,7},{7,6},{8,9},{9,8},{10,11... | collective-permute-start | bytes 3464 | tf_op jit(solution)/shard_map/ppermute | solution.py:27
  838.2 39.4 %collective-permute-start.21 = (f32[3,1152]{1,0:T(4,128)S(1)}, f32[3,1152]{1,0:T(4,128)S(1)}, u32[]{:S(2)}, u32[]{:S(2)}) collective-permute-start(f32[3,1152]{1,0:T(4,128)S(1)} %pad_maximum_fusion.10), channel_id=1, source_target_pairs={{0,1},{1,0},{2,3},{3,2},{4,5},{5,4},{6,7},{7,6},{8,9},{9,8},{10,11... | collective-permute-start | bytes 41480 | tf_op jit(solution)/shard_map/ppermute | solution.py:27
  846.8 22.2 %collective-permute-start.18 = (f32[2,1024]{1,0:T(2,128)S(1)}, f32[2,1024]{1,0:T(2,128)S(1)}, u32[]{:S(2)}, u32[]{:S(2)}) collective-permute-start(f32[2,1024]{1,0:T(2,128)S(1)} %pad_maximum_fusion.13), channel_id=1, source_target_pairs={{0,1},{1,0},{2,3},{3,2},{4,5},{5,4},{6,7},{7,6},{8,9},{9,8},{10,11... | collective-permute-start | bytes 24584 | tf_op jit(solution)/shard_map/ppermute | solution.py:27
  866.5 2.4 collective-permute-start.25
  877.9 2.6 collective-permute-start.23
  880.5 6.1 collective-permute-start.26
  880.5 7.0 collective-permute-start.28
  882.1 12.0 %collective-permute-start.29 = (f32[5472]{0:T(1024)S(1)}, f32[5472]{0:T(1024)S(1)}, u32[]{:S(2)}, u32[]{:S(2)}) collective-permute-start(f32[5472]{0:T(1024)S(1)} %concatenate.207), channel_id=1, source_target_pairs={{0,12},{4,16},{8,20},{12,24},{16,28},{20,0},{24,4},{28,8},{1,13},{... | collective-permute-start | bytes 65672 | tf_op jit(solution)/shard_map/ppermute | solution.py:1162
  883.5 15.0 %collective-permute-start.30 = (f32[5472]{0:T(1024)S(1)}, f32[5472]{0:T(1024)S(1)}, u32[]{:S(2)}, u32[]{:S(2)}) collective-permute-start(f32[5472]{0:T(1024)S(1)} %concatenate.207), channel_id=1, source_target_pairs={{0,16},{4,20},{8,24},{12,28},{16,0},{20,4},{24,8},{28,12},{1,17},{... | collective-permute-start | bytes 65672 | tf_op jit(solution)/shard_map/ppermute | solution.py:1162
  885.4 13.1 %collective-permute-start.31 = (f32[5472]{0:T(1024)S(1)}, f32[5472]{0:T(1024)S(1)}, u32[]{:S(2)}, u32[]{:S(2)}) collective-permute-start(f32[5472]{0:T(1024)S(1)} %concatenate.207), channel_id=1, source_target_pairs={{0,20},{4,24},{8,28},{12,0},{16,4},{20,8},{24,12},{28,16},{1,21},{... | collective-permute-start | bytes 65672 | tf_op jit(solution)/shard_map/ppermute | solution.py:1162
  886.6 11.9 %collective-permute-start.32 = (f32[5472]{0:T(1024)S(1)}, f32[5472]{0:T(1024)S(1)}, u32[]{:S(2)}, u32[]{:S(2)}) collective-permute-start(f32[5472]{0:T(1024)S(1)} %concatenate.207), channel_id=1, source_target_pairs={{0,24},{4,28},{8,0},{12,4},{16,8},{20,12},{24,16},{28,20},{1,25},{... | collective-permute-start | bytes 65672 | tf_op jit(solution)/shard_map/ppermute | solution.py:1162
  887.6 10.9 %collective-permute-start.33 = (f32[5472]{0:T(1024)S(1)}, f32[5472]{0:T(1024)S(1)}, u32[]{:S(2)}, u32[]{:S(2)}) collective-permute-start(f32[5472]{0:T(1024)S(1)} %concatenate.207), channel_id=1, source_target_pairs={{0,28},{4,0},{8,4},{12,8},{16,12},{20,16},{24,20},{28,24},{1,29},{... | collective-permute-start | bytes 65672 | tf_op jit(solution)/shard_map/ppermute | solution.py:1162
  894.1 10.6 %collective-permute-start.17 = (bf16[512,576]{0,1:T(8,128)(2,1)S(1)}, bf16[512,576]{0,1:T(8,128)(2,1)S(1)}, u32[]{:S(2)}, u32[]{:S(2)}) collective-permute-start(bf16[512,576]{0,1:T(8,128)(2,1)S(1)} %copy-done.88), channel_id=1, source_target_pairs={{0,1},{1,0},{2,3},{3,2},{4,5},{5,4},{6,7},{7,6},{8,9},{9,8},{10,11... | collective-permute-start | bytes 1769480 | tf_op jit(solution)/shard_map/ppermute | solution.py:27
  (109 other events, 640.9 us)
Sparse Core Ops, SparseCore 0:
  24.2 59.3 all-gather.4
  85.7 53.4 all-gather.2
  465.4 132.2 all-reduce.2

commit v3 on v2

--- a/solution.py
+++ b/solution.py
@@ -20,7 +20,34 @@
 F32 = jnp.float32
 MESH = pl.DeviceIdType.MESH
 LOG2E = 1.4426950408889634
-FREE = pl.CostEstimate(flops=0, bytes_accessed=0, transcendentals=0)
+TIMES = {
+    "attend": 15,
+    "attend_cross": 7,
+    "attend_back": 29,
+    "attend_back_cross": 16,
+    "into_self": 90,
+    "into_cross": 15,
+    "into_feed": 28,
+    "from_feed": 40,
+    "from_cross": 16,
+    "from_self": 22,
+    "grad_down": 9,
+    "grad_up": 9,
+    "grad_cross_out": 3,
+    "grad_cross_query": 3,
+    "grad_context": 3,
+    "grad_self_out": 3,
+    "grad_self": 8,
+    "grad_skip": 6,
+    "ring_sum": 200,
+}
+SHARE = 3.0
+
+
+def cost(name):
+    return pl.CostEstimate(
+        flops=0, bytes_accessed=int(TIMES[name] * 3.69e6 / SHARE), transcendentals=0
+    )
 
 
 def other_core(values):
@@ -194,7 +221,7 @@
             jax.ShapeDtypeStruct((heads, 1, tokens), F32),
         ],
         compiler_params=pltpu.CompilerParams(vmem_limit_bytes=48 * 2**20),
-        cost_estimate=FREE,
+        cost_estimate=cost("attend" if extra else "attend_cross"),
         name="attend",
     )(q, k, v, qg, kg, *extra)
 
@@ -228,7 +255,7 @@
             pltpu.VMEM((HD, tokens), F32),
         ],
         compiler_params=pltpu.CompilerParams(vmem_limit_bytes=48 * 2**20),
-        cost_estimate=FREE,
+        cost_estimate=cost("attend_back" if extra else "attend_back_cross"),
         name="attend_back",
     )(q, k, v, qg, kg, *extra, out, lse, grad)
 
@@ -310,32 +337,78 @@
     lax.fori_loop(0, half // CHUNK, one, 0)
 
 
+def skip_norm(half, lat, joint, gain, low, average_out, inverse_out, exchange, mine, theirs):
+    tokens, width = lat.shape
+    mine[...] = jnp.zeros_like(mine)
+
+    def sums(step):
+        at = rows_at(step)
+        first, second = lat[at].astype(F32), joint[at].astype(F32)
+        total = jnp.sum(first, axis=1, keepdims=True) + jnp.sum(second, axis=1, keepdims=True)
+        square = jnp.sum(first * first, axis=1, keepdims=True) + jnp.sum(
+            second * second, axis=1, keepdims=True
+        )
+        mine[at, 0:1] = total
+        mine[at, 1:2] = square
+
+    steps(sums, tokens)
+    exchange.start()
+    exchange.wait()
+    begin = lax.axis_index("col") * half
+
+    def norm(step):
+        at = rows_at(step)
+        place = pl.ds(pl.multiple_of(lax.rem(begin + step * CHUNK, tokens), CHUNK), CHUNK)
+        average = (mine[place, 0:1] + theirs[place, 0:1]) * (1.0 / (2 * D))
+        square = (mine[place, 1:2] + theirs[place, 1:2]) * (1.0 / (2 * D))
+        inverse = lax.rsqrt(square - average * average + EPSILON)
+        average_out[at] = average
+        inverse_out[at] = inverse
+        low[at, :width] = ((lat[place].astype(F32) - average) * inverse * gain[0:1]).astype(BF16)
+        low[at, width:] = ((joint[place].astype(F32) - average) * inverse * gain[1:2]).astype(BF16)
+
+    steps(norm, tokens)
+
+
 def forward_kernel(tokens_last, residual, shifted, feed, fetch, *refs):
     refs = list(refs)
     take = lambda: refs.pop(0)
-    a_ref, w1o = take(), take()
+    if fetch:
+        lat_ref, joint_ref, skip_gain = take(), take(), take()
+    else:
+        a_ref = take()
+    w1o = take()
     w1f = None if fetch else take()
     gain = take()
     res_ref = take() if residual else None
     shift = take() if shifted else None
     w2o = take()
     w2f = None if fetch else take()
+    if fetch:
+        next_own = [take(), take()]
     if feed:
         w3o, w3f = take(), take()
     state_ref, x_ref, out_ref = take(), take(), take()
+    if fetch:
+        a_ref, average_ref, inverse_ref = take(), take(), take()
+        next_far = [take(), take()]
     w1, w2, sent, got, sems, x_sems = take(), take(), take(), take(), take(), take()
     if feed:
         w3, sent_out, got_out, out_sems = take(), take(), take(), take()
     half = state_ref.shape[0]
     if fetch:
-        w1f, w2f, far_sems = take(), take(), take()
+        w1f, w2f, far_sems, mine, theirs, stat_sems = (take() for _ in range(6))
         other, across = core_pair(True)
+        owns, fars = [w1o, w2o] + next_own, [w1f, w2f] + next_far
         fetches = [
-            send(own, far, far_sems, step, across)
-            for step, (own, far) in enumerate(((w1o, w1f), (w2o, w2f)))
+            send(own, far, far_sems, step, across) for step, (own, far) in enumerate(zip(owns, fars))
         ]
         for copy in fetches:
             copy.start()
+        skip_norm(
+            half, lat_ref, joint_ref, skip_gain, a_ref, average_ref, inverse_ref,
+            send(mine, theirs, stat_sems, 0, other), mine, theirs,
+        )
         fetches[0].wait_recv()
     else:
         other = core_pair()
@@ -355,7 +428,7 @@
     if not fetch:
         join_rows(w2, w2o, w2f)
     if feed:
-        join_columns(w3, w3o, w3f)
+        join_rows(w3, w3o, w3f)
 
     def keep(step):
         at = rows_at(step)
@@ -384,7 +457,7 @@
 
         def hidden(step, base):
             pre = dot_nn(x_ref[rows_at(step, base)], w2[...])
-            return dot_nn(gelu_parts(pre)[0].astype(BF16), w3[...])
+            return dot_nt(gelu_parts(pre)[0].astype(BF16), w3[...])
 
         def give_out(step):
             at = rows_at(step)
@@ -425,6 +498,8 @@
 
     steps(drain, half)
     if fetch:
+        for copy in fetches[2:]:
+            copy.wait_recv()
         for copy in fetches:
             copy.wait_send()
 
@@ -440,7 +515,7 @@
         compiler_params=pltpu.CompilerParams(
             collective_id=collective, has_side_effects=True, vmem_limit_bytes=60 * 2**20
         ),
-        cost_estimate=FREE,
+        cost_estimate=cost(name),
         name=name,
     )(*operands)
 
@@ -449,32 +524,37 @@
     return pltpu.SemaphoreType.DMA((2, half // CHUNK))
 
 
-def forward_bridge(a, tokens_last, w1, gain, res, shift, w2, w3, collective, name):
-    tokens = a.shape[1] if tokens_last else a.shape[0]
+def forward_bridge(a, tokens_last, w1, gain, res, shift, w2, w3, collective, name, later=()):
+    fetch = len(later) > 0
+    tokens = a[0].shape[0] if fetch else a.shape[1]
     half = tokens // 2
     feed = w3 is not None
-    operands = [a, *w1, gain]
+    operands = [*(a if fetch else (a,)), *w1, gain]
     operands += [res] if res is not None else []
     operands += [shift] if shift is not None else []
-    operands += [*w2] + ([*w3] if feed else [])
+    operands += [*w2, *later] + ([*w3] if feed else [])
     depth, wide = w1[0].shape[0], w2[0].shape[1]
     out_shape = [((half, D), F32), ((tokens, D), BF16)]
     out_shape += [((half, D), BF16)] if feed else [((wide, tokens), F32)]
     part = pltpu.VMEM((half, D), F32)
     joined = [(depth, D), (D, wide)]
     scratch = [part, part, pair_sems(half), pair_sems(half)]
-    if len(w1) == 1:
+    if fetch:
+        out_shape += [((tokens, depth), BF16), ((tokens, 1), F32), ((tokens, 1), F32)]
+        out_shape += [(weight.shape, BF16) for weight in later]
         out_shape += [(shape, BF16) for shape in joined]
     else:
         scratch = [pltpu.VMEM(shape, BF16) for shape in joined] + scratch
     if feed:
-        scratch += [pltpu.VMEM((wide, D), BF16), part, part, pair_sems(half)]
-    fetch = len(w1) == 1
+        scratch += [pltpu.VMEM((D, wide), BF16), part, part, pair_sems(half)]
     if fetch:
         scratch += [
             pltpu.VMEM(w1[0].shape, BF16),
             pltpu.VMEM(w2[0].shape, BF16),
-            pltpu.SemaphoreType.DMA((2, 2)),
+            pltpu.SemaphoreType.DMA((2, 2 + len(later))),
+            pltpu.VMEM((tokens, 128), F32),
+            pltpu.VMEM((tokens, 128), F32),
+            pltpu.SemaphoreType.DMA((2, 1)),
         ]
     return whole_call(
         functools.partial(
@@ -514,14 +594,14 @@
     if not whole:
         join_rows(w2, w2o, w2f)
     if feed:
-        join_columns(w3, w3o, w3f)
+        join_rows(w3, w3o, w3f)
 
     def part(step, base):
         at = rows_at(step, base)
         if feed:
             value, slope = gelu_parts(dot_nn(feed_ref[at], w2[...]))
             hidden_ref[at] = value.astype(BF16)
-            rows = (dot_nt(cot_ref[at], w3[...]) * slope).astype(BF16)
+            rows = (dot_nn(cot_ref[at], w3[...]) * slope).astype(BF16)
             pre_ref[at] = rows
         else:
             rows = g_ref[:, at].T
@@ -602,7 +682,7 @@
     if not whole:
         scratch = [pltpu.VMEM((wide, D), BF16), pltpu.VMEM((D, depth), BF16)] + scratch
     if feed:
-        scratch += [pltpu.VMEM((depth, D), BF16)]
+        scratch += [pltpu.VMEM((D, depth), BF16)]
     return whole_call(
         functools.partial(backward_kernel, bool(feed), summed, tokens_last, whole),
         operands,
@@ -654,7 +734,7 @@
         out_specs=[out_spec, out_spec],
         out_shape=[out_shape, out_shape],
         compiler_params=pltpu.CompilerParams(vmem_limit_bytes=48 * 2**20),
-        cost_estimate=FREE,
+        cost_estimate=cost(name),
         name=name,
     )(left, right)
 
@@ -846,7 +926,7 @@
         compiler_params=pltpu.CompilerParams(
             collective_id=0, has_side_effects=True, vmem_limit_bytes=62 * 2**20
         ),
-        cost_estimate=FREE,
+        cost_estimate=cost("ring_sum"),
         name="ring_sum",
     )(*owns, *fars)
 
@@ -909,9 +989,10 @@
         piece = lax.dynamic_slice_in_dim(weight, lax.axis_index("dp") * share, share, 0)
         return other_chip(piece)
 
-    up_share, down_share = share_of(up_weight), share_of(down_weight)
+    down_turned = down_weight.T
+    up_share, down_share = share_of(up_weight), share_of(down_turned)
     up_pair = (up_weight, lax.all_gather(up_share, "dp", axis=0, tiled=True))
-    down_pair = (down_weight, lax.all_gather(down_share, "dp", axis=0, tiled=True))
+    down_pair = (down_turned, lax.all_gather(down_share, "dp", axis=0, tiled=True))
     norm_gains = jnp.concatenate([jnp.stack([self_gain, cross_gain, feed_gain]), norm_far], axis=1)
     self_gain_all, cross_gain_all, feed_gain_all = norm_gains[0:1], norm_gains[1:2], norm_gains[2:3]
 
@@ -936,23 +1017,9 @@
     skip_own, skip_other = own_first(skip_input)
     lat = jnp.concatenate([lat_own, lat_other]).astype(F32)
     joint = jnp.concatenate([skip_own, skip_other]).astype(F32)
-    sums = jnp.stack(
-        [jnp.sum(lat, axis=1) + jnp.sum(joint, axis=1), jnp.sum(lat * lat, axis=1) + jnp.sum(joint * joint, axis=1)]
-    )
 
     def swap_halves(values):
         return jnp.concatenate([values[:, half:], values[:, :half]], axis=1)
-
-    sums = sums + swap_halves(other_core(sums))
-    average = (sums[0] / (2 * D))[:, None]
-    skip_inverse = lax.rsqrt((sums[1] / (2 * D))[:, None] - average * average + EPSILON)
-    skip_low = jnp.concatenate(
-        [
-            (lat - average) * skip_inverse * skip_gain[0],
-            (joint - average) * skip_inverse * skip_gain[1],
-        ],
-        axis=1,
-    ).astype(BF16)
 
     cond_low = jax.nn.silu(condition.astype(F32)).astype(BF16)
     shift_part = contract(cond_low, shift_weight)
@@ -961,24 +1028,33 @@
     shift_far = other_chip(lax.dynamic_slice_in_dim(shift_part, 1 - chip, 1, 0))
     shift_row = jnp.concatenate([shift_mine, shift_far], axis=1)
 
-    first_state, first_all, mixed_raw, skip_whole, self_whole = forward_bridge(
-        skip_low, False, (skip_flat,), self_gain_all, None, shift_row, (self_flat,), None, 1, "into_self"
+    (
+        first_state,
+        first_all,
+        mixed_raw,
+        skip_low,
+        average,
+        skip_inverse,
+        out_far_half,
+        query_far_half,
+        skip_whole,
+        self_whole,
+    ) = forward_bridge(
+        (latents, skip_input, skip_gain), False, (skip_flat,), self_gain_all, None, shift_row, (self_flat,), None, 1, "into_self",
+        (self_out, cross_query),
     )
     mixed_raw = mixed_raw.reshape(3 * heads_here, HD, tokens)
 
-    def near_and_later(weight):
-        return (weight, other_chip(after(weight, first_all)))
-
-    out_pair = near_and_later(self_out)
-    query_pair = near_and_later(cross_query)
-    text_far = other_chip(after(jnp.where(straight, text_near, text_states), first_all))
-    context_pair = near_and_later(context_flat)
-    context_far = context_pair[1]
-    cross_pair = near_and_later(cross_out)
-    cot_far = other_chip(after(jnp.where(straight, handed, kept), context_far))
-    text_all = jnp.concatenate([text_mine, text_far], axis=1)
-    text_all = jnp.pad(text_all, ((0, -text_here % 128), (0, 0)))
-    context_all = jnp.concatenate([context_flat, context_far])
+
+    def fetched(values, gate):
+        return other_chip(after(values, gate))
+
+    out_pair = (self_out, out_far_half)
+    query_pair = (cross_query, query_far_half)
+    text_far = fetched(jnp.where(straight, text_near, text_states), first_all)
+    context_far = fetched(context_flat, text_far)
+    cross_pair = (cross_out, fetched(cross_out, text_far))
+    mixed_raw = after(mixed_raw, text_far)
     self_args = (
         (mixed_raw, mixed_raw, mixed_raw),
         (0, heads_here, 2 * heads_here),
@@ -990,10 +1066,15 @@
     )
     heads_low, log_first = attend(*self_args[0], *self_args[1:])
     heads_flat = heads_low.reshape(width, tokens)
+    cot_far = fetched(jnp.where(straight, handed, kept), heads_low)
     second_state, cross_all, probe_raw = forward_bridge(
         heads_flat, True, out_pair, cross_gain_all, first_state, None, query_pair, None, 2, "into_cross"
     )
     probe_raw = probe_raw.reshape(heads_here, HD, tokens)
+    text_far, context_far = after((text_far, context_far), cross_all)
+    text_all = jnp.concatenate([text_mine, text_far], axis=1)
+    text_all = jnp.pad(text_all, ((0, -text_here % 128), (0, 0)))
+    context_all = jnp.concatenate([context_flat, context_far])
     memory_raw = lax.dot_general(
         context_all, text_all, (((0,), (1,)), ((), ())), preferred_element_type=F32
     ).reshape(2 * heads_here, HD, -1)
@@ -1015,7 +1096,7 @@
     out_mine = out_own[:, :row_width]
     out_far = other_chip(out_own[:, row_width:])
 
-    cot_own = jnp.concatenate([cot_mine, after(cot_far, cross_all)], axis=1)
+    cot_own = jnp.concatenate([cot_mine, after(cot_far, feed_all)], axis=1)
     cot_all = pair(cot_own)
     (
         hidden_low,
@@ -1037,7 +1118,7 @@
         4,
         "from_feed",
     )
-    down_own, down_far = weight_product(hidden_low, False, cot_all, False, 768, "grad_down")
+    down_own, down_far = weight_product(hidden_low, False, cot_all, True, 1152, "grad_down")
     up_own, up_far = weight_product(grad_pre, False, feed_all, True, 1152, "grad_up")
     cross_own, cross_far = weight_product(
         cross_flat, True, branch_two_all, False, 576, "grad_cross_out"
@@ -1058,6 +1139,10 @@
     context_own, context_far = weight_product(
         memory_low, True, text_all, True, 576, "grad_context"
     )
+    early_own = jnp.concatenate([cross_own, query_own, context_own])
+    early_far = jnp.concatenate([cross_far, query_far, context_far])
+    early_here = other_chip(early_far)
+    probe_low = after(probe_low, early_far)
     text_part = lax.dot_general(
         memory_low, context_all, (((0,), (1,)), ((), ())), preferred_element_type=F32
     )[:text_here]
@@ -1068,7 +1153,6 @@
     )
     text_sum = text_sum.astype(BF16)
     text_back = lax.ppermute(text_sum, ("row", "col"), [(1, 2), (2, 1)])
-    grad_text_states = jnp.where(straight, text_sum, text_back)
 
     grad_second, branch_one_all, grad_heads, cross_gain_part = backward_bridge(
         probe_low,
@@ -1086,7 +1170,13 @@
     out_grad_own, out_grad_far = weight_product(
         heads_flat, True, branch_one_all, False, 576, "grad_self_out"
     )
-    grad_heads_in = after(grad_heads, down_far_here)
+
+    def summed(own, far):
+        return (own.astype(F32) + far.astype(F32)).astype(BF16)
+
+    down_sum = summed(down_own, after(down_far_here, grad_heads))
+    down_share = lax.psum_scatter(down_sum, "dp", scatter_dimension=0, tiled=True)
+    grad_heads_in = after(grad_heads, down_sum)
     grad_mixed, grad_self_gains = attend_back(
         *self_args[0],
         *self_args[1:],
@@ -1095,9 +1185,11 @@
         grad_heads_in.reshape(heads_here, HD, tokens),
     )
     mixed_low = grad_mixed.reshape(3 * width, tokens)
+    up_sum = summed(up_own, up_far_here)
+    mixed_in = after(mixed_low, (down_share, up_sum))
     self_own, self_far = weight_product(mixed_low, True, first_all, True, 576, "grad_self")
     _, grad_first_all, grad_skip_out, self_gain_part, shift_grad = backward_bridge(
-        mixed_low,
+        mixed_in,
         grad_second,
         None,
         (self_whole,),
@@ -1162,22 +1254,17 @@
         lax.ppermute(small, "dp", [(i, (i + k) % groups) for i in range(groups)])
         for k in range(1, groups)
     ]
-    down_sum = (down_own.astype(F32) + down_far_here.astype(F32)).astype(BF16)
-    up_far_here = after(up_far_here, down_sum)
-    high, middle, inner, last = ring_sum(
+    skip_own = after(skip_own, (grad_latents, grad_skip_input, block_out, small))
+    middle, inner, last = ring_sum(
         groups,
         [
-            (False, [up_own], [up_far_here]),
-            (
-                True,
-                [cross_own, out_grad_own, query_own, context_own],
-                [cross_far, out_grad_far, query_far, context_far],
-            ),
-            (True, [self_own], [self_far]),
+            (False, [early_own], [early_here]),
+            (True, [out_grad_own, self_own], [out_grad_far, self_far]),
             (True, [skip_own], [skip_far]),
         ],
     )
-    grad_down = lax.psum(down_sum, "dp")
+    high = lax.psum(up_sum, "dp")
+    low = lax.all_gather(down_share, "dp", axis=0, tiled=True)
 
     def unpack(block, count):
         rows = block.shape[0] // count
@@ -1186,15 +1273,20 @@
             jnp.concatenate([piece[:, :width], piece[:, width:]]).astype(F32) for piece in pieces
         ]
 
-    grad_down = jnp.concatenate(unpack(grad_down, 3))
-    grad_up = jnp.concatenate([high[:row_width], high[row_width : 2 * row_width]], axis=1)
-    grad_up = grad_up.astype(F32)
+
+    def side_by_side(blocks):
+        return jnp.concatenate([blocks[:row_width], blocks[row_width:]], axis=1).astype(F32)
+
+    grad_down = side_by_side(low).T
+    grad_up = side_by_side(high)
     place = width // 2
-    grad_cross_out, grad_self_out, grad_cross_query = unpack(middle[: 3 * place], 3)
-    grad_context = unpack(middle[3 * place : 3 * place + text_width], 2)
-    grad_context = jnp.concatenate([grad_context[0], grad_context[1]], axis=1)
-    grad_self_weight = jnp.stack(unpack(inner[: 3 * place], 3), axis=1)
+    grad_cross_out, grad_cross_query = unpack(middle[: 2 * place], 2)
+    grad_context = jnp.concatenate(unpack(middle[2 * place : 2 * place + text_width], 2), axis=1)
+    (grad_self_out,) = unpack(inner[:place], 1)
+    grad_self_weight = jnp.stack(unpack(inner[place : 4 * place], 3), axis=1)
     grad_skip_weight = jnp.concatenate(unpack(last[: 2 * place], 3))
+
+    grad_text_states = jnp.where(straight, text_sum, after(text_back, last))
 
     smalls = [after(value, last) for value in smalls[1:]] + smalls[:1]
     gain_count = kept_gains.shape[0]

time: 933 us -> 839 us (0.90)
  waiting for transfers between devices: 101 us -> 47.8 us
  local copies, waits for them, and re-layouts: 101 us -> 78.4 us
  Pallas kernels: 590 us -> 575 us
    ppermute x1, waiting for transfers between devices: 48.1 us -> 0.01 us  [shards(): text_back = lax.ppermute(text_sum, ('row', 'col'), [(1, 2), (2, 1)])]
    pallas_call x1, Pallas kernels: 263 us -> 224 us  [ring_sum(): pl.pallas_call(functools.partial(ring_kernel, size, plan), in_specs=[vmem...]
    unnamed x262 -> x187, local copies, waits for them, and re-layouts: 62.9 us -> 36.3 us
    pallas_call x6, Pallas kernels: 221 us -> 244 us  [whole_call(): pl.pallas_call(kernel, in_specs=[vmem] * len(operands), out_specs=[vmem]...]
    ppermute x11 -> x10, starting transfers between devices: 28.2 us -> 9.72 us  [other_core(): return lax.ppermute(values, 'col', SWAP)]
    ppermute x15 -> x14, waiting for transfers between devices: 52.2 us -> 37.4 us  [other_chip(): return lax.ppermute(values, 'row', SWAP)]
    ppermute x1, starting transfers between devices: 3.53 us -> 14 us  [shards(): text_back = lax.ppermute(text_sum, ('row', 'col'), [(1, 2), (2, 1)])]
  transfers between devices with their start and end apart: 37 -> 37, of which waited for: 11 -> 9; matrix products, arithmetic and copies ran while one was open for 13% -> 14% of each run, Pallas kernels for 55% -> 64%
where the time goes in v3:
time: 839 us; the launch traced here: 829 us
  Pallas kernels  575 us (69%)
  local copies, waits for them, and re-layouts  78.4 us (9%)
  other arithmetic  57.9 us (7%)
  waiting for transfers between devices  47.8 us (6%)
  starting transfers between devices  44.5 us (5%)
  between operations  15.6 us (2%)
  matrix products  9.6 us (1%)
    pallas_call x6, Pallas kernels, whole_call(): pl.pallas_call(kernel, in_specs=[vmem] * len(operands), out_specs=[vmem]...  244 us
    pallas_call x1, Pallas kernels, ring_sum(): pl.pallas_call(functools.partial(ring_kernel, size, plan), in_specs=[vmem...  224 us
    pallas_call x2, Pallas kernels, attend_back(): pl.pallas_call(functools.partial(attend_back_kernel, bool(extra), valid),...  44.3 us
    pallas_call x8, Pallas kernels, weight_product(): pl.pallas_call(functools.partial(product_kernel, by_rows, left_last), gri...  40.6 us
    ppermute x14, waiting for transfers between devices, other_chip(): return lax.ppermute(values, 'row', SWAP)  37.4 us
    unnamed x187, local copies, waits for them, and re-layouts  36.3 us
    pallas_call x2, Pallas kernels, attend(): pl.pallas_call(functools.partial(attend_kernel, bool(extra), valid), grid...  22.4 us
  transfers between devices with their start and end apart: 37, of which 9 were waited for; matrix products, arithmetic and copies ran while one was open for 14% of the time, Pallas kernels for 64%

profile of v3, /device:TPU:1, one launch (start us, length us, event | category | flops | bytes accessed | tf_op | source)
XLA Modules:
  0.0 828.9 jit_solution(2097216593590106245)
XLA Ops:
  8.4 2.1 collective-permute-start.7
  10.6 7.6 collective-permute-done.7
  20.5 7.0 collective-permute-done.8
  28.5 2.1 collective-permute-start.1
  36.9 2.9 copy.87
  39.8 2.8 copy.90.refs_6_
  43.9 121.3 %into_self.1 = (f32[512,1152]{1,0:T(8,128)}, bf16[1024,1152]{1,0:T(8,128)(2,1)}, f32[1728,1024]{1,0:T(8,128)}, bf16[1024,1152]{1,0:T(8,128)(2,1)}, f32[1024,1]{1...) custom-call(bf16[1024,576]{1,0:T(8,128)(2,1)} %copy.88.refs_0_, ...), custom_call_target="tpu_custom_call" | custom-call | bytes 110700000 | tf_op jit(solution)/shard_map/into_self/pallas_call | solution.py:509
  170.5 5.4 collective-permute-done.4
  181.1 15.5 %attend.2 = (bf16[8,72,1024]{2,1,0:T(8,128)(2,1)S(1)}, f32[8,1,1024]{2,1,0:T(1,128)S(1)}) custom-call(f32[24,72,1024]{2,1,0:T(8,128)} %bitcast.76, f32[24,72,1024]{2,1,0:T(8,128)} %bitcast.77, f32[24,72,1024]{2,1,0:T(8,128)} %bitcast.78, f32[72,1]{1,0:T(8,128)S(1)} %copy.91.qg_ref, f32[72,1]{1,0:T(8,128)S(1)} %copy.92.kg_ref, ...), custom_call_target="tpu_custom_call" | custom-call | bytes 18450000 | tf_op jit(solution)/shard_map/attend/pallas_call | solution.py:210
  200.7 16.9 %into_cross.1 = (f32[512,1152]{1,0:T(8,128)}, bf16[1024,1152]{1,0:T(8,128)(2,1)}, f32[576,1024]{1,0:T(8,128)}) custom-call(bf16[576,1024]{1,0:T(8,128)(2,1)} %bitcast.64, bf16[576,576]{1,0:T(8,128)(2,1)} %refs_6_.1, bf16[576,576]{1,0:T(8,128)(2,1)} %get-tuple-element.107.refs_2_.refs_7_, f32[1,1152]{1,0:T(1,128)} %get-tuple-element.311.refs_3_.refs_5_, ...), custom_call_target="tpu_custom_call" | custom-call | bytes 18450000 | tf_op jit(solution)/shard_map/into_cross/pallas_call | solution.py:509
  217.6 3.2 fusion.5
  220.9 6.9 attend.3
  228.9 28.8 %into_feed.1 = (f32[512,1152]{1,0:T(8,128)}, bf16[1024,1152]{1,0:T(8,128)(2,1)}, bf16[512,1152]{1,0:T(8,128)(2,1)}) custom-call(bf16[576,1024]{1,0:T(8,128)(2,1)} %bitcast.66, bf16[576,576]{1,0:T(8,128)(2,1)} %refs_8_.3, bf16[576,576]{1,0:T(8,128)(2,1)} %collective-permute-done.6.refs_2_.refs_9_, f32[1,1152]{1,0:T(1,128)} %get-tuple-element.310.refs_3_.refs_7_, ...), custom_call_target="tpu_custom_call" | custom-call | bytes 34440000 | tf_op jit(solution)/shard_map/into_feed/pallas_call | solution.py:509
  260.0 2.5 collective-permute-done.12
  264.1 39.1 %from_feed.1 = (bf16[1024,2304]{1,0:T(8,128)(2,1)}, bf16[1024,2304]{1,0:T(8,128)(2,1)}, f32[512,1152]{1,0:T(8,128)}, bf16[1024,1152]{1,0:T(8,128)(2,1)}, bf16[576,1024]{1,0:T(8,128)(2,1)}, /*index=5*/f32[1,1152]{1,0:T(1,128)}) custom-call(bf16[1024,1152]{1,0:T(8,128)(2,1)} %pad_maximum_fusion.2.refs_0_.right_ref, ...), custom_call_target="tpu_custom_call" | custom-call | bytes 49200000 | tf_op jit(solution)/shard_map/from_feed/pallas_call | solution.py:509
  303.2 9.4 %grad_down.1 = (bf16[1152,1152]{1,0:T(8,128)(2,1)S(1)}, bf16[1152,1152]{1,0:T(8,128)(2,1)}) custom-call(bf16[1024,2304]{1,0:T(8,128)(2,1)} %get-tuple-element.126.left_ref, bf16[1024,1152]{1,0:T(8,128)(2,1)S(1)} %copy-done.3), custom_call_target="tpu_custom_call" | custom-call | bytes 11070000 | tf_op jit(solution)/shard_map/grad_down/pallas_call | solution.py:730
  316.3 9.9 %grad_up.1 = (bf16[1152,1152]{1,0:T(8,128)(2,1)S(1)}, bf16[1152,1152]{1,0:T(8,128)(2,1)}) custom-call(bf16[1024,2304]{1,0:T(8,128)(2,1)} %get-tuple-element.128.left_ref, bf16[1024,1152]{1,0:T(8,128)(2,1)S(1)} %copy-done.8), custom_call_target="tpu_custom_call" | custom-call | bytes 11070000 | tf_op jit(solution)/shard_map/grad_up/pallas_call | solution.py:730
  327.7 15.5 %attend_back.2 = (bf16[8,72,1024]{2,1,0:T(8,128)(2,1)S(1)}, bf16[2,8,72,384]{3,2,1,0:T(8,128)(2,1)S(1)}, f32[8,2,72,1]{3,2,1,0:T(8,128)S(1)}) custom-call(f32[8,72,1024]{2,1,0:T(8,128)} %bitcast.68, f32[16,72,384]{2,1,0:T(8,128)} %bitcast.62, f32[16,72,384]{2,1,0:T(8,128)} %bitcast.63, f32[72,1]{1,0:T(8,128)S(1)} %copy.93.qg_ref, f32[72,1]{1,0:T(8,128)S(1)} %copy.94.kg_ref, ...), custom_call_target="tpu_custom_call" | custom-call | bytes 19680000 | tf_op jit(solution)/shard_map/attend_back/pallas_call | solution.py:244
  343.3 2.0 grad_cross_query.1
  345.3 2.3 grad_context.1
  350.1 16.2 %from_cross.1 = (f32[512,1152]{1,0:T(8,128)}, bf16[1024,1152]{1,0:T(8,128)(2,1)}, bf16[576,1024]{1,0:T(8,128)(2,1)}, f32[1,1152]{1,0:T(1,128)}) custom-call(bf16[576,1024]{1,0:T(8,128)(2,1)} %bitcast.71, f32[512,1152]{1,0:T(8,128)} %get-tuple-element.138.refs_1_, bf16[576,576]{1,0:T(8,128)(2,1)} %refs_2_.3, ...), custom_call_target="tpu_custom_call" | custom-call | bytes 19680000 | tf_op jit(solution)/shard_map/from_cross/pallas_call | solution.py:509
  366.3 7.2 collective-permute-done.13
  373.5 3.9 add_convert_fusion.1
  379.6 2.9 constant_dynamic-slice_fusion.1
  389.2 3.0 fusion.4
  399.0 28.8 %attend_back.3 = (bf16[3,8,72,1024]{3,2,1,0:T(8,128)(2,1)}, f32[8,2,72,1]{3,2,1,0:T(8,128)S(1)}) custom-call(f32[24,72,1024]{2,1,0:T(8,128)} %bitcast.79, f32[24,72,1024]{2,1,0:T(8,128)} %bitcast.80, f32[24,72,1024]{2,1,0:T(8,128)} %bitcast.81, f32[72,1]{1,0:T(8,128)S(1)} %copy-done.36, f32[72,1]{1,0:T(8,128)S(1)} %copy-done.38, ...), custom_call_target="tpu_custom_call" | custom-call | bytes 35670000 | tf_op jit(solution)/shard_map/attend_back/pallas_call | solution.py:244
  427.9 8.5 %collective-permute-done.14 = bf16[1152,1152]{1,0:T(8,128)(2,1)} collective-permute-done((bf16[1152,1152]{1,0:T(8,128)(2,1)}, bf16[1152,1152]{1,0:T(8,128)(2,1)}, u32[]{:S(2)}, u32[]{:S(2)}) %collective-permute-start.14) | collective-permute-done | bytes 2654240 | tf_op jit(solution)/shard_map/ppermute | solution.py:58
  436.4 4.0 add_convert_fusion
  440.4 7.0 reduce-scatter.2.cloned.1.call-done
  451.3 2.4 add_convert_fusion.2
  453.7 8.1 grad_self.1
  464.5 21.8 %from_self.1 = (f32[512,1152]{1,0:T(8,128)}, bf16[1024,1152]{1,0:T(8,128)(2,1)}, f32[1024,1152]{1,0:T(8,128)}, f32[1,1152]{1,0:T(1,128)}, f32[1,1152]{1,0:T(1,128)}) custom-call(bf16[1728,1024]{1,0:T(8,128)(2,1)} %bitcast.83, f32[512,1152]{1,0:T(8,128)} %get-tuple-element.146.refs_1_, bf16[1152,1728]{1,0:T(8,128)(2,1)} %get-tuple-element.147.refs_2_, ...), custom_call_target="tpu_custom_call" | custom-call | bytes 27060000 | tf_op jit(solution)/shard_map/from_self/pallas_call | solution.py:509
  486.6 6.1 multiply_reduce_fusion.1
  493.5 2.3 copy.105
  497.1 2.5 broadcast_select_fusion.1
  499.6 2.1 copy.107
  502.5 5.6 grad_skip.1
  510.4 5.6 multiply_convert_fusion
  521.8 2.1 collective-permute-start.30
  523.9 2.5 maximum_select_fusion.1
  535.4 223.7 %ring_sum.1 = (bf16[1280,1152]{1,0:T(8,128)(2,1)}, bf16[1280,1152]{1,0:T(8,128)(2,1)}, bf16[768,1152]{1,0:T(8,128)(2,1)}) custom-call(bf16[1088,1152]{1,0:T(8,128)(2,1)} %pad_maximum_fusion.refs_0_, bf16[288,1152]{1,0:T(8,128)(2,1)} %copy-done.27, bf16[864,1152]{1,0:T(8,128)(2,1)} %copy-done.19, bf16[576,1152]{1,0:T(8,128)(2,1)} %copy-done.21, ...), custom_call_target="tpu_custom_call" | custom-call | bytes 246000000 | tf_op jit(solution)/shard_map/ring_sum/pallas_call | solution.py:918
  759.1 14.0 %collective-permute-start.18 = (bf16[333,512]{1,0:T(8,128)(2,1)S(1)}, bf16[333,512]{1,0:T(8,128)(2,1)S(1)}, u32[]{:S(2)}, u32[]{:S(2)}) collective-permute-start(bf16[333,512]{1,0:T(8,128)(2,1)S(1)} %copy-done.55), channel_id=1, source_target_pairs={{1,2},{2,1},{5,6},{6,5},{9,10},{10,9},{13,14},{14,13},{17,18},{18,... | collective-permute-start | bytes 1022984 | tf_op jit(solution)/shard_map/ppermute | solution.py:1155
  786.1 2.0 copy.117
  796.7 3.3 convert.5
  807.1 2.5 fusion.38
  809.5 3.0 maximum_convert_fusion.1
  814.5 2.8 maximum_convert_fusion
  819.2 2.8 convert_bitcast_fusion
  (368 shorter events, 113.5 us)
Async XLA Ops:
  7.2 23.4 %copy-start.79 = (f32[576]{0:T(1024)S(1)}, f32[576]{0:T(1024)}, u32[]{:S(2)}) copy-start(f32[576]{0:T(1024)} %param.32) | copy-start | bytes 6916
  7.2 23.4 %copy-start.80 = (f32[576]{0:T(1024)S(1)}, f32[576]{0:T(1024)}, u32[]{:S(2)}) copy-start(f32[576]{0:T(1024)} %param.37) | copy-start | bytes 6916
  7.2 23.4 %copy-start.81 = (f32[576]{0:T(1024)S(1)}, f32[576]{0:T(1024)}, u32[]{:S(2)}) copy-start(f32[576]{0:T(1024)} %param.43) | copy-start | bytes 6916
  7.2 26.8 %copy-start.56 = (bf16[1024,576]{0,1:T(8,128)(2,1)S(1)}, bf16[1024,576]{0,1:T(8,128)(2,1)}, u32[]{:S(2)}) copy-start(bf16[1024,576]{0,1:T(8,128)(2,1)} %param.23) | copy-start | bytes 3538948
  7.2 221.6 %all-gather.4.cloned.1.call-start = ((), (), s32[]{:S(2)}) async-start(), calls=%async_computation.1 | async-start | bytes 2985984 | tf_op jit(solution)/shard_map/all_gather | solution.py:994
  8.4 27.0 %copy-start.57 = (bf16[1024,576]{0,1:T(8,128)(2,1)S(1)}, bf16[1024,576]{0,1:T(8,128)(2,1)}, u32[]{:S(2)}) copy-start(bf16[1024,576]{0,1:T(8,128)(2,1)} %param.24) | copy-start | bytes 3538948
  8.4 9.8 %collective-permute-start.7 = (bf16[72,2304]{1,0:T(8,128)(2,1)S(1)}, bf16[72,2304]{1,0:T(8,128)(2,1)}, u32[]{:S(2)}, u32[]{:S(2)}) collective-permute-start(bf16[72,2304]{1,0:T(8,128)(2,1)S(1)} %constant_dynamic-slice_fusion.6), channel_id=1, source_target_pairs={{0,2},{2,0},{1,3},{3,1},{4,6},{6,4},{5,7},{7,5},{8,10},{10,8},{9,1... | collective-permute-start | bytes 995336 | tf_op jit(solution)/shard_map/ppermute | solution.py:58
  18.2 210.6 %all-gather.6.cloned.1.call-start = ((), (), s32[]{:S(2)}) async-start(), calls=%async_computation.2 | async-start | bytes 2985984 | tf_op jit(solution)/shard_map/all_gather | solution.py:995
  19.3 8.2 collective-permute-start.8
  27.5 419.9 %reduce-scatter.2.cloned.1.call-start = ((), (), s32[]{:S(2)}) async-start(), calls=%async_computation.3 | async-start | bytes 2985984 | tf_op jit(solution)/shard_map/reduce_scatter | solution.py:1178
  28.5 3.0 collective-permute-start.1
  31.5 11.1 %collective-permute-start.2 = (f32[1,576]{1,0:T(1,128)S(1)}, f32[1,576]{1,0:T(1,128)S(1)}, u32[]{:S(2)}, u32[]{:S(2)}) collective-permute-start(f32[1,576]{1,0:T(1,128)S(1)} %get-tuple-element.330), channel_id=1, source_target_pairs={{0,2},{2,0},{1,3},{3,1},{4,6},{6,4},{5,7},{7,5},{8,10},{10,8},{9,1... | collective-permute-start | bytes 6920 | tf_op jit(solution)/shard_map/ppermute | solution.py:58
  32.7 10.5 %collective-permute-start = (f32[3,576]{1,0:T(4,128)S(1)}, f32[3,576]{1,0:T(4,128)S(1)}, u32[]{:S(2)}, u32[]{:S(2)}) collective-permute-start(f32[3,576]{1,0:T(4,128)S(1)} %pad_maximum_fusion.11), channel_id=1, source_target_pairs={{0,2},{2,0},{1,3},{3,1},{4,6},{6,4},{5,7},{7,5},{8,10},{10,8},{9,1... | collective-permute-start | bytes 20744 | tf_op jit(solution)/shard_map/ppermute | solution.py:58
  33.1 132.2 %collective-permute-start.3 = (bf16[333,512]{1,0:T(8,128)(2,1)}, bf16[333,512]{1,0:T(8,128)(2,1)}, u32[]{:S(2)}, u32[]{:S(2)}) collective-permute-start(bf16[333,512]{1,0:T(8,128)(2,1)} %param.26), channel_id=1, source_target_pairs={{0,1},{1,0},{2,3},{3,2},{4,5},{5,4},{6,7},{7,6},{8,9},{9,8},{10,11... | collective-permute-start | bytes 1022984 | tf_op jit(solution)/shard_map/ppermute | solution.py:54
  43.9 124.4 %copy-start.58 = (bf16[1024,576]{0,1:T(8,128)(2,1)S(1)}, bf16[1024,576]{0,1:T(8,128)(2,1)}, u32[]{:S(2)}) copy-start(bf16[1024,576]{0,1:T(8,128)(2,1)} %param.28) | copy-start | bytes 3538948
  167.1 8.8 %collective-permute-start.4 = (bf16[333,512]{1,0:T(8,128)(2,1)S(1)}, bf16[333,512]{1,0:T(8,128)(2,1)S(1)}, u32[]{:S(2)}, u32[]{:S(2)}) collective-permute-start(bf16[333,512]{1,0:T(8,128)(2,1)S(1)} %get-tuple-element.104), channel_id=1, source_target_pairs={{0,2},{2,0},{1,3},{3,1},{4,6},{6,4},{5,7},{7,5},{8,10},{10,8},{9,1... | collective-permute-start | bytes 1022984 | tf_op jit(solution)/shard_map/ppermute | solution.py:58
  169.2 9.2 %collective-permute-start.10 = (bf16[512,576]{0,1:T(8,128)(2,1)}, bf16[512,576]{0,1:T(8,128)(2,1)}, u32[]{:S(2)}, u32[]{:S(2)}) collective-permute-start(bf16[512,576]{0,1:T(8,128)(2,1)} %get-tuple-element.291), channel_id=1, source_target_pairs={{0,1},{1,0},{2,3},{3,2},{4,5},{5,4},{6,7},{7,6},{8,9},{9,8},{10,11... | collective-permute-start | bytes 1769480 | tf_op jit(solution)/shard_map/ppermute | solution.py:54
  175.9 41.6 %collective-permute-start.5 = (bf16[512,1152]{0,1:T(8,128)(2,1)}, bf16[512,1152]{0,1:T(8,128)(2,1)}, u32[]{:S(2)}, u32[]{:S(2)}) collective-permute-start(bf16[512,1152]{0,1:T(8,128)(2,1)} %bitcast.103), channel_id=1, source_target_pairs={{0,2},{2,0},{1,3},{3,1},{4,6},{6,4},{5,7},{7,5},{8,10},{10,8},{9,1... | collective-permute-start | bytes 3538952 | tf_op jit(solution)/shard_map/ppermute | solution.py:58
  179.8 49.1 %collective-permute-start.6 = (bf16[576,576]{1,0:T(8,128)(2,1)S(1)}, bf16[576,576]{1,0:T(8,128)(2,1)}, u32[]{:S(2)}, u32[]{:S(2)}) collective-permute-start(bf16[576,576]{1,0:T(8,128)(2,1)S(1)} %copy-done.49), channel_id=1, source_target_pairs={{0,2},{2,0},{1,3},{3,1},{4,6},{6,4},{5,7},{7,5},{8,10},{10,8},{9,1... | collective-permute-start | bytes 1990664 | tf_op jit(solution)/shard_map/ppermute | solution.py:58
  199.3 58.4 %collective-permute-start.11 = (bf16[512,576]{0,1:T(8,128)(2,1)}, bf16[512,576]{0,1:T(8,128)(2,1)}, u32[]{:S(2)}, u32[]{:S(2)}) collective-permute-start(bf16[512,576]{0,1:T(8,128)(2,1)} %copy.99), channel_id=1, source_target_pairs={{0,2},{2,0},{1,3},{3,1},{4,6},{6,4},{5,7},{7,5},{8,10},{10,8},{9,1... | collective-permute-start | bytes 1769480 | tf_op jit(solution)/shard_map/ppermute | solution.py:58
  228.9 30.2 %copy-start.52 = (bf16[512,576]{1,0:T(8,128)(2,1)S(1)}, bf16[512,576]{1,0:T(8,128)(2,1)}, u32[]{:S(2)}) copy-start(bf16[512,576]{1,0:T(8,128)(2,1)} %get-tuple-element.288) | copy-start | bytes 1769476
  259.4 3.0 collective-permute-start.12
  264.1 39.1 %copy-start.3 = (bf16[1024,1152]{1,0:T(8,128)(2,1)S(1)}, bf16[1024,1152]{1,0:T(8,128)(2,1)}, u32[]{:S(2)}) copy-start(bf16[1024,1152]{1,0:T(8,128)(2,1)} %pad_maximum_fusion.2.refs_0_.right_ref) | copy-start | bytes 7077892
  314.2 59.3 %collective-permute-start.13 = (bf16[1152,1152]{1,0:T(8,128)(2,1)}, bf16[1152,1152]{1,0:T(8,128)(2,1)}, u32[]{:S(2)}, u32[]{:S(2)}) collective-permute-start(bf16[1152,1152]{1,0:T(8,128)(2,1)} %get-tuple-element.127), channel_id=1, source_target_pairs={{0,2},{2,0},{1,3},{3,1},{4,6},{6,4},{5,7},{7,5},{8,10},{10,8},{9,1... | collective-permute-start | bytes 7962632 | tf_op jit(solution)/shard_map/ppermute | solution.py:58
  377.4 435.1 %all-reduce.3.cloned.1.call-start = ((), (), s32[]{:S(2)}) async-start(), calls=%async_computation.4 | async-start | bytes 5308416 | tf_op jit(solution)/shard_map/psum | solution.py:1266
  377.9 58.5 %collective-permute-start.14 = (bf16[1152,1152]{1,0:T(8,128)(2,1)}, bf16[1152,1152]{1,0:T(8,128)(2,1)}, u32[]{:S(2)}, u32[]{:S(2)}) collective-permute-start(bf16[1152,1152]{1,0:T(8,128)(2,1)} %get-tuple-element.129), channel_id=1, source_target_pairs={{0,2},{2,0},{1,3},{3,1},{4,6},{6,4},{5,7},{7,5},{8,10},{10,8},{9,1... | collective-permute-start | bytes 7962632 | tf_op jit(solution)/shard_map/ppermute | solution.py:58
  387.7 98.7 %collective-permute-start.9 = (bf16[512,576]{0,1:T(8,128)(2,1)}, bf16[512,576]{0,1:T(8,128)(2,1)}, u32[]{:S(2)}, u32[]{:S(2)}) collective-permute-start(bf16[512,576]{0,1:T(8,128)(2,1)} %copy.95), channel_id=1, source_target_pairs={{0,2},{2,0},{1,3},{3,1},{4,6},{6,4},{5,7},{7,5},{8,10},{10,8},{9,1... | collective-permute-start | bytes 1769480 | tf_op jit(solution)/shard_map/ppermute | solution.py:58
  388.9 143.3 %collective-permute-start.24 = (bf16[1088,1152]{1,0:T(8,128)(2,1)}, bf16[1088,1152]{1,0:T(8,128)(2,1)}, u32[]{:S(2)}, u32[]{:S(2)}) collective-permute-start(bf16[1088,1152]{1,0:T(8,128)(2,1)} %copy-done.64), channel_id=1, source_target_pairs={{0,2},{2,0},{1,3},{3,1},{4,6},{6,4},{5,7},{7,5},{8,10},{10,8},{9,1... | collective-permute-start | bytes 7520264 | tf_op jit(solution)/shard_map/ppermute | solution.py:58
  393.2 58.1 %collective-permute-start.17 = (f32[333,512]{1,0:T(8,128)}, f32[333,512]{1,0:T(8,128)}, u32[]{:S(2)}, u32[]{:S(2)}) collective-permute-start(f32[333,512]{1,0:T(8,128)} %slice_select_fusion), channel_id=1, source_target_pairs={{0,1},{1,0},{2,3},{3,2},{4,5},{5,4},{6,7},{7,6},{8,9},{9,8},{10,11... | collective-permute-start | bytes 2045960 | tf_op jit(solution)/shard_map/ppermute | solution.py:54
  397.5 30.4 %copy-start.27 = (bf16[288,1152]{1,0:T(8,128)(2,1)}, bf16[288,1152]{1,0:T(8,128)(2,1)S(1)}, u32[]{:S(2)}) copy-start(bf16[288,1152]{1,0:T(8,128)(2,1)S(1)} %get-tuple-element.157.refs_1_) | copy-start | bytes 1990660
  399.0 37.3 %copy-start.12 = (bf16[1152,1152]{1,0:T(8,128)(2,1)S(1)}, bf16[1152,1152]{1,0:T(8,128)(2,1)}, u32[]{:S(2)}) copy-start(bf16[1152,1152]{1,0:T(8,128)(2,1)} %copy-done.11) | copy-start | bytes 7962628
  447.4 369.8 %all-gather.8.cloned.1.call-start = ((), (), s32[]{:S(2)}) async-start(), calls=%async_computation.5 | async-start | bytes 2985984 | tf_op jit(solution)/shard_map/all_gather | solution.py:1267
  449.5 14.9 %collective-permute-start.20 = (f32[4,72]{1,0:T(4,128)S(1)}, f32[4,72]{1,0:T(4,128)S(1)}, u32[]{:S(2)}, u32[]{:S(2)}) collective-permute-start(f32[4,72]{1,0:T(4,128)S(1)} %maximum_bitcast_fusion), channel_id=1, source_target_pairs={{0,1},{1,0},{2,3},{3,2},{4,5},{5,4},{6,7},{7,6},{8,9},{9,8},{10,11... | collective-permute-start | bytes 3464 | tf_op jit(solution)/shard_map/ppermute | solution.py:54
  486.4 9.4 %collective-permute-start.22 = (f32[1,1152]{1,0:T(1,128)}, f32[1,1152]{1,0:T(1,128)S(1)}, u32[]{:S(2)}, u32[]{:S(2)}) collective-permute-start(f32[1,1152]{1,0:T(1,128)} %get-tuple-element.167), channel_id=1, source_target_pairs={{0,1},{1,0},{2,3},{3,2},{4,5},{5,4},{6,7},{7,6},{8,9},{9,8},{10,11... | collective-permute-start | bytes 13832 | tf_op jit(solution)/shard_map/ppermute | solution.py:54
  492.9 17.5 %collective-permute-start.16 = (f32[2,1024]{1,0:T(2,128)S(1)}, f32[2,1024]{1,0:T(2,128)S(1)}, u32[]{:S(2)}, u32[]{:S(2)}) collective-permute-start(f32[2,1024]{1,0:T(2,128)S(1)} %pad_maximum_fusion.12), channel_id=1, source_target_pairs={{0,1},{1,0},{2,3},{3,2},{4,5},{5,4},{6,7},{7,6},{8,9},{9,8},{10,11... | collective-permute-start | bytes 24584 | tf_op jit(solution)/shard_map/ppermute | solution.py:54
  493.4 23.1 %collective-permute-start.19 = (f32[3,1152]{1,0:T(4,128)S(1)}, f32[3,1152]{1,0:T(4,128)S(1)}, u32[]{:S(2)}, u32[]{:S(2)}) collective-permute-start(f32[3,1152]{1,0:T(4,128)S(1)} %pad_maximum_fusion.10), channel_id=1, source_target_pairs={{0,1},{1,0},{2,3},{3,2},{4,5},{5,4},{6,7},{7,6},{8,9},{9,8},{10,11... | collective-permute-start | bytes 41480 | tf_op jit(solution)/shard_map/ppermute | solution.py:54
  495.9 14.4 %collective-permute-start.23 = (f32[1,576]{1,0:T(1,128)S(1)}, f32[1,576]{1,0:T(1,128)S(1)}, u32[]{:S(2)}, u32[]{:S(2)}) collective-permute-start(f32[1,576]{1,0:T(1,128)S(1)} %get-tuple-element.332), channel_id=1, source_target_pairs={{0,2},{2,0},{1,3},{3,1},{4,6},{6,4},{5,7},{7,5},{8,10},{10,8},{9,1... | collective-permute-start | bytes 6920 | tf_op jit(solution)/shard_map/ppermute | solution.py:58
  501.7 27.5 %collective-permute-start.15 = (bf16[512,576]{0,1:T(8,128)(2,1)}, bf16[512,576]{0,1:T(8,128)(2,1)}, u32[]{:S(2)}, u32[]{:S(2)}) collective-permute-start(bf16[512,576]{0,1:T(8,128)(2,1)} %copy.107), channel_id=1, source_target_pairs={{0,1},{1,0},{2,3},{3,2},{4,5},{5,4},{6,7},{7,6},{8,9},{9,8},{10,11... | collective-permute-start | bytes 1769480 | tf_op jit(solution)/shard_map/ppermute | solution.py:54
  516.8 3.0 collective-permute-start.21
  520.5 12.5 %collective-permute-start.31 = (f32[5472]{0:T(1024)}, f32[5472]{0:T(1024)S(1)}, u32[]{:S(2)}, u32[]{:S(2)}) collective-permute-start(f32[5472]{0:T(1024)} %concatenate.199), channel_id=1, source_target_pairs={{0,28},{4,0},{8,4},{12,8},{16,12},{20,16},{24,20},{28,24},{1,29},{... | collective-permute-start | bytes 65672 | tf_op jit(solution)/shard_map/ppermute | solution.py:1254
  521.8 12.9 %collective-permute-start.30 = (f32[5472]{0:T(1024)}, f32[5472]{0:T(1024)}, u32[]{:S(2)}, u32[]{:S(2)}) collective-permute-start(f32[5472]{0:T(1024)} %concatenate.199), channel_id=1, source_target_pairs={{0,24},{4,28},{8,0},{12,4},{16,8},{20,12},{24,16},{28,20},{1,25},{... | collective-permute-start | bytes 65672 | tf_op jit(solution)/shard_map/ppermute | solution.py:1254
  529.2 229.8 %collective-permute-start.29 = (f32[5472]{0:T(1024)}, f32[5472]{0:T(1024)}, u32[]{:S(2)}, u32[]{:S(2)}) collective-permute-start(f32[5472]{0:T(1024)} %concatenate.199), channel_id=1, source_target_pairs={{0,20},{4,24},{8,28},{12,0},{16,4},{20,8},{24,12},{28,16},{1,21},{... | collective-permute-start | bytes 65672 | tf_op jit(solution)/shard_map/ppermute | solution.py:1254
  529.2 243.8 %collective-permute-start.28 = (f32[5472]{0:T(1024)}, f32[5472]{0:T(1024)}, u32[]{:S(2)}, u32[]{:S(2)}) collective-permute-start(f32[5472]{0:T(1024)} %concatenate.199), channel_id=1, source_target_pairs={{0,16},{4,20},{8,24},{12,28},{16,0},{20,4},{24,8},{28,12},{1,17},{... | collective-permute-start | bytes 65672 | tf_op jit(solution)/shard_map/ppermute | solution.py:1254
  532.2 240.8 %collective-permute-start.27 = (f32[5472]{0:T(1024)}, f32[5472]{0:T(1024)}, u32[]{:S(2)}, u32[]{:S(2)}) collective-permute-start(f32[5472]{0:T(1024)} %concatenate.199), channel_id=1, source_target_pairs={{0,12},{4,16},{8,20},{12,24},{16,28},{20,0},{24,4},{28,8},{1,13},{... | collective-permute-start | bytes 65672 | tf_op jit(solution)/shard_map/ppermute | solution.py:1254
  533.0 240.0 %collective-permute-start.26 = (f32[5472]{0:T(1024)}, f32[5472]{0:T(1024)}, u32[]{:S(2)}, u32[]{:S(2)}) collective-permute-start(f32[5472]{0:T(1024)} %concatenate.199), channel_id=1, source_target_pairs={{0,8},{4,12},{8,16},{12,20},{16,24},{20,28},{24,0},{28,4},{1,9},{5... | collective-permute-start | bytes 65672 | tf_op jit(solution)/shard_map/ppermute | solution.py:1254
  534.8 238.3 %collective-permute-start.25 = (f32[5472]{0:T(1024)}, f32[5472]{0:T(1024)}, u32[]{:S(2)}, u32[]{:S(2)}) collective-permute-start(f32[5472]{0:T(1024)} %concatenate.199), channel_id=1, source_target_pairs={{0,4},{4,8},{8,12},{12,16},{16,20},{20,24},{24,28},{28,0},{1,5},{5... | collective-permute-start | bytes 65672 | tf_op jit(solution)/shard_map/ppermute | solution.py:1254
  535.3 223.7 %copy-start.55 = (bf16[333,512]{1,0:T(8,128)(2,1)S(1)}, bf16[333,512]{1,0:T(8,128)(2,1)}, u32[]{:S(2)}) copy-start(bf16[333,512]{1,0:T(8,128)(2,1)} %add_convert_fusion.2) | copy-start | bytes 1022980
  759.1 23.9 %collective-permute-start.18 = (bf16[333,512]{1,0:T(8,128)(2,1)S(1)}, bf16[333,512]{1,0:T(8,128)(2,1)S(1)}, u32[]{:S(2)}, u32[]{:S(2)}) collective-permute-start(bf16[333,512]{1,0:T(8,128)(2,1)S(1)} %copy-done.55), channel_id=1, source_target_pairs={{1,2},{2,1},{5,6},{6,5},{9,10},{10,9},{13,14},{14,13},{17,18},{18,... | collective-permute-start | bytes 1022984 | tf_op jit(solution)/shard_map/ppermute | solution.py:1155
  (75 other events, 567.7 us)
Sparse Core Ops, SparseCore 0:
  18.3 55.7 all-gather.3
  76.3 53.6 all-gather.5
  377.6 69.8 reduce-scatter.1
  451.9 129.2 all-reduce.2
  583.5 79.2 all-gather.7

commit v4 on v3

--- a/solution.py
+++ b/solution.py
@@ -260,7 +260,7 @@
     )(q, k, v, qg, kg, *extra, out, lse, grad)
 
 
-CHUNK = 256
+CHUNK = 512
 
 
 def core_pair(with_chip=False):

time: 839 us -> 838 us (level)
    pallas_call x6, Pallas kernels: 244 us -> 254 us  [whole_call(): pl.pallas_call(kernel, in_specs=[vmem] * len(operands), out_specs=[vmem]...]
where the time goes in v4:
time: 838 us; the launch traced here: 833 us
  Pallas kernels  583 us (70%)
  local copies, waits for them, and re-layouts  78.4 us (9%)
  other arithmetic  58.1 us (7%)
  waiting for transfers between devices  44.9 us (5%)
  starting transfers between devices  43.4 us (5%)
  between operations  15.3 us (2%)
  matrix products  9.58 us (1%)
    pallas_call x6, Pallas kernels, whole_call(): pl.pallas_call(kernel, in_specs=[vmem] * len(operands), out_specs=[vmem]...  254 us
    pallas_call x1, Pallas kernels, ring_sum(): pl.pallas_call(functools.partial(ring_kernel, size, plan), in_specs=[vmem...  221 us
    pallas_call x2, Pallas kernels, attend_back(): pl.pallas_call(functools.partial(attend_back_kernel, bool(extra), valid),...  44.5 us
    pallas_call x8, Pallas kernels, weight_product(): pl.pallas_call(functools.partial(product_kernel, by_rows, left_last), gri...  41 us
    unnamed x187, local copies, waits for them, and re-layouts  36.2 us
    ppermute x14, waiting for transfers between devices, other_chip(): return lax.ppermute(values, 'row', SWAP)  33.9 us
    pallas_call x2, Pallas kernels, attend(): pl.pallas_call(functools.partial(attend_kernel, bool(extra), valid), grid...  22.8 us
  transfers between devices with their start and end apart: 37, of which 9 were waited for; matrix products, arithmetic and copies ran while one was open for 14% of the time, Pallas kernels for 64%

profile of v4, /device:TPU:1, one launch (start us, length us, event | category | flops | bytes accessed | tf_op | source)
XLA Modules:
  0.0 832.8 jit_solution(6479671072526929342)
XLA Ops:
  8.4 2.1 collective-permute-start.7
  10.6 7.6 collective-permute-done.7
  20.5 7.0 collective-permute-done.8
  28.5 2.1 collective-permute-start.1
  36.9 2.9 copy.87
  39.8 2.8 copy.90.refs_6_
  43.9 121.2 %into_self.1 = (f32[512,1152]{1,0:T(8,128)}, bf16[1024,1152]{1,0:T(8,128)(2,1)}, f32[1728,1024]{1,0:T(8,128)}, bf16[1024,1152]{1,0:T(8,128)(2,1)}, f32[1024,1]{1...) custom-call(bf16[1024,576]{1,0:T(8,128)(2,1)} %copy.88.refs_0_, ...), custom_call_target="tpu_custom_call" | custom-call | bytes 110700000 | tf_op jit(solution)/shard_map/into_self/pallas_call | solution.py:509
  170.5 5.4 collective-permute-done.4
  181.1 15.5 %attend.2 = (bf16[8,72,1024]{2,1,0:T(8,128)(2,1)S(1)}, f32[8,1,1024]{2,1,0:T(1,128)S(1)}) custom-call(f32[24,72,1024]{2,1,0:T(8,128)} %bitcast.76, f32[24,72,1024]{2,1,0:T(8,128)} %bitcast.77, f32[24,72,1024]{2,1,0:T(8,128)} %bitcast.78, f32[72,1]{1,0:T(8,128)S(1)} %copy.91.qg_ref, f32[72,1]{1,0:T(8,128)S(1)} %copy.92.kg_ref, ...), custom_call_target="tpu_custom_call" | custom-call | bytes 18450000 | tf_op jit(solution)/shard_map/attend/pallas_call | solution.py:210
  200.6 18.8 %into_cross.1 = (f32[512,1152]{1,0:T(8,128)}, bf16[1024,1152]{1,0:T(8,128)(2,1)}, f32[576,1024]{1,0:T(8,128)}) custom-call(bf16[576,1024]{1,0:T(8,128)(2,1)} %bitcast.64, bf16[576,576]{1,0:T(8,128)(2,1)} %refs_6_.1, bf16[576,576]{1,0:T(8,128)(2,1)} %get-tuple-element.107.refs_2_.refs_7_, f32[1,1152]{1,0:T(1,128)} %get-tuple-element.311.refs_3_.refs_5_, ...), custom_call_target="tpu_custom_call" | custom-call | bytes 18450000 | tf_op jit(solution)/shard_map/into_cross/pallas_call | solution.py:509
  219.5 3.2 fusion.5
  222.8 7.3 attend.3
  231.2 30.7 %into_feed.1 = (f32[512,1152]{1,0:T(8,128)}, bf16[1024,1152]{1,0:T(8,128)(2,1)}, bf16[512,1152]{1,0:T(8,128)(2,1)}) custom-call(bf16[576,1024]{1,0:T(8,128)(2,1)} %bitcast.66, bf16[576,576]{1,0:T(8,128)(2,1)} %refs_8_.3, bf16[576,576]{1,0:T(8,128)(2,1)} %collective-permute-done.6.refs_2_.refs_9_, f32[1,1152]{1,0:T(1,128)} %get-tuple-element.310.refs_3_.refs_7_, ...), custom_call_target="tpu_custom_call" | custom-call | bytes 34440000 | tf_op jit(solution)/shard_map/into_feed/pallas_call | solution.py:509
  264.2 2.5 collective-permute-done.12
  268.2 38.7 %from_feed.1 = (bf16[1024,2304]{1,0:T(8,128)(2,1)}, bf16[1024,2304]{1,0:T(8,128)(2,1)}, f32[512,1152]{1,0:T(8,128)}, bf16[1024,1152]{1,0:T(8,128)(2,1)}, bf16[576,1024]{1,0:T(8,128)(2,1)}, /*index=5*/f32[1,1152]{1,0:T(1,128)}) custom-call(bf16[1024,1152]{1,0:T(8,128)(2,1)} %pad_maximum_fusion.2.refs_0_.right_ref, ...), custom_call_target="tpu_custom_call" | custom-call | bytes 49200000 | tf_op jit(solution)/shard_map/from_feed/pallas_call | solution.py:509
  307.0 9.9 %grad_down.1 = (bf16[1152,1152]{1,0:T(8,128)(2,1)S(1)}, bf16[1152,1152]{1,0:T(8,128)(2,1)}) custom-call(bf16[1024,2304]{1,0:T(8,128)(2,1)} %get-tuple-element.126.left_ref, bf16[1024,1152]{1,0:T(8,128)(2,1)S(1)} %copy-done.3), custom_call_target="tpu_custom_call" | custom-call | bytes 11070000 | tf_op jit(solution)/shard_map/grad_down/pallas_call | solution.py:730
  320.6 9.6 %grad_up.1 = (bf16[1152,1152]{1,0:T(8,128)(2,1)S(1)}, bf16[1152,1152]{1,0:T(8,128)(2,1)}) custom-call(bf16[1024,2304]{1,0:T(8,128)(2,1)} %get-tuple-element.128.left_ref, bf16[1024,1152]{1,0:T(8,128)(2,1)S(1)} %copy-done.8), custom_call_target="tpu_custom_call" | custom-call | bytes 11070000 | tf_op jit(solution)/shard_map/grad_up/pallas_call | solution.py:730
  331.6 15.5 %attend_back.2 = (bf16[8,72,1024]{2,1,0:T(8,128)(2,1)S(1)}, bf16[2,8,72,384]{3,2,1,0:T(8,128)(2,1)S(1)}, f32[8,2,72,1]{3,2,1,0:T(8,128)S(1)}) custom-call(f32[8,72,1024]{2,1,0:T(8,128)} %bitcast.68, f32[16,72,384]{2,1,0:T(8,128)} %bitcast.62, f32[16,72,384]{2,1,0:T(8,128)} %bitcast.63, f32[72,1]{1,0:T(8,128)S(1)} %copy.93.qg_ref, f32[72,1]{1,0:T(8,128)S(1)} %copy.94.kg_ref, ...), custom_call_target="tpu_custom_call" | custom-call | bytes 19680000 | tf_op jit(solution)/shard_map/attend_back/pallas_call | solution.py:244
  347.1 2.0 grad_cross_query.1
  349.2 2.4 grad_context.1
  354.2 19.0 %from_cross.1 = (f32[512,1152]{1,0:T(8,128)}, bf16[1024,1152]{1,0:T(8,128)(2,1)}, bf16[576,1024]{1,0:T(8,128)(2,1)}, f32[1,1152]{1,0:T(1,128)}) custom-call(bf16[576,1024]{1,0:T(8,128)(2,1)} %bitcast.71, f32[512,1152]{1,0:T(8,128)} %get-tuple-element.138.refs_1_, bf16[576,576]{1,0:T(8,128)(2,1)} %refs_2_.3, ...), custom_call_target="tpu_custom_call" | custom-call | bytes 19680000 | tf_op jit(solution)/shard_map/from_cross/pallas_call | solution.py:509
  373.2 4.3 collective-permute-done.13
  377.5 3.9 add_convert_fusion.1
  383.4 2.9 constant_dynamic-slice_fusion.1
  392.9 3.0 fusion.4
  402.9 29.0 %attend_back.3 = (bf16[3,8,72,1024]{3,2,1,0:T(8,128)(2,1)}, f32[8,2,72,1]{3,2,1,0:T(8,128)S(1)}) custom-call(f32[24,72,1024]{2,1,0:T(8,128)} %bitcast.79, f32[24,72,1024]{2,1,0:T(8,128)} %bitcast.80, f32[24,72,1024]{2,1,0:T(8,128)} %bitcast.81, f32[72,1]{1,0:T(8,128)S(1)} %copy-done.36, f32[72,1]{1,0:T(8,128)S(1)} %copy-done.38, ...), custom_call_target="tpu_custom_call" | custom-call | bytes 35670000 | tf_op jit(solution)/shard_map/attend_back/pallas_call | solution.py:244
  431.9 7.9 collective-permute-done.14
  439.7 4.0 add_convert_fusion
  443.7 7.6 reduce-scatter.2.cloned.1.call-done
  453.2 2.1 collective-permute-start.20
  455.2 2.4 add_convert_fusion.2
  457.7 8.1 grad_self.1
  468.5 25.2 %from_self.1 = (f32[512,1152]{1,0:T(8,128)}, bf16[1024,1152]{1,0:T(8,128)(2,1)}, f32[1024,1152]{1,0:T(8,128)}, f32[1,1152]{1,0:T(1,128)}, f32[1,1152]{1,0:T(1,128)}) custom-call(bf16[1728,1024]{1,0:T(8,128)(2,1)} %bitcast.83, f32[512,1152]{1,0:T(8,128)} %get-tuple-element.146.refs_1_, bf16[1152,1728]{1,0:T(8,128)(2,1)} %get-tuple-element.147.refs_2_, ...), custom_call_target="tpu_custom_call" | custom-call | bytes 27060000 | tf_op jit(solution)/shard_map/from_self/pallas_call | solution.py:509
  494.3 6.6 multiply_reduce_fusion.1
  501.7 2.3 copy.105
  505.2 2.5 broadcast_select_fusion.1
  507.7 2.1 copy.107
  510.2 5.6 grad_skip.1
  518.1 5.5 multiply_convert_fusion
  531.3 2.5 maximum_select_fusion.1
  542.8 221.3 %ring_sum.1 = (bf16[1280,1152]{1,0:T(8,128)(2,1)}, bf16[1280,1152]{1,0:T(8,128)(2,1)}, bf16[768,1152]{1,0:T(8,128)(2,1)}) custom-call(bf16[1088,1152]{1,0:T(8,128)(2,1)} %pad_maximum_fusion.refs_0_, bf16[288,1152]{1,0:T(8,128)(2,1)} %copy-done.27, bf16[864,1152]{1,0:T(8,128)(2,1)} %copy-done.19, bf16[576,1152]{1,0:T(8,128)(2,1)} %copy-done.21, ...), custom_call_target="tpu_custom_call" | custom-call | bytes 246000000 | tf_op jit(solution)/shard_map/ring_sum/pallas_call | solution.py:918
  764.1 13.3 %collective-permute-start.18 = (bf16[333,512]{1,0:T(8,128)(2,1)S(1)}, bf16[333,512]{1,0:T(8,128)(2,1)S(1)}, u32[]{:S(2)}, u32[]{:S(2)}) collective-permute-start(bf16[333,512]{1,0:T(8,128)(2,1)S(1)} %copy-done.55), channel_id=1, source_target_pairs={{1,2},{2,1},{5,6},{6,5},{9,10},{10,9},{13,14},{14,13},{17,18},{18,... | collective-permute-start | bytes 1022984 | tf_op jit(solution)/shard_map/ppermute | solution.py:1155
  790.2 2.0 copy.117
  800.9 3.3 convert.5
  811.2 2.5 fusion.38
  813.7 3.0 maximum_convert_fusion.1
  818.6 2.8 maximum_convert_fusion
  823.3 2.8 convert_bitcast_fusion
  (368 shorter events, 113.0 us)
Async XLA Ops:
  7.2 26.8 %copy-start.56 = (bf16[1024,576]{0,1:T(8,128)(2,1)S(1)}, bf16[1024,576]{0,1:T(8,128)(2,1)}, u32[]{:S(2)}) copy-start(bf16[1024,576]{0,1:T(8,128)(2,1)} %param.23) | copy-start | bytes 3538948
  7.2 223.9 %all-gather.4.cloned.1.call-start = ((), (), s32[]{:S(2)}) async-start(), calls=%async_computation.1 | async-start | bytes 2985984 | tf_op jit(solution)/shard_map/all_gather | solution.py:994
  8.4 27.0 %copy-start.57 = (bf16[1024,576]{0,1:T(8,128)(2,1)S(1)}, bf16[1024,576]{0,1:T(8,128)(2,1)}, u32[]{:S(2)}) copy-start(bf16[1024,576]{0,1:T(8,128)(2,1)} %param.24) | copy-start | bytes 3538948
  8.4 9.8 %collective-permute-start.7 = (bf16[72,2304]{1,0:T(8,128)(2,1)S(1)}, bf16[72,2304]{1,0:T(8,128)(2,1)}, u32[]{:S(2)}, u32[]{:S(2)}) collective-permute-start(bf16[72,2304]{1,0:T(8,128)(2,1)S(1)} %constant_dynamic-slice_fusion.6), channel_id=1, source_target_pairs={{0,2},{2,0},{1,3},{3,1},{4,6},{6,4},{5,7},{7,5},{8,10},{10,8},{9,1... | collective-permute-start | bytes 995336 | tf_op jit(solution)/shard_map/ppermute | solution.py:58
  18.2 212.9 %all-gather.6.cloned.1.call-start = ((), (), s32[]{:S(2)}) async-start(), calls=%async_computation.2 | async-start | bytes 2985984 | tf_op jit(solution)/shard_map/all_gather | solution.py:995
  19.3 8.2 collective-permute-start.8
  27.5 423.7 %reduce-scatter.2.cloned.1.call-start = ((), (), s32[]{:S(2)}) async-start(), calls=%async_computation.3 | async-start | bytes 2985984 | tf_op jit(solution)/shard_map/reduce_scatter | solution.py:1178
  28.5 3.0 collective-permute-start.1
  31.5 11.1 %collective-permute-start.2 = (f32[1,576]{1,0:T(1,128)S(1)}, f32[1,576]{1,0:T(1,128)S(1)}, u32[]{:S(2)}, u32[]{:S(2)}) collective-permute-start(f32[1,576]{1,0:T(1,128)S(1)} %get-tuple-element.330), channel_id=1, source_target_pairs={{0,2},{2,0},{1,3},{3,1},{4,6},{6,4},{5,7},{7,5},{8,10},{10,8},{9,1... | collective-permute-start | bytes 6920 | tf_op jit(solution)/shard_map/ppermute | solution.py:58
  32.7 10.5 %collective-permute-start = (f32[3,576]{1,0:T(4,128)S(1)}, f32[3,576]{1,0:T(4,128)S(1)}, u32[]{:S(2)}, u32[]{:S(2)}) collective-permute-start(f32[3,576]{1,0:T(4,128)S(1)} %pad_maximum_fusion.11), channel_id=1, source_target_pairs={{0,2},{2,0},{1,3},{3,1},{4,6},{6,4},{5,7},{7,5},{8,10},{10,8},{9,1... | collective-permute-start | bytes 20744 | tf_op jit(solution)/shard_map/ppermute | solution.py:58
  33.1 132.1 %collective-permute-start.3 = (bf16[333,512]{1,0:T(8,128)(2,1)}, bf16[333,512]{1,0:T(8,128)(2,1)}, u32[]{:S(2)}, u32[]{:S(2)}) collective-permute-start(bf16[333,512]{1,0:T(8,128)(2,1)} %param.26), channel_id=1, source_target_pairs={{0,1},{1,0},{2,3},{3,2},{4,5},{5,4},{6,7},{7,6},{8,9},{9,8},{10,11... | collective-permute-start | bytes 1022984 | tf_op jit(solution)/shard_map/ppermute | solution.py:54
  43.9 124.3 %copy-start.58 = (bf16[1024,576]{0,1:T(8,128)(2,1)S(1)}, bf16[1024,576]{0,1:T(8,128)(2,1)}, u32[]{:S(2)}) copy-start(bf16[1024,576]{0,1:T(8,128)(2,1)} %param.28) | copy-start | bytes 3538948
  167.1 8.8 %collective-permute-start.4 = (bf16[333,512]{1,0:T(8,128)(2,1)S(1)}, bf16[333,512]{1,0:T(8,128)(2,1)S(1)}, u32[]{:S(2)}, u32[]{:S(2)}) collective-permute-start(bf16[333,512]{1,0:T(8,128)(2,1)S(1)} %get-tuple-element.104), channel_id=1, source_target_pairs={{0,2},{2,0},{1,3},{3,1},{4,6},{6,4},{5,7},{7,5},{8,10},{10,8},{9,1... | collective-permute-start | bytes 1022984 | tf_op jit(solution)/shard_map/ppermute | solution.py:58
  169.2 9.2 %collective-permute-start.10 = (bf16[512,576]{0,1:T(8,128)(2,1)}, bf16[512,576]{0,1:T(8,128)(2,1)}, u32[]{:S(2)}, u32[]{:S(2)}) collective-permute-start(bf16[512,576]{0,1:T(8,128)(2,1)} %get-tuple-element.291), channel_id=1, source_target_pairs={{0,1},{1,0},{2,3},{3,2},{4,5},{5,4},{6,7},{7,6},{8,9},{9,8},{10,11... | collective-permute-start | bytes 1769480 | tf_op jit(solution)/shard_map/ppermute | solution.py:54
  175.9 43.6 %collective-permute-start.5 = (bf16[512,1152]{0,1:T(8,128)(2,1)}, bf16[512,1152]{0,1:T(8,128)(2,1)}, u32[]{:S(2)}, u32[]{:S(2)}) collective-permute-start(bf16[512,1152]{0,1:T(8,128)(2,1)} %bitcast.103), channel_id=1, source_target_pairs={{0,2},{2,0},{1,3},{3,1},{4,6},{6,4},{5,7},{7,5},{8,10},{10,8},{9,1... | collective-permute-start | bytes 3538952 | tf_op jit(solution)/shard_map/ppermute | solution.py:58
  179.7 51.4 %collective-permute-start.6 = (bf16[576,576]{1,0:T(8,128)(2,1)S(1)}, bf16[576,576]{1,0:T(8,128)(2,1)}, u32[]{:S(2)}, u32[]{:S(2)}) collective-permute-start(bf16[576,576]{1,0:T(8,128)(2,1)S(1)} %copy-done.49), channel_id=1, source_target_pairs={{0,2},{2,0},{1,3},{3,1},{4,6},{6,4},{5,7},{7,5},{8,10},{10,8},{9,1... | collective-permute-start | bytes 1990664 | tf_op jit(solution)/shard_map/ppermute | solution.py:58
  199.3 62.6 %collective-permute-start.11 = (bf16[512,576]{0,1:T(8,128)(2,1)}, bf16[512,576]{0,1:T(8,128)(2,1)}, u32[]{:S(2)}, u32[]{:S(2)}) collective-permute-start(bf16[512,576]{0,1:T(8,128)(2,1)} %copy.99), channel_id=1, source_target_pairs={{0,2},{2,0},{1,3},{3,1},{4,6},{6,4},{5,7},{7,5},{8,10},{10,8},{9,1... | collective-permute-start | bytes 1769480 | tf_op jit(solution)/shard_map/ppermute | solution.py:58
  231.1 32.1 %copy-start.52 = (bf16[512,576]{1,0:T(8,128)(2,1)S(1)}, bf16[512,576]{1,0:T(8,128)(2,1)}, u32[]{:S(2)}) copy-start(bf16[512,576]{1,0:T(8,128)(2,1)} %get-tuple-element.288) | copy-start | bytes 1769476
  263.6 3.0 collective-permute-start.12
  268.2 38.7 %copy-start.3 = (bf16[1024,1152]{1,0:T(8,128)(2,1)S(1)}, bf16[1024,1152]{1,0:T(8,128)(2,1)}, u32[]{:S(2)}) copy-start(bf16[1024,1152]{1,0:T(8,128)(2,1)} %pad_maximum_fusion.2.refs_0_.right_ref) | copy-start | bytes 7077892
  318.4 59.1 %collective-permute-start.13 = (bf16[1152,1152]{1,0:T(8,128)(2,1)}, bf16[1152,1152]{1,0:T(8,128)(2,1)}, u32[]{:S(2)}, u32[]{:S(2)}) collective-permute-start(bf16[1152,1152]{1,0:T(8,128)(2,1)} %get-tuple-element.127), channel_id=1, source_target_pairs={{0,2},{2,0},{1,3},{3,1},{4,6},{6,4},{5,7},{7,5},{8,10},{10,8},{9,1... | collective-permute-start | bytes 7962632 | tf_op jit(solution)/shard_map/ppermute | solution.py:58
  381.4 435.3 %all-reduce.3.cloned.1.call-start = ((), (), s32[]{:S(2)}) async-start(), calls=%async_computation.4 | async-start | bytes 5308416 | tf_op jit(solution)/shard_map/psum | solution.py:1266
  381.5 58.2 %collective-permute-start.14 = (bf16[1152,1152]{1,0:T(8,128)(2,1)}, bf16[1152,1152]{1,0:T(8,128)(2,1)}, u32[]{:S(2)}, u32[]{:S(2)}) collective-permute-start(bf16[1152,1152]{1,0:T(8,128)(2,1)} %get-tuple-element.129), channel_id=1, source_target_pairs={{0,2},{2,0},{1,3},{3,1},{4,6},{6,4},{5,7},{7,5},{8,10},{10,8},{9,1... | collective-permute-start | bytes 7962632 | tf_op jit(solution)/shard_map/ppermute | solution.py:58
  391.5 102.2 %collective-permute-start.9 = (bf16[512,576]{0,1:T(8,128)(2,1)}, bf16[512,576]{0,1:T(8,128)(2,1)}, u32[]{:S(2)}, u32[]{:S(2)}) collective-permute-start(bf16[512,576]{0,1:T(8,128)(2,1)} %copy.95), channel_id=1, source_target_pairs={{0,2},{2,0},{1,3},{3,1},{4,6},{6,4},{5,7},{7,5},{8,10},{10,8},{9,1... | collective-permute-start | bytes 1769480 | tf_op jit(solution)/shard_map/ppermute | solution.py:58
  392.4 147.3 %collective-permute-start.24 = (bf16[1088,1152]{1,0:T(8,128)(2,1)}, bf16[1088,1152]{1,0:T(8,128)(2,1)}, u32[]{:S(2)}, u32[]{:S(2)}) collective-permute-start(bf16[1088,1152]{1,0:T(8,128)(2,1)} %copy-done.64), channel_id=1, source_target_pairs={{0,2},{2,0},{1,3},{3,1},{4,6},{6,4},{5,7},{7,5},{8,10},{10,8},{9,1... | collective-permute-start | bytes 7520264 | tf_op jit(solution)/shard_map/ppermute | solution.py:58
  396.9 58.3 %collective-permute-start.17 = (f32[333,512]{1,0:T(8,128)}, f32[333,512]{1,0:T(8,128)}, u32[]{:S(2)}, u32[]{:S(2)}) collective-permute-start(f32[333,512]{1,0:T(8,128)} %slice_select_fusion), channel_id=1, source_target_pairs={{0,1},{1,0},{2,3},{3,2},{4,5},{5,4},{6,7},{7,6},{8,9},{9,8},{10,11... | collective-permute-start | bytes 2045960 | tf_op jit(solution)/shard_map/ppermute | solution.py:54
  401.3 30.6 %copy-start.27 = (bf16[288,1152]{1,0:T(8,128)(2,1)}, bf16[288,1152]{1,0:T(8,128)(2,1)S(1)}, u32[]{:S(2)}) copy-start(bf16[288,1152]{1,0:T(8,128)(2,1)S(1)} %get-tuple-element.157.refs_1_) | copy-start | bytes 1990660
  402.9 36.8 %copy-start.12 = (bf16[1152,1152]{1,0:T(8,128)(2,1)S(1)}, bf16[1152,1152]{1,0:T(8,128)(2,1)}, u32[]{:S(2)}) copy-start(bf16[1152,1152]{1,0:T(8,128)(2,1)} %copy-done.11) | copy-start | bytes 7962628
  451.3 370.1 %all-gather.8.cloned.1.call-start = ((), (), s32[]{:S(2)}) async-start(), calls=%async_computation.5 | async-start | bytes 2985984 | tf_op jit(solution)/shard_map/all_gather | solution.py:1267
  453.2 15.1 %collective-permute-start.20 = (f32[4,72]{1,0:T(4,128)S(1)}, f32[4,72]{1,0:T(4,128)S(1)}, u32[]{:S(2)}, u32[]{:S(2)}) collective-permute-start(f32[4,72]{1,0:T(4,128)S(1)} %maximum_bitcast_fusion), channel_id=1, source_target_pairs={{0,1},{1,0},{2,3},{3,2},{4,5},{5,4},{6,7},{7,6},{8,9},{9,8},{10,11... | collective-permute-start | bytes 3464 | tf_op jit(solution)/shard_map/ppermute | solution.py:54
  468.4 25.8 %copy-start.43 = (bf16[512,576]{1,0:T(8,128)(2,1)S(1)}, bf16[512,576]{1,0:T(8,128)(2,1)}, u32[]{:S(2)}) copy-start(bf16[512,576]{1,0:T(8,128)(2,1)} %get-tuple-element.285) | copy-start | bytes 1769476
  468.4 25.8 %copy-start.44 = (bf16[512,576]{1,0:T(8,128)(2,1)S(1)}, bf16[512,576]{1,0:T(8,128)(2,1)}, u32[]{:S(2)}) copy-start(bf16[512,576]{1,0:T(8,128)(2,1)} %get-tuple-element.333) | copy-start | bytes 1769476
  468.4 25.8 %copy-start.45 = (bf16[512,576]{1,0:T(8,128)(2,1)S(1)}, bf16[512,576]{1,0:T(8,128)(2,1)}, u32[]{:S(2)}) copy-start(bf16[512,576]{1,0:T(8,128)(2,1)} %get-tuple-element.334) | copy-start | bytes 1769476
  493.6 10.3 %collective-permute-start.22 = (f32[1,1152]{1,0:T(1,128)}, f32[1,1152]{1,0:T(1,128)S(1)}, u32[]{:S(2)}, u32[]{:S(2)}) collective-permute-start(f32[1,1152]{1,0:T(1,128)} %get-tuple-element.167), channel_id=1, source_target_pairs={{0,1},{1,0},{2,3},{3,2},{4,5},{5,4},{6,7},{7,6},{8,9},{9,8},{10,11... | collective-permute-start | bytes 13832 | tf_op jit(solution)/shard_map/ppermute | solution.py:54
  501.0 17.1 %collective-permute-start.16 = (f32[2,1024]{1,0:T(2,128)S(1)}, f32[2,1024]{1,0:T(2,128)S(1)}, u32[]{:S(2)}, u32[]{:S(2)}) collective-permute-start(f32[2,1024]{1,0:T(2,128)S(1)} %pad_maximum_fusion.12), channel_id=1, source_target_pairs={{0,1},{1,0},{2,3},{3,2},{4,5},{5,4},{6,7},{7,6},{8,9},{9,8},{10,11... | collective-permute-start | bytes 24584 | tf_op jit(solution)/shard_map/ppermute | solution.py:54
  501.1 23.0 %collective-permute-start.19 = (f32[3,1152]{1,0:T(4,128)S(1)}, f32[3,1152]{1,0:T(4,128)S(1)}, u32[]{:S(2)}, u32[]{:S(2)}) collective-permute-start(f32[3,1152]{1,0:T(4,128)S(1)} %pad_maximum_fusion.10), channel_id=1, source_target_pairs={{0,1},{1,0},{2,3},{3,2},{4,5},{5,4},{6,7},{7,6},{8,9},{9,8},{10,11... | collective-permute-start | bytes 41480 | tf_op jit(solution)/shard_map/ppermute | solution.py:54
  504.1 13.9 %collective-permute-start.23 = (f32[1,576]{1,0:T(1,128)S(1)}, f32[1,576]{1,0:T(1,128)S(1)}, u32[]{:S(2)}, u32[]{:S(2)}) collective-permute-start(f32[1,576]{1,0:T(1,128)S(1)} %get-tuple-element.332), channel_id=1, source_target_pairs={{0,2},{2,0},{1,3},{3,1},{4,6},{6,4},{5,7},{7,5},{8,10},{10,8},{9,1... | collective-permute-start | bytes 6920 | tf_op jit(solution)/shard_map/ppermute | solution.py:58
  509.8 26.7 %collective-permute-start.15 = (bf16[512,576]{0,1:T(8,128)(2,1)}, bf16[512,576]{0,1:T(8,128)(2,1)}, u32[]{:S(2)}, u32[]{:S(2)}) collective-permute-start(bf16[512,576]{0,1:T(8,128)(2,1)} %copy.107), channel_id=1, source_target_pairs={{0,1},{1,0},{2,3},{3,2},{4,5},{5,4},{6,7},{7,6},{8,9},{9,8},{10,11... | collective-permute-start | bytes 1769480 | tf_op jit(solution)/shard_map/ppermute | solution.py:54
  524.4 3.0 collective-permute-start.21
  528.0 12.4 %collective-permute-start.31 = (f32[5472]{0:T(1024)}, f32[5472]{0:T(1024)S(1)}, u32[]{:S(2)}, u32[]{:S(2)}) collective-permute-start(f32[5472]{0:T(1024)} %concatenate.199), channel_id=1, source_target_pairs={{0,28},{4,0},{8,4},{12,8},{16,12},{20,16},{24,20},{28,24},{1,29},{... | collective-permute-start | bytes 65672 | tf_op jit(solution)/shard_map/ppermute | solution.py:1254
  529.8 12.4 %collective-permute-start.30 = (f32[5472]{0:T(1024)}, f32[5472]{0:T(1024)}, u32[]{:S(2)}, u32[]{:S(2)}) collective-permute-start(f32[5472]{0:T(1024)} %concatenate.199), channel_id=1, source_target_pairs={{0,24},{4,28},{8,0},{12,4},{16,8},{20,12},{24,16},{28,20},{1,25},{... | collective-permute-start | bytes 65672 | tf_op jit(solution)/shard_map/ppermute | solution.py:1254
  536.6 227.5 %collective-permute-start.29 = (f32[5472]{0:T(1024)}, f32[5472]{0:T(1024)}, u32[]{:S(2)}, u32[]{:S(2)}) collective-permute-start(f32[5472]{0:T(1024)} %concatenate.199), channel_id=1, source_target_pairs={{0,20},{4,24},{8,28},{12,0},{16,4},{20,8},{24,12},{28,16},{1,21},{... | collective-permute-start | bytes 65672 | tf_op jit(solution)/shard_map/ppermute | solution.py:1254
  536.6 240.8 %collective-permute-start.28 = (f32[5472]{0:T(1024)}, f32[5472]{0:T(1024)}, u32[]{:S(2)}, u32[]{:S(2)}) collective-permute-start(f32[5472]{0:T(1024)} %concatenate.199), channel_id=1, source_target_pairs={{0,16},{4,20},{8,24},{12,28},{16,0},{20,4},{24,8},{28,12},{1,17},{... | collective-permute-start | bytes 65672 | tf_op jit(solution)/shard_map/ppermute | solution.py:1254
  539.7 237.7 %collective-permute-start.27 = (f32[5472]{0:T(1024)}, f32[5472]{0:T(1024)}, u32[]{:S(2)}, u32[]{:S(2)}) collective-permute-start(f32[5472]{0:T(1024)} %concatenate.199), channel_id=1, source_target_pairs={{0,12},{4,16},{8,20},{12,24},{16,28},{20,0},{24,4},{28,8},{1,13},{... | collective-permute-start | bytes 65672 | tf_op jit(solution)/shard_map/ppermute | solution.py:1254
  540.4 237.0 %collective-permute-start.26 = (f32[5472]{0:T(1024)}, f32[5472]{0:T(1024)}, u32[]{:S(2)}, u32[]{:S(2)}) collective-permute-start(f32[5472]{0:T(1024)} %concatenate.199), channel_id=1, source_target_pairs={{0,8},{4,12},{8,16},{12,20},{16,24},{20,28},{24,0},{28,4},{1,9},{5... | collective-permute-start | bytes 65672 | tf_op jit(solution)/shard_map/ppermute | solution.py:1254
  542.2 235.3 %collective-permute-start.25 = (f32[5472]{0:T(1024)}, f32[5472]{0:T(1024)}, u32[]{:S(2)}, u32[]{:S(2)}) collective-permute-start(f32[5472]{0:T(1024)} %concatenate.199), channel_id=1, source_target_pairs={{0,4},{4,8},{8,12},{12,16},{16,20},{20,24},{24,28},{28,0},{1,5},{5... | collective-permute-start | bytes 65672 | tf_op jit(solution)/shard_map/ppermute | solution.py:1254
  542.7 221.3 %copy-start.55 = (bf16[333,512]{1,0:T(8,128)(2,1)S(1)}, bf16[333,512]{1,0:T(8,128)(2,1)}, u32[]{:S(2)}) copy-start(bf16[333,512]{1,0:T(8,128)(2,1)} %add_convert_fusion.2) | copy-start | bytes 1022980
  764.1 23.0 %collective-permute-start.18 = (bf16[333,512]{1,0:T(8,128)(2,1)S(1)}, bf16[333,512]{1,0:T(8,128)(2,1)S(1)}, u32[]{:S(2)}, u32[]{:S(2)}) collective-permute-start(bf16[333,512]{1,0:T(8,128)(2,1)S(1)} %copy-done.55), channel_id=1, source_target_pairs={{1,2},{2,1},{5,6},{6,5},{9,10},{10,9},{13,14},{14,13},{17,18},{18,... | collective-permute-start | bytes 1022984 | tf_op jit(solution)/shard_map/ppermute | solution.py:1155
  (75 other events, 596.5 us)
Sparse Core Ops, SparseCore 0:
  18.3 55.7 all-gather.3
  76.3 53.5 all-gather.5
  381.5 69.6 reduce-scatter.1
  455.8 129.3 all-reduce.2
  587.5 77.7 all-gather.7
